TPU v7x, 256 devices: a whole 4x4x8 slice. The times are simulated.
256 devices in a mesh: frame: 8 (over y, core), slab: 32 (over z, x).
Axes of the slice: x: 4, y: 4, z: 8, core: 2. Of those that a mesh axis runs over, the one named last changes fastest.
Arguments:
- positions: float32 [16, 3, 8192], P('frame', None, 'slab'), may hold values from 0 to 6
- species: int32 [16, 8192], P('frame', 'slab'), may hold values from 0 to 1
- atom_count: int32 [16, 32], P('frame', 'slab'), may hold values from 192 to 256, as said below
- halo_index: int32 [16, 2, 4096], P('frame', None, 'slab'), may hold values from 0 to 255, as said below
- neighbours: int32 [16, 48, 8192], P('frame', None, 'slab'), may hold values from -1 to 511, as said below
- embedding: bfloat16 [2, 128], replicated, may hold values from -6 to 6
- w_msg: bfloat16 [2, 128, 128], replicated, may hold values from -0.5 to 0.5
- w_rad1: bfloat16 [2, 8, 64], replicated, may hold values from -2 to 2
- w_rad2: bfloat16 [2, 64, 256], replicated, may hold values from -0.75 to 0.75
- w_up: bfloat16 [2, 256, 128], replicated, may hold values from -0.375 to 0.375
- w_out: float32 [128], replicated, may hold values from -0.5 to 0.5
- e_shift: float32 [2], replicated, may hold values from 0.2 to 0.6
- u_reference: float32 [16], P('frame'), may hold values from -201000 to 1000
- inverse_temp: float32 [1], replicated, may hold values from 0.002 to 0.006
- q_vectors: float32 [3, 16], replicated, may hold values from -1.5 to 1.5
- s_target: float32 [16], replicated, may hold values from 0.2 to 1
Outputs:
- atom_energy: float32 [16, 8192], P('frame', 'slab')
- mean_structure: float32 [16], replicated
- grad_up: float32 [256, 128], replicated
- grad_out: float32 [128], replicated
Inputs may be any that keep to these rules, and one draw needn't show every extreme that they name: `atom_count`: in every frame some slab holds 256 live atoms; the live atoms of a slab are its first slots. `halo_index`: each slab's blocks hold 128 indices of its own live atoms; indices may repeat. `neighbours`: an entry below 256 is another live atom of the same slab, 256 + h the h-th atom passed up from the slab below, 384 + h the h-th atom passed down from the slab above, -1 an empty slot. Each live atom has 24 to 48 entries, empty atom slots have none; entries may repeat.
All inputs are finite; a program needn't handle non-finite values.
Results may differ from a plain program's by a relative error of at most 0.0065.
Values may be sent and summed in bfloat16 or wider, within the bound.
No kernel may reach another device: no remote copies, remote signals or barrier semaphores. Data moves between devices by JAX's collectives and lax.ppermute only.
A program may use at most 128 MiB of HBM per device.

v0:
```python
import jax
import jax.numpy as jnp
from jax import lax
from jax.sharding import PartitionSpec as P

LAYERS = 2


slab_depth = 6.0
vector_scale = 0.2
target_var = 0.01
hydrogen_length = -0.64


def with_halo(value, sides, width):
    for axis, dim in sides:
        devices, length = (lax.axis_size(axis), value.shape[dim])
        up = [(i, (i + 1) % devices) for i in range(devices)]
        down = [(j, i) for i, j in up]
        last = lax.slice_in_dim(value, length - width, length, axis=dim)
        first = lax.slice_in_dim(value, 0, width, axis=dim)
        before = lax.ppermute(last, axis, up)
        after = lax.ppermute(first, axis, down)
        value = jnp.concatenate([before, value, after], axis=dim)
    return value


def radial_basis(distance, number):
    centers = jnp.arange(number, dtype=jnp.float32)
    return jnp.exp(-jnp.square(distance[..., None] - centers))


def silu_slope(values):
    sigmoid = jax.nn.sigmoid(values)
    return sigmoid * (1.0 + values * (1.0 - sigmoid))


def edge_terms(feature_all, coord_all, own_coords, slot_lists, rad_first, rad_second):
    present = slot_lists >= 0
    target_idx = jnp.maximum(slot_lists, 0)
    row_total = feature_all.shape[0]
    picker = target_idx[..., None] == jnp.arange(row_total, dtype=jnp.int32)
    picked_coords = jnp.einsum(
        "kbr,dr->dkb", picker.astype(jnp.float32), coord_all, precision=lax.Precision.HIGHEST
    )
    offsets = picked_coords - own_coords[:, None, :]
    distance = jnp.sqrt(jnp.sum(offsets * offsets, axis=0))
    expanded = radial_basis(distance, rad_first.shape[0]).astype(jnp.bfloat16)
    hidden = jax.nn.silu(
        jnp.einsum("kbn,nh->kbh", expanded, rad_first, preferred_element_type=jnp.float32)
    ).astype(jnp.bfloat16)
    radial = jnp.einsum("kbh,hc->kbc", hidden, rad_second, preferred_element_type=jnp.float32)
    radial = radial * present[..., None]
    channels = feature_all.shape[1]
    gathered = jnp.einsum(
        "kbr,rc->kbc", picker.astype(jnp.bfloat16), feature_all, preferred_element_type=jnp.float32
    )
    scaling = slot_lists.shape[0] ** (-0.5)
    scalar_part = scaling * jnp.sum(radial[..., :channels] * gathered, axis=0)
    vector_term = radial[..., channels:] * gathered
    squared = jnp.zeros_like(scalar_part)
    for component in range(3):
        projected = scaling * jnp.sum(
            (vector_scale * offsets[component])[..., None] * vector_term, axis=0
        )
        squared = squared + projected * projected
    return jnp.concatenate([scalar_part, squared], axis=1)


def per_device(
    positions,
    species,
    atom_count,
    halo_index,
    neighbours,
    embedding,
    w_msg,
    w_rad1,
    w_rad2,
    w_up,
    w_out,
    e_shift,
    u_reference,
    inverse_temp,
    q_vectors,
    s_target,
):
    frame_count = positions.shape[0]
    atom_rows = positions.shape[2]
    halo_rows = halo_index.shape[2]
    slot_count = neighbours.shape[1]
    channels = w_msg.shape[1]
    slab_devs = lax.axis_size("slab")
    slab_pos = lax.axis_index("slab")
    pick_columns = jax.vmap(lambda source, chosen: source[:, chosen])
    pick_rows = jax.vmap(lambda source, chosen: source[chosen])
    outgoing = jnp.concatenate(
        [
            pick_columns(positions, halo_index[:, 0, :]),
            pick_columns(positions, halo_index[:, 1, :]),
        ],
        axis=2,
    )
    extended = with_halo(outgoing, (("slab", 2),), halo_rows)
    slab_lift = jnp.array([0.0, 0.0, slab_depth], dtype=jnp.float32)[None, :, None]
    coord_all = jnp.concatenate(
        [
            positions,
            extended[:, :, :halo_rows] - slab_lift,
            extended[:, :, 3 * halo_rows :] + slab_lift,
        ],
        axis=2,
    )
    kind_table = (species[..., None] == jnp.arange(embedding.shape[0], dtype=jnp.int32)).astype(
        jnp.bfloat16
    )
    features = jnp.einsum("fas,sc->fac", kind_table, embedding, preferred_element_type=jnp.float32)
    living = (jnp.arange(atom_rows, dtype=jnp.int32)[None, :] < atom_count).astype(jnp.float32)
    block_rows = min(256, atom_rows)
    block_count = atom_rows // block_rows
    mixed_in = None
    update = None
    for layer_idx in range(LAYERS):
        message = jnp.einsum(
            "fac,cd->fad",
            features.astype(jnp.bfloat16),
            w_msg[layer_idx],
            preferred_element_type=jnp.float32,
        ).astype(jnp.bfloat16)
        leaving = jnp.concatenate(
            [pick_rows(message, halo_index[:, 0, :]), pick_rows(message, halo_index[:, 1, :])],
            axis=1,
        )
        arrived = with_halo(leaving, (("slab", 1),), halo_rows)
        feature_all = jnp.concatenate(
            [message, arrived[:, :halo_rows], arrived[:, 3 * halo_rows :]], axis=1
        )
        first_rad = w_rad1[layer_idx]
        second_rad = w_rad2[layer_idx]
        mixed_rows = []
        for frame_idx in range(frame_count):
            slot_lists = (
                neighbours[frame_idx]
                .reshape(slot_count, block_count, block_rows)
                .transpose(1, 0, 2)
            )
            own_coords = positions[frame_idx].reshape(3, block_count, block_rows).transpose(1, 0, 2)
            frame_features = feature_all[frame_idx]
            frame_coords = coord_all[frame_idx]
            blocks = lax.map(
                lambda operands: edge_terms(
                    frame_features, frame_coords, operands[1], operands[0], first_rad, second_rad
                ),
                (slot_lists, own_coords),
            )
            mixed_rows.append(blocks.reshape(atom_rows, 2 * channels))
        mixed_in = jnp.stack(mixed_rows).astype(jnp.bfloat16)
        update = jnp.einsum(
            "fak,kc->fac", mixed_in, w_up[layer_idx], preferred_element_type=jnp.float32
        )
        features = features + jax.nn.silu(update)
    readout = jnp.einsum("fac,c->fa", features, w_out, precision=lax.Precision.HIGHEST)
    shift_rows = jnp.sum(kind_table.astype(jnp.float32) * e_shift, axis=-1)
    atom_energy = living * (readout + shift_rows)
    energy_loc = jnp.sum(atom_energy, axis=1)
    global_z = positions[:, 2, :] + slab_pos.astype(jnp.float32) * slab_depth
    phases = (
        q_vectors[0][None, :, None] * positions[:, 0, :][:, None, :]
        + q_vectors[1][None, :, None] * positions[:, 1, :][:, None, :]
        + q_vectors[2][None, :, None] * global_z[:, None, :]
    )
    lengths = living * jnp.where(species == 1, 1.0, hydrogen_length)
    cos_part = jnp.sum(lengths[:, None, :] * jnp.cos(phases), axis=2)
    sin_part = jnp.sum(lengths[:, None, :] * jnp.sin(phases), axis=2)
    grad_out_loc = jnp.sum(living[..., None] * features, axis=1)
    slope_rows = (living[..., None] * w_out * silu_slope(update)).astype(jnp.bfloat16)
    grad_up_loc = jnp.einsum(
        "fak,fac->fkc", mixed_in, slope_rows, preferred_element_type=jnp.float32
    )
    totals, cos_tot, sin_tot, grad_up_tot, grad_out_tot = lax.psum(
        (energy_loc, cos_part, sin_part, grad_up_loc, grad_out_loc), "slab"
    )
    atoms_all = atom_rows * slab_devs
    structure = (cos_tot * cos_tot + sin_tot * sin_tot) / atoms_all
    log_weight = -inverse_temp[0] * (totals - u_reference)
    top_weight = lax.pmax(jnp.max(log_weight), "frame")
    scaled = jnp.exp(log_weight - top_weight)
    weight_total, weighted_sq = lax.psum(
        (jnp.sum(scaled), jnp.sum(scaled[:, None] * structure, axis=0)), "frame"
    )
    weights = scaled / weight_total
    mean_structure = weighted_sq / weight_total
    slope_sq = (mean_structure - s_target) / target_var
    observed = jnp.sum(structure * slope_sq, axis=1)
    average = jnp.sum(mean_structure * slope_sq)
    factor = -inverse_temp[0] * weights * (observed - average)
    weighted_up = jnp.sum(factor[:, None, None] * grad_up_tot, axis=0)
    weighted_out = jnp.sum(factor[:, None] * grad_out_tot, axis=0)
    grad_up, grad_out = lax.psum((weighted_up, weighted_out), "frame")
    return (atom_energy, mean_structure, grad_up, grad_out)


def solution(mesh):
    in_specs = (
        P("frame", None, "slab"),
        P("frame", "slab"),
        P("frame", "slab"),
        P("frame", None, "slab"),
        P("frame", None, "slab"),
        P(),
        P(),
        P(),
        P(),
        P(),
        P(),
        P(),
        P("frame"),
        P(),
        P(),
        P(),
    )
    out_specs = (P("frame", "slab"), P(), P(), P())
    return jax.shard_map(
        per_device, mesh=mesh, in_specs=in_specs, out_specs=out_specs, check_vma=False
    )
```

profile of v0, /device:TPU:1, one launch (start us, length us, event | category | flops | bytes accessed | tf_op | source)
XLA Modules:
  0.0 454.9 jit_solution(5601656016719658932)
XLA Ops:
  7.2 0.8 fusion.105
  8.0 0.8 copy.36
  8.9 1.9 gather_fusion
  10.8 2.1 collective-permute-start
  12.9 1.9 gather_fusion.1
  14.9 6.6 %collective-permute-start.1 = (f32[2,3,128]{2,1,0:T(4,128)S(1)}, f32[2,3,128]{2,1,0:T(4,128)S(1)}, u32[]{:S(2)}, u32[]{:S(2)}) collective-permute-start(f32[2,3,128]{2,1,0:T(4,128)S(1)} %bitcast.181), channel_id=1, source_target_pairs={{1,0},{2,1},{3,2},{4,3},{5,4},{6,5},{7,6},{8,7},{9,8},{10,9},{11,1... | collective-permute-start | bytes 9224 | tf_op jit(solution)/shard_map/ppermute | solution.py:23
  21.5 0.9 fusion.60
  22.5 0.9 convolution_convert_fusion.1
  23.4 1.7 gather_fusion.2
  25.2 1.7 gather_fusion.3
  26.8 4.8 %collective-permute-start.3 = (bf16[2,128,128]{2,1,0:T(8,128)(2,1)S(1)}, bf16[2,128,128]{2,1,0:T(8,128)(2,1)S(1)}, u32[]{:S(2)}, u32[]{:S(2)}) collective-permute-start(bf16[2,128,128]{2,1,0:T(8,128)(2,1)S(1)} %bitcast.165), channel_id=1, source_target_pairs={{1,0},{2,1},{3,2},{4,3},{5,4},{6,5},{7,6},{8,7},{9,8},{10,9},{11,1... | collective-permute-start | bytes 196616 | tf_op jit(solution)/shard_map/ppermute | solution.py:23
  31.7 0.8 fusion.104
  32.4 0.8 maximum_bitcast_fusion.5
  33.3 0.8 convert_bitcast_fusion.1
  34.1 0.7 fusion.72
  34.8 0.7 slice_bitcast_fusion.13
  35.6 0.8 slice_bitcast_fusion.16
  36.4 0.8 multiply_reduce_fusion.18
  37.1 0.7 copy.42
  38.5 0.7 broadcast_add_fusion
  39.2 0.7 broadcast_add_fusion.1
  40.0 12.7 %multiply_reduce_fusion.15 = (f32[48,256]{1,0:T(8,128)S(1)}, f32[3,48,256]{2,0,1:T(4,128)S(1)}) fusion(f32[3,256]{1,0:T(4,128)S(1)} %get-tuple-element.159, s32[48,256]{1,0:T(8,128)S(1)} %get-tuple-element.140, f32[2,3,512]{2,1,0:T(4,128)S(1)} %pad_maximum_fusion.5), kind=kOutput, calls=%fused_computation.80 | convolution fusion | flops 232882176 | bytes 258048 | tf_op jit(solution)/shard_map/while/body/eval_jaxpr/kbr,dr->dkb/dot_general | solution.py:43
  52.7 6.2 %broadcast_multiply_fusion.3 = f32[48,256,256]{2,1,0:T(8,128)} fusion(f32[48,256]{1,0:T(8,128)S(1)} %get-tuple-element.138, f32[48,256]{1,0:T(8,128)S(1)} %sqrt.20, bf16[2,64,256]{2,1,0:T(8,128)(2,1)S(1)} %copy-done.9, bf16[2,8,64]{2,1,0:T(8,128)(2,1)S(1)} %copy-done.10), kind=kOutput, calls=%fused_computation.47 | convolution fusion | flops 422707200 | bytes 12716032 | tf_op jit(solution)/shard_map/while/body/eval_jaxpr/kbh,hc->kbc/dot_general | solution.py:52
  58.9 6.3 %broadcast_multiply_fusion.2 = f32[48,256,256]{2,1,0:T(8,128)} fusion(f32[48,256]{1,0:T(8,128)S(1)} %get-tuple-element.138, f32[48,256]{1,0:T(8,128)S(1)} %sqrt.20, bf16[2,64,256]{2,1,0:T(8,128)(2,1)S(1)} %copy-done.9, bf16[2,8,64]{2,1,0:T(8,128)(2,1)S(1)} %copy-done.10), kind=kOutput, calls=%fused_computation.46 | convolution fusion | flops 422707200 | bytes 12716032 | tf_op jit(solution)/shard_map/while/body/eval_jaxpr/kbh,hc->kbc/dot_general | solution.py:52
  65.3 12.5 %multiply_reduce_fusion.14 = (f32[48,256]{1,0:T(8,128)S(1)}, f32[3,48,256]{2,0,1:T(4,128)S(1)}) fusion(f32[3,256]{1,0:T(4,128)S(1)} %get-tuple-element.158, s32[48,256]{1,0:T(8,128)S(1)} %get-tuple-element.141, f32[2,3,512]{2,1,0:T(4,128)S(1)} %pad_maximum_fusion.5), kind=kOutput, calls=%fused_computation.77 | convolution fusion | flops 232882176 | bytes 258048 | tf_op jit(solution)/shard_map/while/body/eval_jaxpr/kbr,dr->dkb/dot_general | solution.py:43
  77.9 6.3 %broadcast_multiply_fusion.1 = f32[48,256,256]{2,1,0:T(8,128)} fusion(f32[48,256]{1,0:T(8,128)S(1)} %get-tuple-element.139, f32[48,256]{1,0:T(8,128)S(1)} %sqrt.21, bf16[2,64,256]{2,1,0:T(8,128)(2,1)S(1)} %copy-done.9, bf16[2,8,64]{2,1,0:T(8,128)(2,1)S(1)} %copy-done.10), kind=kOutput, calls=%fused_computation.42 | convolution fusion | flops 422707200 | bytes 12716032 | tf_op jit(solution)/shard_map/while/body/eval_jaxpr/kbh,hc->kbc/dot_general | solution.py:52
  84.5 10.9 %fusion.15 = (f32[256,128]{1,0:T(8,128)S(1)}, f32[256,128]{1,0:T(8,128)S(1)}, f32[256,128]{1,0:T(8,128)S(1)}, f32[256,128]{1,0:T(8,128)S(1)}) fusion(f32[48,256,256]{2,1,0:T(8,128)} %broadcast_multiply_fusion.3, f32[48,256]{1,0:T(8,128)S(1)} %bitcast.176, f32[48,256]{1,0:T(8,128)S(1)} %bitcast.174, f32[48,256]{1,0:T(8,128)S(1)} %bitcast.178, ...), kind=kOutput, calls=%fused_computation.31 | convolution fusion | flops 1630928896 | bytes 13434880 | tf_op jit(solution)/shard_map/while/body/eval_jaxpr/kbr,rc->kbc/dot_general | solution.py:55
  95.5 9.1 %fusion.14 = (f32[256,128]{1,0:T(8,128)S(1)}, f32[256,128]{1,0:T(8,128)S(1)}, f32[256,128]{1,0:T(8,128)S(1)}, f32[256,128]{1,0:T(8,128)S(1)}) fusion(f32[48,256,256]{2,1,0:T(8,128)S(1)} %bitcast.187, f32[48,256]{1,0:T(8,128)S(1)} %bitcast.170, f32[48,256]{1,0:T(8,128)S(1)} %bitcast.168, f32[48,256]{1,0:T(8,128)S(1)} %bitcast.172, ...), kind=kOutput, calls=%fused_computation.28 | convolution fusion | flops 1630928896 | bytes 13434880 | tf_op jit(solution)/shard_map/while/body/eval_jaxpr/kbr,rc->kbc/dot_general | solution.py:55
  105.2 1.7 gather_fusion.4
  106.9 1.7 gather_fusion.5
  108.8 4.8 %collective-permute-start.5 = (bf16[2,128,128]{2,1,0:T(8,128)(2,1)S(1)}, bf16[2,128,128]{2,1,0:T(8,128)(2,1)S(1)}, u32[]{:S(2)}, u32[]{:S(2)}) collective-permute-start(bf16[2,128,128]{2,1,0:T(8,128)(2,1)S(1)} %bitcast.166), channel_id=1, source_target_pairs={{1,0},{2,1},{3,2},{4,3},{5,4},{6,5},{7,6},{8,7},{9,8},{10,9},{11,1... | collective-permute-start | bytes 196616 | tf_op jit(solution)/shard_map/ppermute | solution.py:23
  113.6 6.2 %broadcast_multiply_fusion = f32[48,256,256]{2,1,0:T(8,128)} fusion(f32[48,256]{1,0:T(8,128)S(1)} %get-tuple-element.139, f32[48,256]{1,0:T(8,128)S(1)} %sqrt.21, bf16[2,64,256]{2,1,0:T(8,128)(2,1)S(1)} %copy-done.9, bf16[2,8,64]{2,1,0:T(8,128)(2,1)S(1)} %copy-done.10), kind=kOutput, calls=%fused_computation.41 | convolution fusion | flops 422707200 | bytes 12716032 | tf_op jit(solution)/shard_map/while/body/eval_jaxpr/kbh,hc->kbc/dot_general | solution.py:52
  119.8 10.9 %fusion.13 = (f32[256,128]{1,0:T(8,128)S(1)}, f32[256,128]{1,0:T(8,128)S(1)}, f32[256,128]{1,0:T(8,128)S(1)}, f32[256,128]{1,0:T(8,128)S(1)}) fusion(f32[48,256,256]{2,1,0:T(8,128)} %broadcast_multiply_fusion.2, f32[48,256]{1,0:T(8,128)S(1)} %bitcast.177, f32[48,256]{1,0:T(8,128)S(1)} %bitcast.175, f32[48,256]{1,0:T(8,128)S(1)} %bitcast.179, ...), kind=kOutput, calls=%fused_computation.25 | convolution fusion | flops 1630928896 | bytes 13434880 | tf_op jit(solution)/shard_map/while/body/eval_jaxpr/kbr,rc->kbc/dot_general | solution.py:55
  130.9 9.1 %fusion.12 = (f32[256,128]{1,0:T(8,128)S(1)}, f32[256,128]{1,0:T(8,128)S(1)}, f32[256,128]{1,0:T(8,128)S(1)}, f32[256,128]{1,0:T(8,128)S(1)}) fusion(f32[48,256,256]{2,1,0:T(8,128)S(1)} %bitcast.189, f32[48,256]{1,0:T(8,128)S(1)} %bitcast.171, f32[48,256]{1,0:T(8,128)S(1)} %bitcast.169, f32[48,256]{1,0:T(8,128)S(1)} %bitcast.173, ...), kind=kOutput, calls=%fused_computation.22 | convolution fusion | flops 1630928896 | bytes 13434880 | tf_op jit(solution)/shard_map/while/body/eval_jaxpr/kbr,rc->kbc/dot_general | solution.py:55
  140.8 0.8 fusion.102
  141.8 56.0 %all-reduce = (f32[2]{0:T(128)S(1)}, f32[2,16]{1,0:T(2,128)S(1)}, f32[2,16]{1,0:T(2,128)S(1)}, f32[2,128]{1,0:T(2,128)S(1)}) all-reduce(f32[2]{0:T(128)S(1)} %get-tuple-element.130, f32[2,16]{1,0:T(2,128)S(1)} %get-tuple-element.101, f32[2,16]{1,0:T(2,128)S(1)} %get-tuple-element.100, ...), channel_id=1, replica_groups=mesh['frame'=8,'slab'=32] {'slab'}, use_global_device_ids=true, to_apply=%region_24.25 | all-reduce | flops 322 | bytes 2576 | tf_op jit(solution)/shard_map/psum | solution.py:180
  197.8 0.6 fusion.100
  198.4 29.7 %pmax.7 = f32[]{:T(128)} all-reduce(f32[]{:T(128)} %fusion.100), channel_id=1, replica_groups=mesh['frame'=8,'slab'=32] {'frame'}, use_global_device_ids=true, to_apply=%region_26.27 | all-reduce | flops 1 | bytes 8 | tf_op jit(solution)/shard_map/pmax | solution.py:186
  228.1 1.3 fusion.101
  229.4 12.9 %all-reduce.1 = (f32[16]{0:T(128)S(1)}, f32[]{:T(128)}) all-reduce(f32[16]{0:T(128)S(1)} %multiply_reduce_fusion.21, f32[]{:T(128)} %get-tuple-element.118), channel_id=1, replica_groups=mesh['frame'=8,'slab'=32] {'frame'}, use_global_device_ids=true, to_apply=%region_28.29 | all-reduce | flops 17 | bytes 136 | tf_op jit(solution)/shard_map/psum | solution.py:188
  242.3 1.3 multiply_reduce_fusion.22
  243.6 1.1 fusion.36
  244.9 1.3 subtract_multiply_fusion
  246.3 133.5 %all-reduce.5.cloned.1.call-done = f32[2,256,128]{2,1,0:T(8,128)} async-done(((f32[2,256,128]{2,1,0:T(8,128)}), f32[2,256,128]{2,1,0:T(8,128)}) %all-reduce.5.cloned.1.call-update) | async-done | bytes 262160 | tf_op jit(solution)/shard_map/psum | solution.py:180
  379.8 1.7 multiply_reduce_fusion.13
  381.6 17.4 %psum.71 = f32[128]{0:T(128)} all-reduce(f32[128]{0:T(128)S(1)} %multiply_reduce_fusion.19), channel_id=1, replica_groups=mesh['frame'=8,'slab'=32] {'frame'}, use_global_device_ids=true, to_apply=%region_39.40 | all-reduce | flops 128 | bytes 1024 | tf_op jit(solution)/shard_map/psum | solution.py:199
  398.9 47.5 %all-reduce.7.cloned.1.call-done = f32[256,128]{1,0:T(8,128)} async-done(((f32[256,128]{1,0:T(8,128)}), f32[256,128]{1,0:T(8,128)}) %all-reduce.7.cloned.1.call-update) | async-done | bytes 131088 | tf_op jit(solution)/shard_map/psum | solution.py:199
  446.5 1.6 copy.78
  (88 shorter events, 3.1 us)
Async XLA Ops:
  7.2 14.4 %copy-start = (bf16[2,128]{1,0:T(2,128)(2,1)S(1)}, bf16[2,128]{1,0:T(2,128)(2,1)}, u32[]{:S(2)}) copy-start(bf16[2,128]{1,0:T(2,128)(2,1)} %param.22) | copy-start | bytes 1540
  7.2 45.5 %copy-start.10 = (bf16[2,8,64]{2,1,0:T(8,128)(2,1)S(1)}, bf16[2,8,64]{2,1,0:T(8,128)(2,1)}, u32[]{:S(2)}) copy-start(bf16[2,8,64]{2,1,0:T(8,128)(2,1)} %param.24) | copy-start | bytes 6148
  7.2 45.5 %copy-start.9 = (bf16[2,64,256]{2,1,0:T(8,128)(2,1)S(1)}, bf16[2,64,256]{2,1,0:T(8,128)(2,1)}, u32[]{:S(2)}) copy-start(bf16[2,64,256]{2,1,0:T(8,128)(2,1)} %param.25) | copy-start | bytes 196612
  7.2 372.6 %all-reduce.5.cloned.1.call-start = ((), (), s32[]{:S(2)}) async-start(), calls=%async_computation | async-start | bytes 524288 | tf_op jit(solution)/shard_map/psum | solution.py:180
  10.8 27.6 %collective-permute-start = (f32[2,3,128]{2,1,0:T(4,128)S(1)}, f32[2,3,128]{2,1,0:T(4,128)S(1)}, u32[]{:S(2)}, u32[]{:S(2)}) collective-permute-start(f32[2,3,128]{2,1,0:T(4,128)S(1)} %bitcast.180), channel_id=1, source_target_pairs={{0,1},{1,2},{2,3},{3,4},{4,5},{5,6},{6,7},{7,8},{8,9},{9,10},{10,1... | collective-permute-start | bytes 9224 | tf_op jit(solution)/shard_map/ppermute | solution.py:22
  14.9 24.3 %collective-permute-start.1 = (f32[2,3,128]{2,1,0:T(4,128)S(1)}, f32[2,3,128]{2,1,0:T(4,128)S(1)}, u32[]{:S(2)}, u32[]{:S(2)}) collective-permute-start(f32[2,3,128]{2,1,0:T(4,128)S(1)} %bitcast.181), channel_id=1, source_target_pairs={{1,0},{2,1},{3,2},{4,3},{5,4},{6,5},{7,6},{8,7},{9,8},{10,9},{11,1... | collective-permute-start | bytes 9224 | tf_op jit(solution)/shard_map/ppermute | solution.py:23
  25.1 59.3 %collective-permute-start.2 = (bf16[2,128,128]{2,1,0:T(8,128)(2,1)S(1)}, bf16[2,128,128]{2,1,0:T(8,128)(2,1)S(1)}, u32[]{:S(2)}, u32[]{:S(2)}) collective-permute-start(bf16[2,128,128]{2,1,0:T(8,128)(2,1)S(1)} %bitcast.164), channel_id=1, source_target_pairs={{0,1},{1,2},{2,3},{3,4},{4,5},{5,6},{6,7},{7,8},{8,9},{9,10},{10,1... | collective-permute-start | bytes 196616 | tf_op jit(solution)/shard_map/ppermute | solution.py:22
  26.8 57.6 %collective-permute-start.3 = (bf16[2,128,128]{2,1,0:T(8,128)(2,1)S(1)}, bf16[2,128,128]{2,1,0:T(8,128)(2,1)S(1)}, u32[]{:S(2)}, u32[]{:S(2)}) collective-permute-start(bf16[2,128,128]{2,1,0:T(8,128)(2,1)S(1)} %bitcast.165), channel_id=1, source_target_pairs={{1,0},{2,1},{3,2},{4,3},{5,4},{6,5},{7,6},{8,7},{9,8},{10,9},{11,1... | collective-permute-start | bytes 196616 | tf_op jit(solution)/shard_map/ppermute | solution.py:23
  84.4 11.0 %slice-start = ((s8[12582912]{0:T(1024)(128)(4,1)}), s8[4194304]{0:T(1024)(128)(4,1)S(1)}, s32[]{:S(2)}) async-start(s8[12582912]{0:T(1024)(128)(4,1)} %bitcast.186), calls=%async_computation.2 | async-start | bytes 8388608
  84.5 11.0 %slice-start.1 = ((s8[12582912]{0:T(1024)(128)(4,1)}), s8[4194304]{0:T(1024)(128)(4,1)S(1)}, s32[]{:S(2)}) async-start(s8[12582912]{0:T(1024)(128)(4,1)} %bitcast.186), calls=%async_computation.3 | async-start | bytes 8388608
  84.5 11.0 %slice-start.2 = ((s8[12582912]{0:T(1024)(128)(4,1)}), s8[4194304]{0:T(1024)(128)(4,1)S(1)}, s32[]{:S(2)}) async-start(s8[12582912]{0:T(1024)(128)(4,1)} %bitcast.186), calls=%async_computation.4 | async-start | bytes 8388608
  95.5 9.3 %copy-start.8 = (bf16[2,256,128]{2,1,0:T(8,128)(2,1)S(1)}, bf16[2,256,128]{2,1,0:T(8,128)(2,1)}, u32[]{:S(2)}) copy-start(bf16[2,256,128]{2,1,0:T(8,128)(2,1)} %param.26) | copy-start | bytes 393220
  95.5 9.6 %copy-start.1 = (bf16[2,128,128]{2,1,0:T(8,128)(2,1)S(1)}, bf16[2,128,128]{2,1,0:T(8,128)(2,1)}, u32[]{:S(2)}) copy-start(bf16[2,128,128]{2,1,0:T(8,128)(2,1)} %param.23) | copy-start | bytes 196612
  108.5 11.3 %collective-permute-start.4 = (bf16[2,128,128]{2,1,0:T(8,128)(2,1)S(1)}, bf16[2,128,128]{2,1,0:T(8,128)(2,1)S(1)}, u32[]{:S(2)}, u32[]{:S(2)}) collective-permute-start(bf16[2,128,128]{2,1,0:T(8,128)(2,1)S(1)} %bitcast.167), channel_id=1, source_target_pairs={{0,1},{1,2},{2,3},{3,4},{4,5},{5,6},{6,7},{7,8},{8,9},{9,10},{10,1... | collective-permute-start | bytes 196616 | tf_op jit(solution)/shard_map/ppermute | solution.py:22
  108.8 11.0 %collective-permute-start.5 = (bf16[2,128,128]{2,1,0:T(8,128)(2,1)S(1)}, bf16[2,128,128]{2,1,0:T(8,128)(2,1)S(1)}, u32[]{:S(2)}, u32[]{:S(2)}) collective-permute-start(bf16[2,128,128]{2,1,0:T(8,128)(2,1)S(1)} %bitcast.166), channel_id=1, source_target_pairs={{1,0},{2,1},{3,2},{4,3},{5,4},{6,5},{7,6},{8,7},{9,8},{10,9},{11,1... | collective-permute-start | bytes 196616 | tf_op jit(solution)/shard_map/ppermute | solution.py:23
  119.8 11.0 %slice-start.3 = ((s8[12582912]{0:T(1024)(128)(4,1)}), s8[4194304]{0:T(1024)(128)(4,1)S(1)}, s32[]{:S(2)}) async-start(s8[12582912]{0:T(1024)(128)(4,1)} %bitcast.188), calls=%async_computation.5 | async-start | bytes 8388608
  119.8 11.0 %slice-start.4 = ((s8[12582912]{0:T(1024)(128)(4,1)}), s8[4194304]{0:T(1024)(128)(4,1)S(1)}, s32[]{:S(2)}) async-start(s8[12582912]{0:T(1024)(128)(4,1)} %bitcast.188), calls=%async_computation.6 | async-start | bytes 8388608
  119.8 11.0 %slice-start.5 = ((s8[12582912]{0:T(1024)(128)(4,1)}), s8[4194304]{0:T(1024)(128)(4,1)S(1)}, s32[]{:S(2)}) async-start(s8[12582912]{0:T(1024)(128)(4,1)} %bitcast.188), calls=%async_computation.7 | async-start | bytes 8388608
  130.8 9.6 %copy-start.5 = (f32[128]{0:T(128)S(1)}, f32[128]{0:T(128)}, u32[]{:S(2)}) copy-start(f32[128]{0:T(128)} %param.27) | copy-start | bytes 1540
  130.8 9.9 %copy-start.2 = (s32[2,256]{1,0:T(2,128)S(1)}, s32[2,256]{1,0:T(2,128)}, u32[]{:S(2)}) copy-start(s32[2,256]{1,0:T(2,128)} %param.18) | copy-start | bytes 6148
  130.8 9.9 %copy-start.3 = (s32[2,1]{0,1:T(1,128)S(1)}, s32[2,1]{0,1:T(1,128)}, u32[]{:S(2)}) copy-start(s32[2,1]{0,1:T(1,128)} %param.19) | copy-start | bytes 28
  130.8 67.0 %copy-start.4 = (f32[2]{0:T(128)S(1)}, f32[2]{0:T(128)}, u32[]{:S(2)}) copy-start(f32[2]{0:T(128)} %param.29) | copy-start | bytes 28
  130.9 111.5 %copy-start.6 = (f32[16]{0:T(128)S(1)}, f32[16]{0:T(128)}, u32[]{:S(2)}) copy-start(f32[16]{0:T(128)} %param.32) | copy-start | bytes 196
  243.6 204.4 %copy-start.7 = (f32[16]{0:T(128)}, f32[16]{0:T(128)S(1)}, u32[]{:S(2)}) copy-start(f32[16]{0:T(128)S(1)} %get-tuple-element.161) | copy-start | bytes 196
  244.7 201.7 %all-reduce.7.cloned.1.call-start = ((), (), s32[]{:S(2)}) async-start(), calls=%async_computation.1 | async-start | bytes 262144 | tf_op jit(solution)/shard_map/psum | solution.py:199
Sparse Core Ops, SparseCore 0:
  244.9 134.8 all-reduce.4
  382.7 63.7 all-reduce.6
where the time goes:
time: 457 us; the launch traced here: 455 us
  waiting for transfers between devices  181 us (40%)
  blocking collectives  116 us (25%)
  matrix products  94.1 us (21%)
  starting transfers between devices  18.8 us (4%)
  local copies, waits for them, and re-layouts  16.2 us (4%)
  between operations  15.3 us (3%)
  other arithmetic  13.6 us (3%)
    psum x1, waiting for transfers between devices, per_device(): lax.psum((energy_loc, cos_part, sin_part, grad_up_loc, grad_out_loc), 'sl...  134 us
    psum x1, blocking collectives, per_device(): lax.psum((energy_loc, cos_part, sin_part, grad_up_loc, grad_out_loc), 'sl...  56 us
    psum x1, waiting for transfers between devices, per_device(): grad_up, grad_out = lax.psum((weighted_up, weighted_out), 'frame')  47.5 us
    dot_general x4, matrix products, edge_terms(): jnp.einsum('kbr,rc->kbc', picker.astype(jnp.bfloat16), feature_all, prefe...  40 us
    pmax x1, blocking collectives, per_device(): top_weight = lax.pmax(jnp.max(log_weight), 'frame')  29.7 us
    dot_general x2, matrix products, edge_terms(): jnp.einsum('kbr,dr->dkb', picker.astype(jnp.float32), coord_all, precisio...  25.3 us
    dot_general x4, matrix products, edge_terms(): jnp.einsum('kbh,hc->kbc', hidden, rad_second, preferred_element_type=jnp....  24.9 us
    psum x1, blocking collectives, per_device(): grad_up, grad_out = lax.psum((weighted_up, weighted_out), 'frame')  17.4 us
  transfers between devices with their start and end apart: 8, of which 2 were waited for; matrix products, arithmetic and copies ran while one was open for 15% of the time, Pallas kernels for 0%

commit v1 on v0

v1 whole, which is shorter than its diff:
```python
import functools

import jax
import jax.numpy as jnp
from jax import lax
from jax.experimental import pallas as pl
from jax.experimental.pallas import tpu as pltpu
from jax.sharding import PartitionSpec as P

slab_depth = 6.0
vector_scale = 0.2
target_var = 0.01
hydrogen_length = -0.64
LANES = 128
GROUP = 4
EXTRA = 8
VMEM_BYTES = 48 * 1024 * 1024

f32 = jnp.float32
bf16 = jnp.bfloat16


def lane_gather(table, index):
    numbers = lax.GatherDimensionNumbers(
        offset_dims=(),
        collapsed_slice_dims=(1,),
        start_index_map=(1,),
        operand_batching_dims=(0,),
        start_indices_batching_dims=(0,),
    )
    return lax.gather(
        table,
        index[..., None],
        numbers,
        slice_sizes=(1, 1),
        mode=lax.GatherScatterMode.PROMISE_IN_BOUNDS,
    )


def spread(row, rows):
    return jnp.broadcast_to(row, (rows, row.shape[1]))


def column(row):
    return spread(row, LANES).T


def as_row(col):
    wide = jnp.broadcast_to(col, (col.shape[0], LANES))
    if col.shape[0] < LANES:
        wide = jnp.concatenate([wide, jnp.zeros((LANES - col.shape[0], LANES), f32)], axis=0)
    return wide.T[0:1]


def sigmoid(values):
    return 0.5 * (1.0 + jnp.tanh(0.5 * values))


def silu(values):
    half = 0.5 * values
    return half + half * jnp.tanh(half)


def mm(a, b):
    return jnp.dot(a, b, preferred_element_type=f32)


def rad1_blocks(w_rad1):
    basis, hidden = w_rad1.shape
    w = w_rad1.astype(f32)
    wide = jnp.concatenate([w] * GROUP, axis=1)
    tall = jnp.concatenate([wide] * GROUP, axis=0)
    row = lax.broadcasted_iota(jnp.int32, tall.shape, 0) // basis
    col = lax.broadcasted_iota(jnp.int32, tall.shape, 1) // hidden
    tall = jnp.where(row == col, tall, 0.0)
    tall = jnp.concatenate([tall, jnp.zeros((LANES - GROUP * basis, GROUP * hidden), f32)], axis=0)
    return tall.T[:, : GROUP * basis].astype(bf16)


def transposed(w):
    return w.astype(f32).T.astype(bf16)


def pack_kernel(pos_ref, spec_ref, halo_ref, down_ref, up_ref):
    frames = pos_ref.shape[0]
    for f in range(frames):
        rows = [pos_ref[f, c : c + 1, :] for c in range(3)]
        rows.append(spec_ref[f : f + 1, :].astype(f32))
        for side, out in ((0, down_ref), (1, up_ref)):
            index = halo_ref[f, side : side + 1, :]
            lane = spread(index & (LANES - 1), 8)
            high = spread(index, 8) >= LANES
            for c, row in enumerate(rows):
                low_g = lane_gather(spread(row[:, :LANES], 8), lane)
                high_g = lane_gather(spread(row[:, LANES:], 8), lane)
                out[4 * f + c : 4 * f + c + 1, :] = jnp.where(high, high_g, low_g)[0:1]


def structure_kernel(slab_ref, count_ref, pos_ref, spec_ref, qt_ref, out_ref):
    frames, _, atoms = pos_ref.shape
    lift = slab_ref[0].astype(f32) * slab_depth
    number = lax.broadcasted_iota(jnp.int32, (1, atoms), 1)
    for f in range(frames):
        x, y, z = (pos_ref[f, c : c + 1, :] for c in range(3))
        phases = qt_ref[:, 0:1] * x + qt_ref[:, 1:2] * y + qt_ref[:, 2:3] * (z + lift)
        lengths = jnp.where(spec_ref[f : f + 1, :] == 1, 1.0, hydrogen_length)
        lengths = jnp.where(number < count_ref[f, 0], lengths, 0.0)
        cos_part = jnp.sum(lengths * jnp.cos(phases), axis=1, keepdims=True)
        sin_part = jnp.sum(lengths * jnp.sin(phases), axis=1, keepdims=True)
        out_ref[2 + f : 3 + f, :] = as_row(cos_part)
        out_ref[4 + f : 5 + f, :] = as_row(sin_part)
    out_ref[0:2, :] = jnp.zeros((2, LANES), f32)
    out_ref[6:8, :] = jnp.zeros((2, LANES), f32)


def basis_rows(dist_ref, f, i, first, atoms):
    center = lax.broadcasted_iota(jnp.int32, (8, atoms), 0).astype(f32)
    parts = []
    for j in range(first, first + GROUP):
        off = spread(dist_ref[f, 3, i, j : j + 1, :], 8) - center
        parts.append(jnp.exp(-(off * off)))
    return jnp.concatenate(parts, axis=0).astype(bf16)


def first_kernel(
    pos_ref,
    spec_ref,
    below_ref,
    above_ref,
    nb_ref,
    halo_ref,
    emb_ref,
    wmsg_ref,
    wr1_ref,
    wr2_ref,
    wup_ref,
    geo_ref,
    feat_ref,
    msg_ref,
    down_ref,
    up_ref,
    wgt_ref,
    acc_ref,
    w1_ref,
):
    frames, _, atoms = pos_ref.shape
    batches = nb_ref.shape[1]
    slots = batches * 8
    hidden = wr1_ref.shape[2]
    w1_ref[...] = rad1_blocks(wr1_ref[0])
    w2 = transposed(wr2_ref[0])
    w2s = jnp.concatenate([w2[:LANES]] * 2, axis=1)
    w2v = jnp.concatenate([w2[LANES:]] * 2, axis=1)
    wup = transposed(wup_ref[0])
    wmsg = transposed(wmsg_ref[1])
    emb = emb_ref[...]
    table = mm(emb, wmsg_ref[0]).astype(bf16).astype(f32)
    emb_cols = [column(emb[s : s + 1].astype(f32)) for s in range(2)]
    msg_cols = [column(table[s : s + 1]) for s in range(2)]
    scale = slots**-0.5
    for f in range(frames):
        for half in range(atoms // LANES):
            cols = slice(half * LANES, (half + 1) * LANES)
            for s in range(batches):
                index = nb_ref[f, s, :, cols]
                lane = index & (LANES - 1)
                block = index >> 7
                present = (index >= 0).astype(f32)

                def fetch(own_row, halo_row):
                    parts = [
                        own_row[:, :LANES],
                        own_row[:, LANES:],
                        below_ref[halo_row : halo_row + 1, :],
                        above_ref[halo_row : halo_row + 1, :],
                    ]
                    return parts

                squares = None
                offsets = []
                for c in range(3):
                    own_row = pos_ref[f, c : c + 1, :]
                    parts = fetch(own_row, 4 * f + c)
                    if c == 2:
                        parts[2] = parts[2] - slab_depth
                        parts[3] = parts[3] + slab_depth
                    got = [lane_gather(spread(p, 8), lane) for p in parts]
                    there = jnp.where(
                        block == 0,
                        got[0],
                        jnp.where(block == 1, got[1], jnp.where(block == 2, got[2], got[3])),
                    )
                    offset = there - own_row[:, cols]
                    offsets.append(offset)
                    geo_ref[f, c, s, :, cols] = offset
                    squares = offset * offset if squares is None else squares + offset * offset
                geo_ref[f, 3, s, :, cols] = jnp.sqrt(squares)
                parts = fetch(spec_ref[f : f + 1, :].astype(f32), 4 * f + 3)
                got = [lane_gather(spread(p, 8), lane) for p in parts]
                kind = jnp.where(
                    block == 0,
                    got[0],
                    jnp.where(block == 1, got[1], jnp.where(block == 2, got[2], got[3])),
                )
                kinds = (present * (1.0 - kind), present * kind)
                for k in range(2):
                    wgt_ref[k, s, :, cols] = kinds[k]
                    for c in range(3):
                        wgt_ref[2 * (c + 1) + k, s, :, cols] = offsets[c] * kinds[k]
        acc_ref[...] = jnp.zeros_like(acc_ref)

        def step(i, carry):
            acts = []
            for first in range(0, 8, GROUP):
                pre = mm(w1_ref[...], basis_rows(geo_ref, f, i, first, atoms))
                acts.append(silu(pre).astype(bf16).astype(f32))
            for half in range(atoms // LANES):
                cols = slice(half * LANES, (half + 1) * LANES)
                for part in range(0, hidden, 32):
                    hid = []
                    for j in range(8):
                        at = (j % GROUP) * hidden + part
                        hid.append(acts[j // GROUP][at : at + 32, cols])
                    for k in range(8):
                        total = acc_ref[k, part : part + 32, cols]
                        for j in range(8):
                            total = total + wgt_ref[k, i, j : j + 1, cols] * hid[j]
                        acc_ref[k, part : part + 32, cols] = total
            return carry

        lax.fori_loop(0, batches, step, 0)

        def project(k, w):
            total = acc_ref[k]
            high = total.astype(bf16)
            low = (total - high.astype(f32)).astype(bf16)
            return mm(w, jnp.concatenate([high, low], axis=0))

        cols0 = jnp.concatenate([msg_cols[0]] * 2, axis=1)
        cols1 = jnp.concatenate([msg_cols[1]] * 2, axis=1)
        scalar = scale * (cols0 * project(0, w2s) + cols1 * project(1, w2s))
        squared = None
        for c in range(3):
            vec = (scale * vector_scale) * (
                cols0 * project(2 * c + 2, w2v) + cols1 * project(2 * c + 3, w2v)
            )
            squared = vec * vec if squared is None else squared + vec * vec
        mixed = jnp.concatenate([scalar, squared], axis=0).astype(bf16)
        update = mm(wup, mixed)
        e0 = jnp.concatenate([emb_cols[0]] * 2, axis=1)
        e1 = jnp.concatenate([emb_cols[1]] * 2, axis=1)
        features = jnp.where(spec_ref[f : f + 1, :] == 1, e1, e0) + silu(update)
        feat_ref[f] = features
        message = mm(wmsg, features.astype(bf16)).astype(bf16)
        msg_ref[f] = message
        message = message.astype(f32)
        for side, out in ((0, down_ref), (1, up_ref)):
            index = halo_ref[f, side : side + 1, :]
            lane = spread(index & (LANES - 1), LANES)
            low_g = lane_gather(message[:, :LANES], lane)
            high_g = lane_gather(message[:, LANES:], lane)
            out[f] = jnp.where(index >= LANES, high_g, low_g).astype(bf16)


def hidden_kernel(geo_ref, nb_ref, wr1_ref, out_ref, w1_ref):
    frames, batches, _, atoms = nb_ref.shape
    hidden = wr1_ref.shape[2]
    w1_ref[...] = rad1_blocks(wr1_ref[1])
    for f in range(frames):

        def step(i, carry):
            for first in range(0, 8, GROUP):
                act = silu(mm(w1_ref[...], basis_rows(geo_ref, f, i, first, atoms)))
                for j in range(GROUP):
                    here = nb_ref[f, i, first + j : first + j + 1, :] >= 0
                    rows = slice(j * hidden, (j + 1) * hidden)
                    kept = jnp.where(here, act[rows], 0.0).astype(bf16)
                    out_ref[f, i, (first + j) * hidden : (first + j + 1) * hidden, :] = kept
            return carry

        lax.fori_loop(0, batches, step, 0)


def second_kernel(
    rows_each,
    count_ref,
    spec_ref,
    eshift_ref,
    nb_ref,
    geo_ref,
    hid_ref,
    feat_ref,
    msg_ref,
    below_ref,
    above_ref,
    wr2_ref,
    wup_ref,
    wout_ref,
    struct_ref,
    energy_ref,
    chunk_ref,
    acc_ref,
    src_ref,
    w2_ref,
):
    frames, batches, _, atoms = nb_ref.shape
    slots = batches * 8
    hidden = wr2_ref.shape[1]
    chunks = chunk_ref.shape[0]
    w2_ref[...] = transposed(wr2_ref[1])
    wup = transposed(wup_ref[1])
    wout = jnp.concatenate([column(wout_ref[...])] * 2, axis=1)
    scale = slots**-0.5
    number = lax.broadcasted_iota(jnp.int32, (1, atoms), 1)
    extra = [None] * EXTRA
    for f in range(frames):
        src_ref[0] = msg_ref[f, :, :LANES].astype(f32)
        src_ref[1] = msg_ref[f, :, LANES:].astype(f32)
        src_ref[2] = below_ref[f].astype(f32)
        src_ref[3] = above_ref[f].astype(f32)
        acc_ref[...] = jnp.zeros_like(acc_ref)

        def step(i, carry):
            filters = [
                mm(w2_ref[...], hid_ref[f, i, j * hidden : (j + 1) * hidden, :]) for j in range(8)
            ]
            width = 32
            for half in range(atoms // LANES):
                cols = slice(half * LANES, (half + 1) * LANES)
                index = [nb_ref[f, i, j : j + 1, cols] for j in range(8)]
                lane = [spread(v & (LANES - 1), width) for v in index]
                block = [spread(v >> 7, width) for v in index]
                offset = [[geo_ref[f, c, i, j : j + 1, cols] for c in range(3)] for j in range(8)]
                for part in range(0, LANES, width):
                    rows = slice(part, part + width)
                    total = [acc_ref[k, rows, cols] for k in range(4)]
                    for j in range(8):
                        got = [lane_gather(src_ref[b, rows, :], lane[j]) for b in range(4)]
                        there = jnp.where(
                            block[j] < 2,
                            jnp.where(block[j] == 1, got[1], got[0]),
                            jnp.where(block[j] == 2, got[2], got[3]),
                        )
                        total[0] = total[0] + filters[j][rows, cols] * there
                        vec = filters[j][LANES + part : LANES + part + width, cols] * there
                        for c in range(3):
                            total[c + 1] = total[c + 1] + offset[j][c] * vec
                    for k in range(4):
                        acc_ref[k, rows, cols] = total[k]
            return carry

        lax.fori_loop(0, batches, step, 0)

        scalar = scale * acc_ref[0]
        squared = None
        for c in range(3):
            vec = (scale * vector_scale) * acc_ref[c + 1]
            squared = vec * vec if squared is None else squared + vec * vec
        mixed = jnp.concatenate([scalar, squared], axis=0).astype(bf16)
        update = mm(wup, mixed)
        gate = sigmoid(update)
        features = feat_ref[f] + update * gate
        living = (number < count_ref[f, 0]).astype(f32)
        slope = (living * wout * (gate * (1.0 + update * (1.0 - gate)))).astype(bf16)
        kind = spec_ref[f : f + 1, :]
        readout = jnp.sum(features * wout, axis=0, keepdims=True)
        energy = living * (readout + jnp.where(kind == 1, eshift_ref[1], eshift_ref[0]))
        energy_ref[f : f + 1, :] = energy
        grad = lax.dot_general(mixed, slope, (((1,), (1,)), ((), ())), preferred_element_type=f32)
        chunk_ref[:, f * rows_each : (f + 1) * rows_each, :] = grad.reshape(
            chunks, rows_each, LANES
        )
        extra[f] = as_row(jnp.sum(living * features, axis=1, keepdims=True))
        extra[2 + f] = struct_ref[2 + f : 3 + f, :]
        extra[4 + f] = struct_ref[4 + f : 5 + f, :]
        extra[6 + f] = jnp.broadcast_to(jnp.sum(energy, axis=1, keepdims=True), (1, LANES))
    block = jnp.concatenate(extra, axis=0)
    chunk_ref[:, frames * rows_each :, :] = jnp.broadcast_to(block[None], (chunks, EXTRA, LANES))


def total_kernel(uref_ref, beta_ref, in_ref, out_ref):
    rows = in_ref.shape[1]
    total = in_ref[0]
    for s in range(1, in_ref.shape[0]):
        total = total + in_ref[s]
    for d in range(out_ref.shape[0]):
        out_ref[d] = total
    for f in range(2):
        row = total[rows - 2 + f : rows - 1 + f]
        log_weight = -beta_ref[0] * (row - uref_ref[f])
        for d in range(out_ref.shape[0]):
            out_ref[d, rows - 2 + f : rows - 1 + f, :] = log_weight


def final_kernel(rows_each, atoms_all, beta_ref, in_ref, target_ref, chunk_ref, mean_ref, out_ref):
    devices = in_ref.shape[0]
    q = target_ref.shape[1]
    base = 2 * rows_each

    def gather(at):
        return jnp.concatenate([in_ref[d, base + at : base + at + 2, :] for d in range(devices)], 0)

    cos_tot, sin_tot, log_weight = gather(2), gather(4), gather(6)
    structure = ((cos_tot * cos_tot + sin_tot * sin_tot) / atoms_all)[:, :q]
    scaled = jnp.exp(log_weight - jnp.max(log_weight, axis=0, keepdims=True))
    weights = scaled / jnp.sum(scaled, axis=0, keepdims=True)
    mean = jnp.sum(weights[:, :q] * structure, axis=0, keepdims=True)
    slope_sq = (mean - target_ref[...]) / target_var
    observed = jnp.sum(structure * slope_sq, axis=1, keepdims=True)
    average = jnp.sum(mean * slope_sq, axis=1, keepdims=True)
    factor = (-beta_ref[0]) * weights * (observed - average)
    grad = jnp.zeros((rows_each, LANES), f32)
    for d in range(devices):
        for f in range(2):
            k = 2 * d + f
            grad = grad + factor[k : k + 1] * in_ref[d, f * rows_each : (f + 1) * rows_each, :]
    mean_ref[...] = mean
    out_ref[...] = jnp.sum(factor * gather(0), axis=0, keepdims=True)
    for s in range(chunk_ref.shape[0]):
        chunk_ref[s] = grad


VM = pl.BlockSpec(memory_space=pltpu.VMEM)
SM = pl.BlockSpec(memory_space=pltpu.SMEM)


def call(kernel, name, ins, outs, scratch, *operands):
    return pl.pallas_call(
        kernel,
        name=name,
        out_shape=outs,
        in_specs=ins,
        out_specs=jax.tree.map(lambda _: VM, outs),
        scratch_shapes=scratch,
        compiler_params=pltpu.CompilerParams(vmem_limit_bytes=VMEM_BYTES),
    )(*operands)


def array(shape, dtype=f32):
    return jax.ShapeDtypeStruct(shape, dtype)


def per_device(
    positions,
    species,
    atom_count,
    halo_index,
    neighbours,
    embedding,
    w_msg,
    w_rad1,
    w_rad2,
    w_up,
    w_out,
    e_shift,
    u_reference,
    inverse_temp,
    q_vectors,
    s_target,
):
    frames, _, atoms = positions.shape
    slots = neighbours.shape[1]
    halo = halo_index.shape[2]
    hidden = w_rad1.shape[2]
    channels = w_msg.shape[1]
    neighbours = neighbours.reshape(frames, slots // 8, 8, atoms)
    slab_devs = lax.axis_size("slab")
    frame_devs = lax.axis_size("frame")
    rows_each = 2 * channels // slab_devs
    chunk_rows = frames * rows_each + EXTRA
    up = [(i, (i + 1) % slab_devs) for i in range(slab_devs)]
    down = [(j, i) for i, j in up]

    rows = array((4 * frames, halo))
    leave_down, leave_up = call(
        pack_kernel, "halo_rows", [VM] * 3, (rows, rows), [], positions, species, halo_index
    )
    below = lax.ppermute(leave_up, "slab", up)
    above = lax.ppermute(leave_down, "slab", down)
    slab_pos = lax.axis_index("slab").reshape(1)
    structure = call(
        structure_kernel,
        "structure_sums",
        [SM, SM, VM, VM, VM],
        array((EXTRA, LANES)),
        [],
        slab_pos,
        atom_count,
        positions,
        species,
        q_vectors.T,
    )
    halo_rows = array((frames, channels, halo), bf16)
    geometry, features, message, msg_down, msg_up = call(
        first_kernel,
        "first_layer",
        [VM] * 11,
        (
            array((frames, 4, slots // 8, 8, atoms)),
            array((frames, channels, atoms)),
            array((frames, channels, atoms), bf16),
            halo_rows,
            halo_rows,
        ),
        [
            pltpu.VMEM((8, slots // 8, 8, atoms), f32),
            pltpu.VMEM((8, hidden, atoms), f32),
            pltpu.VMEM((GROUP * hidden, GROUP * w_rad1.shape[1]), bf16),
        ],
        positions,
        species,
        below,
        above,
        neighbours,
        halo_index,
        embedding,
        w_msg,
        w_rad1,
        w_rad2,
        w_up,
    )
    msg_below = lax.ppermute(msg_up, "slab", up)
    msg_above = lax.ppermute(msg_down, "slab", down)
    radial_hidden = call(
        hidden_kernel,
        "radial_hidden",
        [VM] * 3,
        array((frames, slots // 8, 8 * hidden, atoms), bf16),
        [pltpu.VMEM((GROUP * hidden, GROUP * w_rad1.shape[1]), bf16)],
        geometry,
        neighbours,
        w_rad1,
    )
    atom_energy, chunks = call(
        functools.partial(second_kernel, rows_each),
        "second_layer",
        [SM, VM, SM] + [VM] * 11,
        (array((frames, atoms)), array((slab_devs, chunk_rows, LANES))),
        [
            pltpu.VMEM((4, channels, atoms), f32),
            pltpu.VMEM((4, channels, LANES), f32),
            pltpu.VMEM((2 * channels, hidden), bf16),
        ],
        atom_count,
        species,
        e_shift,
        neighbours,
        geometry,
        radial_hidden,
        features,
        message,
        msg_below,
        msg_above,
        w_rad2,
        w_up,
        w_out.reshape(1, channels),
        structure,
    )
    chunks = lax.all_to_all(chunks, "slab", 0, 0, tiled=True)
    totals = call(
        total_kernel,
        "slab_totals",
        [SM, SM, VM],
        array((frame_devs, chunk_rows, LANES)),
        [],
        u_reference,
        inverse_temp,
        chunks,
    )
    totals = lax.all_to_all(totals, "frame", 0, 0, tiled=True)
    q = s_target.shape[0]
    grad_rows, mean_structure, grad_out = call(
        functools.partial(final_kernel, rows_each, atoms * slab_devs),
        "reweighted",
        [SM, VM, VM],
        (array((slab_devs, rows_each, LANES)), array((1, q)), array((1, channels))),
        [],
        inverse_temp,
        totals,
        s_target.reshape(1, q),
    )
    grad_up = lax.all_to_all(grad_rows, "slab", 0, 0, tiled=True)
    return (
        atom_energy,
        mean_structure.reshape(q),
        grad_up.reshape(2 * channels, channels),
        grad_out.reshape(channels),
    )


def solution(mesh):
    in_specs = (
        P("frame", None, "slab"),
        P("frame", "slab"),
        P("frame", "slab"),
        P("frame", None, "slab"),
        P("frame", None, "slab"),
        P(),
        P(),
        P(),
        P(),
        P(),
        P(),
        P(),
        P("frame"),
        P(),
        P(),
        P(),
    )
    out_specs = (P("frame", "slab"), P(), P(), P())
    return jax.shard_map(
        per_device, mesh=mesh, in_specs=in_specs, out_specs=out_specs, check_vma=False
    )
```

time: 457 us -> 106 us (0.23)
  waiting for transfers between devices: 181 us -> 11.8 us
  matrix products: 94.1 us -> 0 us
  blocking collectives: 116 us -> 27.1 us
  Pallas kernels: 0 us -> 34 us
  between operations: 15.3 us -> 1.45 us
  other arithmetic: 13.6 us -> 0 us
  local copies, waits for them, and re-layouts: 16.2 us -> 11.4 us
    psum x2 -> x0, waiting for transfers between devices: 181 us -> none  [the longest x1 134 us: per_device(): lax.psum((energy_loc, cos_part, sin_part, grad_up_loc, grad_out_loc), 'sl...]
    dot_general x17 -> x0, matrix products: 94.1 us -> none  [the longest x4 40 us: edge_terms(): jnp.einsum('kbr,rc->kbc', picker.astype(jnp.bfloat16), feature_all, prefe...]
    psum x3 -> x0, blocking collectives: 86.2 us -> none  [the longest x1 56 us: per_device(): lax.psum((energy_loc, cos_part, sin_part, grad_up_loc, grad_out_loc), 'sl...]
    pallas_call x0 -> x7, Pallas kernels: none -> 34 us  [call(): pl.pallas_call(kernel, name=name, out_shape=outs, in_specs=ins, out_specs...]
    pmax x1 -> x0, blocking collectives: 29.7 us -> none  [per_device(): top_weight = lax.pmax(jnp.max(log_weight), 'frame')]
    all_to_all x0 -> x2, blocking collectives: none -> 27.1 us  [the longest x1 14.1 us: per_device(): totals = lax.all_to_all(totals, 'frame', 0, 0, tiled=True)]
    all_to_all x0 -> x1, waiting for transfers between devices: none -> 10.9 us  [per_device(): chunks = lax.all_to_all(chunks, 'slab', 0, 0, tiled=True)]
    gather x8 -> x0, local copies, waits for them, and re-layouts: 10.6 us -> none  [the longest x4 6.63 us: per_device(): pick_rows = jax.vmap(lambda source, chosen: source[chosen])]
  transfers between devices with their start and end apart: 8 -> 5, of which waited for: 2 -> 2; matrix products, arithmetic and copies ran while one was open for 15% -> 1% of each run, Pallas kernels for 0% -> 4%
where the time goes in v1:
time: 106 us; the launch traced here: 105 us
  Pallas kernels  34 us (32%)
  blocking collectives  27.1 us (26%)
  starting transfers between devices  19.3 us (18%)
  waiting for transfers between devices  11.8 us (11%)
  local copies, waits for them, and re-layouts  11.4 us (11%)
  between operations  1.45 us (1%)
    pallas_call x7, Pallas kernels, call(): pl.pallas_call(kernel, name=name, out_shape=outs, in_specs=ins, out_specs...  34 us
    all_to_all x1, blocking collectives, per_device(): totals = lax.all_to_all(totals, 'frame', 0, 0, tiled=True)  14.1 us
    all_to_all x1, blocking collectives, per_device(): grad_up = lax.all_to_all(grad_rows, 'slab', 0, 0, tiled=True)  13 us
    unnamed x42, local copies, waits for them, and re-layouts  11.4 us
    all_to_all x1, waiting for transfers between devices, per_device(): chunks = lax.all_to_all(chunks, 'slab', 0, 0, tiled=True)  10.9 us
    ppermute x1, starting transfers between devices, per_device(): above = lax.ppermute(leave_down, 'slab', down)  6.65 us
    all_to_all x1, starting transfers between devices, per_device(): chunks = lax.all_to_all(chunks, 'slab', 0, 0, tiled=True)  5.51 us
    ppermute x1, starting transfers between devices, per_device(): msg_above = lax.ppermute(msg_down, 'slab', down)  4.94 us
  transfers between devices with their start and end apart: 5, of which 2 were waited for; matrix products, arithmetic and copies ran while one was open for 1% of the time, Pallas kernels for 4%

profile of v1, /device:TPU:1, one launch (start us, length us, event | category | flops | bytes accessed | tf_op | source)
XLA Modules:
  0.0 105.1 jit_solution(10217964743690038051)
XLA Ops:
  0.6 0.0 copy-start.10
  0.6 0.0 copy-start.16
  0.7 0.0 copy-start.15
  0.7 0.7 copy.21.pos_ref
  1.4 0.0 copy-start.8
  1.4 0.7 copy-done.8
  2.1 0.7 copy-done.13
  2.7 0.1 halo_rows.1
  2.9 2.1 %collective-permute-start = (f32[8,128]{1,0:T(8,128)S(1)}, f32[8,128]{1,0:T(8,128)S(1)}, u32[]{:S(2)}, u32[]{:S(2)}) collective-permute-start(f32[8,128]{1,0:T(8,128)S(1)} %get-tuple-element.16), channel_id=1, source_target_pairs={{0,1},{1,2},{2,3},{3,4},{4,5},{5,6},{6,7},{7,8},{8,9},{9,10},{10,1... | collective-permute-start | bytes 12296 | tf_op jit(solution)/shard_map/ppermute | solution.py:478
  5.0 6.6 %collective-permute-start.1 = (f32[8,128]{1,0:T(8,128)S(1)}, f32[8,128]{1,0:T(8,128)S(1)}, u32[]{:S(2)}, u32[]{:S(2)}) collective-permute-start(f32[8,128]{1,0:T(8,128)S(1)} %get-tuple-element.17), channel_id=1, source_target_pairs={{1,0},{2,1},{3,2},{4,3},{5,4},{6,5},{7,6},{8,7},{9,8},{10,9},{11,1... | collective-permute-start | bytes 12296 | tf_op jit(solution)/shard_map/ppermute | solution.py:479
  11.6 0.9 collective-permute-done.below_ref
  12.5 0.0 collective-permute-done.1.above_ref
  12.5 0.9 copy-done
  13.4 0.9 copy-done.3
  14.3 0.8 copy-done.5
  15.2 0.8 copy-done.7
  16.0 0.7 copy-done.11
  16.7 0.7 copy-done.14
  17.4 9.3 %first_layer.1 = (f32[2,4,6,8,256]{4,3,2,1,0:T(8,128)S(1)}, f32[2,128,256]{2,1,0:T(8,128)S(1)}, bf16[2,128,256]{2,1,0:T(8,128)(2,1)S(1)}, bf16[2,128,128]{2,1,0:T(8,128)(2,1)S(1)}, bf16[2,128,128]{2,1,0:T(8,128)(2,1)S(1)}) custom-call(f32[2,3,256]{2,1,0:T(4,128)S(1)} %copy.21.pos_ref, s32[2,256]{1,0:T(2,128)S(1)} %copy-done.8, ...), custom_call_target="tpu_custom_call" | custom-call | tf_op jit(solution)/shard_map/first_layer/pallas_call | solution.py:428
  26.6 0.1 collective-permute-start.2
  26.7 4.9 %collective-permute-start.3 = (bf16[2,128,128]{2,1,0:T(8,128)(2,1)S(1)}, bf16[2,128,128]{2,1,0:T(8,128)(2,1)S(1)}, u32[]{:S(2)}, u32[]{:S(2)}) collective-permute-start(bf16[2,128,128]{2,1,0:T(8,128)(2,1)S(1)} %get-tuple-element.22), channel_id=1, source_target_pairs={{1,0},{2,1},{3,2},{4,3},{5,4},{6,5},{7,6},{8,7},{9,8},{10,9},{11,1... | collective-permute-start | bytes 196616 | tf_op jit(solution)/shard_map/ppermute | solution.py:523
  31.7 0.7 copy.25.count_ref
  32.4 0.8 copy.22
  33.2 0.7 copy-done.9
  33.9 0.9 structure_sums.1.struct_ref
  34.7 0.9 copy-done.1
  35.6 0.7 copy-done.12
  36.3 3.4 %radial_hidden.1.hid_ref = bf16[2,6,512,256]{3,2,1,0:T(8,128)(2,1)S(1)} custom-call(f32[2,4,6,8,256]{4,3,2,1,0:T(8,128)S(1)} %get-tuple-element.18.geo_ref, s32[2,6,8,256]{3,2,1,0:T(8,128)S(1)} %bitcast.9, bf16[2,8,64]{2,1,0:T(8,128)(2,1)S(1)} %copy-done.12), custom_call_target="tpu_custom_call" | custom-call | tf_op jit(solution)/shard_map/radial_hidden/pallas_call | solution.py:428
  39.7 0.0 copy-start.18
  39.8 0.0 copy-start.17
  39.8 0.0 collective-permute-done.2.below_ref
  39.8 0.0 collective-permute-done.3.above_ref
  39.8 0.0 copy-done.10
  39.8 0.0 copy-done.16
  39.8 0.0 copy-done.15
  39.8 0.0 copy-done.2
  39.8 0.0 copy-done.4
  39.8 0.0 copy-done.6
  39.9 19.1 %second_layer.1 = (f32[2,256]{1,0:T(2,128)}, f32[32,24,128]{2,1,0:T(8,128)}) custom-call(s32[2,1]{1,0:T(2,128)S(1)} %copy.25.count_ref, s32[2,256]{1,0:T(2,128)S(1)} %copy-done.10, f32[2]{0:T(128)S(1)} %copy-done.15, s32[2,6,8,256]{3,2,1,0:T(8,128)S(1)} %bitcast.10, f32[2,4,6,8,256]{4,3,2,1,0:T(8,128)S(1)} %get-tuple-element.18.geo_ref, ...), custom_call_target="tpu_custom_call" | custom-call | tf_op jit(solution)/shard_map/second_layer/pallas_call | solution.py:428
  59.0 5.5 %all-to-all-start = ((f32[32,24,128]{2,1,0:T(8,128)}), f32[32,24,128]{2,1,0:T(8,128)S(1)}, u32[]{:S(2)}, u32[]{:S(2)}) async-start(f32[32,24,128]{2,1,0:T(8,128)} %get-tuple-element.24), calls=%async_computation | async-start | bytes 786432 | tf_op jit(solution)/shard_map/all_to_all | solution.py:559
  65.2 10.9 %all-to-all-done.in_ref = f32[32,24,128]{2,1,0:T(8,128)S(1)} async-done(((f32[32,24,128]{2,1,0:T(8,128)}), f32[32,24,128]{2,1,0:T(8,128)S(1)}, u32[]{:S(2)}, u32[]{:S(2)}) %all-to-all-start) | async-done | bytes 393248 | tf_op jit(solution)/shard_map/all_to_all | solution.py:559
  76.0 0.0 copy-done.18
  76.0 0.6 slab_totals.1
  76.6 14.1 %all_to_all.15.in_ref = f32[8,24,128]{2,1,0:T(8,128)S(1)} all-to-all(f32[8,24,128]{2,1,0:T(8,128)S(1)} %slab_totals.1), channel_id=1, replica_groups=mesh['frame'=8,'slab'=32] {'frame'}, dimensions={0} | all-to-all | bytes 196608 | tf_op jit(solution)/shard_map/all_to_all | solution.py:570
  90.7 0.0 copy-done.17
  90.7 0.6 reweighted.1
  91.4 13.0 %all_to_all.16 = f32[32,8,128]{2,1,0:T(8,128)S(1)} all-to-all(f32[32,8,128]{2,1,0:T(8,128)S(1)} %get-tuple-element.26), channel_id=1, replica_groups=mesh['frame'=8,'slab'=32] {'slab'}, dimensions={0} | all-to-all | bytes 262144 | tf_op jit(solution)/shard_map/all_to_all | solution.py:582
  104.4 0.7 copy.28
  (13 shorter events, 0.0 us)
Async XLA Ops:
  0.6 39.2 %copy-start.10 = (s32[2,256]{1,0:T(2,128)S(1)}, s32[2,256]{1,0:T(2,128)}, u32[]{:S(2)}) copy-start(s32[2,256]{1,0:T(2,128)} %spec_ref.7) | copy-start | bytes 6148
  0.6 39.2 %copy-start.16 = (f32[128]{0:T(128)S(1)}, f32[128]{0:T(128)}, u32[]{:S(2)}) copy-start(f32[128]{0:T(128)} %param.26) | copy-start | bytes 1540
  0.7 39.2 %copy-start.15 = (f32[2]{0:T(128)S(1)}, f32[2]{0:T(128)}, u32[]{:S(2)}) copy-start(f32[2]{0:T(128)} %eshift_ref.1) | copy-start | bytes 28
  1.4 0.7 copy-start.8
  2.1 0.7 copy-start.13
  2.9 9.7 %collective-permute-start = (f32[8,128]{1,0:T(8,128)S(1)}, f32[8,128]{1,0:T(8,128)S(1)}, u32[]{:S(2)}, u32[]{:S(2)}) collective-permute-start(f32[8,128]{1,0:T(8,128)S(1)} %get-tuple-element.16), channel_id=1, source_target_pairs={{0,1},{1,2},{2,3},{3,4},{4,5},{5,6},{6,7},{7,8},{8,9},{9,10},{10,1... | collective-permute-start | bytes 12296 | tf_op jit(solution)/shard_map/ppermute | solution.py:478
  5.0 7.6 %collective-permute-start.1 = (f32[8,128]{1,0:T(8,128)S(1)}, f32[8,128]{1,0:T(8,128)S(1)}, u32[]{:S(2)}, u32[]{:S(2)}) collective-permute-start(f32[8,128]{1,0:T(8,128)S(1)} %get-tuple-element.17), channel_id=1, source_target_pairs={{1,0},{2,1},{3,2},{4,3},{5,4},{6,5},{7,6},{8,7},{9,8},{10,9},{11,1... | collective-permute-start | bytes 12296 | tf_op jit(solution)/shard_map/ppermute | solution.py:479
  12.5 0.9 copy-start
  13.4 0.9 copy-start.3
  14.3 0.8 copy-start.5
  15.2 0.8 copy-start.7
  16.0 0.7 copy-start.11
  16.7 0.7 copy-start.14
  17.4 22.5 %copy-start.2 = (s32[2,48,256]{2,1,0:T(8,128)S(1)}, s32[2,48,256]{2,1,0:T(8,128)}, u32[]{:S(2)}) copy-start(s32[2,48,256]{2,1,0:T(8,128)} %param.20) | copy-start | bytes 294916
  17.4 22.5 %copy-start.4 = (bf16[2,256,128]{2,1,0:T(8,128)(2,1)S(1)}, bf16[2,256,128]{2,1,0:T(8,128)(2,1)}, u32[]{:S(2)}) copy-start(bf16[2,256,128]{2,1,0:T(8,128)(2,1)} %wup_ref.3) | copy-start | bytes 393220
  17.4 22.5 %copy-start.6 = (bf16[2,64,256]{2,1,0:T(8,128)(2,1)S(1)}, bf16[2,64,256]{2,1,0:T(8,128)(2,1)}, u32[]{:S(2)}) copy-start(bf16[2,64,256]{2,1,0:T(8,128)(2,1)} %wr2_ref.3) | copy-start | bytes 196612
  26.6 13.1 %collective-permute-start.2 = (bf16[2,128,128]{2,1,0:T(8,128)(2,1)S(1)}, bf16[2,128,128]{2,1,0:T(8,128)(2,1)S(1)}, u32[]{:S(2)}, u32[]{:S(2)}) collective-permute-start(bf16[2,128,128]{2,1,0:T(8,128)(2,1)S(1)} %get-tuple-element.21), channel_id=1, source_target_pairs={{0,1},{1,2},{2,3},{3,4},{4,5},{5,6},{6,7},{7,8},{8,9},{9,10},{10,1... | collective-permute-start | bytes 196616 | tf_op jit(solution)/shard_map/ppermute | solution.py:522
  26.7 13.1 %collective-permute-start.3 = (bf16[2,128,128]{2,1,0:T(8,128)(2,1)S(1)}, bf16[2,128,128]{2,1,0:T(8,128)(2,1)S(1)}, u32[]{:S(2)}, u32[]{:S(2)}) collective-permute-start(bf16[2,128,128]{2,1,0:T(8,128)(2,1)S(1)} %get-tuple-element.22), channel_id=1, source_target_pairs={{1,0},{2,1},{3,2},{4,3},{5,4},{6,5},{7,6},{8,7},{9,8},{10,9},{11,1... | collective-permute-start | bytes 196616 | tf_op jit(solution)/shard_map/ppermute | solution.py:523
  33.2 0.7 copy-start.9
  34.7 0.9 copy-start.1
  35.6 0.7 copy-start.12
  39.7 36.3 %copy-start.18 = (f32[2]{0:T(128)S(1)}, f32[2]{0:T(128)}, u32[]{:S(2)}) copy-start(f32[2]{0:T(128)} %uref_ref.1) | copy-start | bytes 28
  39.8 51.0 %copy-start.17 = (f32[16]{0:T(128)S(1)}, f32[16]{0:T(128)}, u32[]{:S(2)}) copy-start(f32[16]{0:T(128)} %param.31) | copy-start | bytes 196
  59.0 17.0 %all-to-all-start = ((f32[32,24,128]{2,1,0:T(8,128)}), f32[32,24,128]{2,1,0:T(8,128)S(1)}, u32[]{:S(2)}, u32[]{:S(2)}) async-start(f32[32,24,128]{2,1,0:T(8,128)} %get-tuple-element.24), calls=%async_computation | async-start | bytes 786432 | tf_op jit(solution)/shard_map/all_to_all | solution.py:559

commit v2 on v1

--- a/solution.py
+++ b/solution.py
@@ -14,6 +14,11 @@
 LANES = 128
 GROUP = 4
 EXTRA = 8
+XLU = 32
+UN1 = 6
+UNH = 3
+UN2 = 2
+WIDTH = 32
 VMEM_BYTES = 48 * 1024 * 1024
 
 f32 = jnp.float32
@@ -81,10 +86,20 @@
     return w.astype(f32).T.astype(bf16)
 
 
-def pack_kernel(pos_ref, spec_ref, halo_ref, down_ref, up_ref):
-    frames = pos_ref.shape[0]
+def fetch_all(sems, pairs):
+    copies = [pltpu.make_async_copy(src, dst, sems.at[i]) for i, (src, dst) in enumerate(pairs)]
+    for copy in copies:
+        copy.start()
+    return copies
+
+
+def pack_kernel(pos_hbm, spec_hbm, halo_hbm, down_ref, up_ref, pos_ref, spec_ref, halo_ref, sems):
+    pairs = ((pos_hbm, pos_ref), (spec_hbm, spec_ref), (halo_hbm, halo_ref))
+    for copy in fetch_all(sems, pairs):
+        copy.wait()
+    frames = spec_ref.shape[0]
     for f in range(frames):
-        rows = [pos_ref[f, c : c + 1, :] for c in range(3)]
+        rows = [pos_ref[c, f : f + 1, :] for c in range(3)]
         rows.append(spec_ref[f : f + 1, :].astype(f32))
         for side, out in ((0, down_ref), (1, up_ref)):
             index = halo_ref[f, side : side + 1, :]
@@ -96,21 +111,87 @@
                 out[4 * f + c : 4 * f + c + 1, :] = jnp.where(high, high_g, low_g)[0:1]
 
 
-def structure_kernel(slab_ref, count_ref, pos_ref, spec_ref, qt_ref, out_ref):
-    frames, _, atoms = pos_ref.shape
+def stage_kernel(
+    slab_ref,
+    pos_ref,
+    spec_ref,
+    nb_hbm,
+    count_hbm,
+    q_hbm,
+    emb_hbm,
+    wmsg_hbm,
+    wr1_hbm,
+    wr2_hbm,
+    wup_hbm,
+    wout_hbm,
+    nb_ref,
+    w1_ref,
+    w2_ref,
+    wup_ref,
+    wmsg_ref,
+    kind_ref,
+    wout_ref,
+    struct_ref,
+    live_ref,
+    count_in,
+    q_in,
+    emb_in,
+    wmsg_in,
+    wr1_in,
+    wr2_in,
+    wup_in,
+    wout_in,
+    sems,
+):
+    pairs = (
+        (count_hbm, count_in),
+        (q_hbm, q_in),
+        (wr1_hbm, wr1_in),
+        (wr2_hbm, wr2_in),
+        (wup_hbm, wup_in),
+        (wmsg_hbm, wmsg_in),
+        (emb_hbm, emb_in),
+        (wout_hbm, wout_in),
+        (nb_hbm, nb_ref),
+    )
+    copies = fetch_all(sems, pairs)
+    for copy in copies[:-1]:
+        copy.wait()
+    _, frames, atoms = pos_ref.shape
+    number_q = q_in.shape[1]
+    same = lax.broadcasted_iota(jnp.int32, (number_q, number_q), 0) == lax.broadcasted_iota(
+        jnp.int32, (number_q, number_q), 1
+    )
+    q = [
+        jnp.sum(jnp.where(same, spread(q_in[c : c + 1, :], number_q), 0.0), axis=1, keepdims=True)
+        for c in range(3)
+    ]
     lift = slab_ref[0].astype(f32) * slab_depth
     number = lax.broadcasted_iota(jnp.int32, (1, atoms), 1)
+    struct_ref[...] = jnp.zeros_like(struct_ref)
     for f in range(frames):
-        x, y, z = (pos_ref[f, c : c + 1, :] for c in range(3))
-        phases = qt_ref[:, 0:1] * x + qt_ref[:, 1:2] * y + qt_ref[:, 2:3] * (z + lift)
+        x, y, z = (pos_ref[c, f : f + 1, :] for c in range(3))
+        phases = q[0] * x + q[1] * y + q[2] * (z + lift)
         lengths = jnp.where(spec_ref[f : f + 1, :] == 1, 1.0, hydrogen_length)
-        lengths = jnp.where(number < count_ref[f, 0], lengths, 0.0)
+        living = (number < count_in[:, f : f + 1]).astype(f32)
+        live_ref[f : f + 1, :] = living
+        lengths = living * lengths
         cos_part = jnp.sum(lengths * jnp.cos(phases), axis=1, keepdims=True)
         sin_part = jnp.sum(lengths * jnp.sin(phases), axis=1, keepdims=True)
-        out_ref[2 + f : 3 + f, :] = as_row(cos_part)
-        out_ref[4 + f : 5 + f, :] = as_row(sin_part)
-    out_ref[0:2, :] = jnp.zeros((2, LANES), f32)
-    out_ref[6:8, :] = jnp.zeros((2, LANES), f32)
+        struct_ref[2 + f : 3 + f, :] = as_row(cos_part)
+        struct_ref[4 + f : 5 + f, :] = as_row(sin_part)
+    for layer in range(2):
+        w1_ref[layer] = rad1_blocks(wr1_in[layer])
+        w2_ref[layer] = transposed(wr2_in[layer])
+        wup_ref[layer] = transposed(wup_in[layer])
+    wmsg_ref[...] = transposed(wmsg_in[1])
+    emb = emb_in[...]
+    table = mm(emb, wmsg_in[0]).astype(bf16).astype(f32)
+    for k in range(2):
+        kind_ref[k] = column(emb[k : k + 1].astype(f32))
+        kind_ref[2 + k] = column(table[k : k + 1])
+    wout_ref[...] = column(wout_in[...])
+    copies[-1].wait()
 
 
 def basis_rows(dist_ref, f, i, first, atoms):
@@ -129,11 +210,11 @@
     above_ref,
     nb_ref,
     halo_ref,
-    emb_ref,
+    w1_ref,
+    w2_ref,
+    wup_ref,
     wmsg_ref,
-    wr1_ref,
-    wr2_ref,
-    wup_ref,
+    kind_ref,
     geo_ref,
     feat_ref,
     msg_ref,
@@ -141,22 +222,13 @@
     up_ref,
     wgt_ref,
     acc_ref,
-    w1_ref,
 ):
-    frames, _, atoms = pos_ref.shape
+    _, frames, atoms = pos_ref.shape
     batches = nb_ref.shape[1]
     slots = batches * 8
-    hidden = wr1_ref.shape[2]
-    w1_ref[...] = rad1_blocks(wr1_ref[0])
-    w2 = transposed(wr2_ref[0])
-    w2s = jnp.concatenate([w2[:LANES]] * 2, axis=1)
-    w2v = jnp.concatenate([w2[LANES:]] * 2, axis=1)
-    wup = transposed(wup_ref[0])
-    wmsg = transposed(wmsg_ref[1])
-    emb = emb_ref[...]
-    table = mm(emb, wmsg_ref[0]).astype(bf16).astype(f32)
-    emb_cols = [column(emb[s : s + 1].astype(f32)) for s in range(2)]
-    msg_cols = [column(table[s : s + 1]) for s in range(2)]
+    hidden = w2_ref.shape[2]
+    w2s = jnp.concatenate([w2_ref[0, :LANES, :]] * 2, axis=1)
+    w2v = jnp.concatenate([w2_ref[0, LANES:, :]] * 2, axis=1)
     scale = slots**-0.5
     for f in range(frames):
         for half in range(atoms // LANES):
@@ -179,7 +251,7 @@
                 squares = None
                 offsets = []
                 for c in range(3):
-                    own_row = pos_ref[f, c : c + 1, :]
+                    own_row = pos_ref[c, f : f + 1, :]
                     parts = fetch(own_row, 4 * f + c)
                     if c == 2:
                         parts[2] = parts[2] - slab_depth
@@ -212,7 +284,7 @@
         def step(i, carry):
             acts = []
             for first in range(0, 8, GROUP):
-                pre = mm(w1_ref[...], basis_rows(geo_ref, f, i, first, atoms))
+                pre = mm(w1_ref[0], basis_rows(geo_ref, f, i, first, atoms))
                 acts.append(silu(pre).astype(bf16).astype(f32))
             for half in range(atoms // LANES):
                 cols = slice(half * LANES, (half + 1) * LANES)
@@ -228,7 +300,7 @@
                         acc_ref[k, part : part + 32, cols] = total
             return carry
 
-        lax.fori_loop(0, batches, step, 0)
+        lax.fori_loop(0, batches, step, 0, unroll=UN1)
 
         def project(k, w):
             total = acc_ref[k]
@@ -236,8 +308,8 @@
             low = (total - high.astype(f32)).astype(bf16)
             return mm(w, jnp.concatenate([high, low], axis=0))
 
-        cols0 = jnp.concatenate([msg_cols[0]] * 2, axis=1)
-        cols1 = jnp.concatenate([msg_cols[1]] * 2, axis=1)
+        cols0 = jnp.concatenate([kind_ref[2]] * 2, axis=1)
+        cols1 = jnp.concatenate([kind_ref[3]] * 2, axis=1)
         scalar = scale * (cols0 * project(0, w2s) + cols1 * project(1, w2s))
         squared = None
         for c in range(3):
@@ -246,12 +318,12 @@
             )
             squared = vec * vec if squared is None else squared + vec * vec
         mixed = jnp.concatenate([scalar, squared], axis=0).astype(bf16)
-        update = mm(wup, mixed)
-        e0 = jnp.concatenate([emb_cols[0]] * 2, axis=1)
-        e1 = jnp.concatenate([emb_cols[1]] * 2, axis=1)
+        update = mm(wup_ref[0], mixed)
+        e0 = jnp.concatenate([kind_ref[0]] * 2, axis=1)
+        e1 = jnp.concatenate([kind_ref[1]] * 2, axis=1)
         features = jnp.where(spec_ref[f : f + 1, :] == 1, e1, e0) + silu(update)
         feat_ref[f] = features
-        message = mm(wmsg, features.astype(bf16)).astype(bf16)
+        message = mm(wmsg_ref[...], features.astype(bf16)).astype(bf16)
         msg_ref[f] = message
         message = message.astype(f32)
         for side, out in ((0, down_ref), (1, up_ref)):
@@ -262,15 +334,14 @@
             out[f] = jnp.where(index >= LANES, high_g, low_g).astype(bf16)
 
 
-def hidden_kernel(geo_ref, nb_ref, wr1_ref, out_ref, w1_ref):
+def hidden_kernel(geo_ref, nb_ref, w1_ref, w2_ref, out_ref):
     frames, batches, _, atoms = nb_ref.shape
-    hidden = wr1_ref.shape[2]
-    w1_ref[...] = rad1_blocks(wr1_ref[1])
+    hidden = w2_ref.shape[2]
     for f in range(frames):
 
         def step(i, carry):
             for first in range(0, 8, GROUP):
-                act = silu(mm(w1_ref[...], basis_rows(geo_ref, f, i, first, atoms)))
+                act = silu(mm(w1_ref[1], basis_rows(geo_ref, f, i, first, atoms)))
                 for j in range(GROUP):
                     here = nb_ref[f, i, first + j : first + j + 1, :] >= 0
                     rows = slice(j * hidden, (j + 1) * hidden)
@@ -278,12 +349,12 @@
                     out_ref[f, i, (first + j) * hidden : (first + j + 1) * hidden, :] = kept
             return carry
 
-        lax.fori_loop(0, batches, step, 0)
+        lax.fori_loop(0, batches, step, 0, unroll=UNH)
 
 
 def second_kernel(
     rows_each,
-    count_ref,
+    live_ref,
     spec_ref,
     eshift_ref,
     nb_ref,
@@ -293,7 +364,7 @@
     msg_ref,
     below_ref,
     above_ref,
-    wr2_ref,
+    w2_ref,
     wup_ref,
     wout_ref,
     struct_ref,
@@ -301,46 +372,61 @@
     chunk_ref,
     acc_ref,
     src_ref,
-    w2_ref,
+    pair_ref,
 ):
     frames, batches, _, atoms = nb_ref.shape
     slots = batches * 8
-    hidden = wr2_ref.shape[1]
+    hidden = w2_ref.shape[2]
     chunks = chunk_ref.shape[0]
-    w2_ref[...] = transposed(wr2_ref[1])
-    wup = transposed(wup_ref[1])
-    wout = jnp.concatenate([column(wout_ref[...])] * 2, axis=1)
+    wout = jnp.concatenate([wout_ref[...]] * 2, axis=1)
     scale = slots**-0.5
-    number = lax.broadcasted_iota(jnp.int32, (1, atoms), 1)
     extra = [None] * EXTRA
     for f in range(frames):
-        src_ref[0] = msg_ref[f, :, :LANES].astype(f32)
-        src_ref[1] = msg_ref[f, :, LANES:].astype(f32)
-        src_ref[2] = below_ref[f].astype(f32)
-        src_ref[3] = above_ref[f].astype(f32)
+        src_ref[0] = msg_ref[f, :, :LANES]
+        src_ref[1] = msg_ref[f, :, LANES:]
+        src_ref[2] = below_ref[f]
+        src_ref[3] = above_ref[f]
+        halo = jnp.concatenate([below_ref[f, XLU:, :], above_ref[f, XLU:, :]], axis=1)
+        pair_ref[...] = jnp.concatenate([msg_ref[f, XLU:, :], halo], axis=0)
         acc_ref[...] = jnp.zeros_like(acc_ref)
 
         def step(i, carry):
             filters = [
-                mm(w2_ref[...], hid_ref[f, i, j * hidden : (j + 1) * hidden, :]) for j in range(8)
+                mm(w2_ref[1], hid_ref[f, i, j * hidden : (j + 1) * hidden, :]) for j in range(8)
             ]
-            width = 32
+            width = WIDTH
+            if XLU < LANES:
+                target = lax.broadcasted_iota(jnp.int32, (2 * LANES, atoms), 0).astype(bf16)
+                found = []
+                for j in range(8):
+                    want = (nb_ref[f, i, j : j + 1, :] & (2 * LANES - 1)).astype(f32).astype(bf16)
+                    hot = jnp.where(target == want, jnp.asarray(1, bf16), jnp.asarray(0, bf16))
+                    found.append(mm(pair_ref[...], hot))
             for half in range(atoms // LANES):
                 cols = slice(half * LANES, (half + 1) * LANES)
                 index = [nb_ref[f, i, j : j + 1, cols] for j in range(8)]
-                lane = [spread(v & (LANES - 1), width) for v in index]
+                lane = [spread(v & (LANES - 1), width).astype(jnp.int16) for v in index]
                 block = [spread(v >> 7, width) for v in index]
+                block16 = [v.astype(jnp.int16) for v in block]
                 offset = [[geo_ref[f, c, i, j : j + 1, cols] for c in range(3)] for j in range(8)]
                 for part in range(0, LANES, width):
                     rows = slice(part, part + width)
                     total = [acc_ref[k, rows, cols] for k in range(4)]
                     for j in range(8):
-                        got = [lane_gather(src_ref[b, rows, :], lane[j]) for b in range(4)]
-                        there = jnp.where(
-                            block[j] < 2,
-                            jnp.where(block[j] == 1, got[1], got[0]),
-                            jnp.where(block[j] == 2, got[2], got[3]),
-                        )
+                        if part < XLU:
+                            got = [lane_gather(src_ref[b, rows, :], lane[j]) for b in range(4)]
+                            there = jnp.where(
+                                block16[j] < 2,
+                                jnp.where(block16[j] == 1, got[1], got[0]),
+                                jnp.where(block16[j] == 2, got[2], got[3]),
+                            ).astype(f32)
+                        else:
+                            at = part - XLU
+                            there = jnp.where(
+                                block[j] < 2,
+                                found[j][at : at + width, cols],
+                                found[j][LANES - XLU + at : LANES - XLU + at + width, cols],
+                            )
                         total[0] = total[0] + filters[j][rows, cols] * there
                         vec = filters[j][LANES + part : LANES + part + width, cols] * there
                         for c in range(3):
@@ -349,7 +435,7 @@
                         acc_ref[k, rows, cols] = total[k]
             return carry
 
-        lax.fori_loop(0, batches, step, 0)
+        lax.fori_loop(0, batches, step, 0, unroll=UN2)
 
         scalar = scale * acc_ref[0]
         squared = None
@@ -357,10 +443,10 @@
             vec = (scale * vector_scale) * acc_ref[c + 1]
             squared = vec * vec if squared is None else squared + vec * vec
         mixed = jnp.concatenate([scalar, squared], axis=0).astype(bf16)
-        update = mm(wup, mixed)
+        update = mm(wup_ref[1], mixed)
         gate = sigmoid(update)
         features = feat_ref[f] + update * gate
-        living = (number < count_ref[f, 0]).astype(f32)
+        living = live_ref[f : f + 1, :]
         slope = (living * wout * (gate * (1.0 + update * (1.0 - gate)))).astype(bf16)
         kind = spec_ref[f : f + 1, :]
         readout = jnp.sum(features * wout, axis=0, keepdims=True)
@@ -422,6 +508,7 @@
 
 VM = pl.BlockSpec(memory_space=pltpu.VMEM)
 SM = pl.BlockSpec(memory_space=pltpu.SMEM)
+HB = pl.BlockSpec(memory_space=pltpu.HBM)
 
 
 def call(kernel, name, ins, outs, scratch, *operands):
@@ -434,6 +521,10 @@
         scratch_shapes=scratch,
         compiler_params=pltpu.CompilerParams(vmem_limit_bytes=VMEM_BYTES),
     )(*operands)
+
+
+def in_hbm(value):
+    return pltpu.with_memory_space_constraint(value, pltpu.HBM)
 
 
 def array(shape, dtype=f32):
@@ -464,6 +555,7 @@
     hidden = w_rad1.shape[2]
     channels = w_msg.shape[1]
     neighbours = neighbours.reshape(frames, slots // 8, 8, atoms)
+    positions = positions.transpose(1, 0, 2)
     slab_devs = lax.axis_size("slab")
     frame_devs = lax.axis_size("frame")
     rows_each = 2 * channels // slab_devs
@@ -471,24 +563,55 @@
     up = [(i, (i + 1) % slab_devs) for i in range(slab_devs)]
     down = [(j, i) for i, j in up]
 
+    basis = w_rad1.shape[1]
     rows = array((4 * frames, halo))
-    leave_down, leave_up = call(
-        pack_kernel, "halo_rows", [VM] * 3, (rows, rows), [], positions, species, halo_index
+    leave_down, leave_up, positions, species, halo_index = call(
+        pack_kernel,
+        "halo_rows",
+        [HB] * 3,
+        (
+            rows,
+            rows,
+            array(positions.shape),
+            array(species.shape, jnp.int32),
+            array(halo_index.shape, jnp.int32),
+        ),
+        [pltpu.SemaphoreType.DMA((3,))],
+        *map(in_hbm, (positions, species, halo_index)),
     )
     below = lax.ppermute(leave_up, "slab", up)
     above = lax.ppermute(leave_down, "slab", down)
-    slab_pos = lax.axis_index("slab").reshape(1)
-    structure = call(
-        structure_kernel,
-        "structure_sums",
-        [SM, SM, VM, VM, VM],
-        array((EXTRA, LANES)),
-        [],
-        slab_pos,
-        atom_count,
+    small = (
+        atom_count.reshape(1, frames),
+        q_vectors,
+        embedding,
+        w_msg,
+        w_rad1,
+        w_rad2,
+        w_up,
+        w_out.reshape(1, channels),
+    )
+    neighbours, w1, w2, wup, wmsg, kinds, wout, structure, living = call(
+        stage_kernel,
+        "staged_inputs",
+        [SM, VM, VM] + [HB] * 9,
+        (
+            array(neighbours.shape, jnp.int32),
+            array((2, GROUP * hidden, GROUP * basis), bf16),
+            array((2, 2 * channels, hidden), bf16),
+            array((2, channels, 2 * channels), bf16),
+            array((channels, channels), bf16),
+            array((4, channels, LANES)),
+            array((channels, LANES)),
+            array((EXTRA, LANES)),
+            array((frames, atoms)),
+        ),
+        [pltpu.VMEM(w.shape, w.dtype) for w in small] + [pltpu.SemaphoreType.DMA((9,))],
+        lax.axis_index("slab").reshape(1),
         positions,
         species,
-        q_vectors.T,
+        in_hbm(neighbours),
+        *map(in_hbm, small),
     )
     halo_rows = array((frames, channels, halo), bf16)
     geometry, features, message, msg_down, msg_up = call(
@@ -502,46 +625,43 @@
             halo_rows,
             halo_rows,
         ),
-        [
-            pltpu.VMEM((8, slots // 8, 8, atoms), f32),
-            pltpu.VMEM((8, hidden, atoms), f32),
-            pltpu.VMEM((GROUP * hidden, GROUP * w_rad1.shape[1]), bf16),
-        ],
+        [pltpu.VMEM((8, slots // 8, 8, atoms), f32), pltpu.VMEM((8, hidden, atoms), f32)],
         positions,
         species,
         below,
         above,
         neighbours,
         halo_index,
-        embedding,
-        w_msg,
-        w_rad1,
-        w_rad2,
-        w_up,
+        w1,
+        w2,
+        wup,
+        wmsg,
+        kinds,
     )
     msg_below = lax.ppermute(msg_up, "slab", up)
     msg_above = lax.ppermute(msg_down, "slab", down)
     radial_hidden = call(
         hidden_kernel,
         "radial_hidden",
-        [VM] * 3,
+        [VM] * 4,
         array((frames, slots // 8, 8 * hidden, atoms), bf16),
-        [pltpu.VMEM((GROUP * hidden, GROUP * w_rad1.shape[1]), bf16)],
+        [],
         geometry,
         neighbours,
-        w_rad1,
+        w1,
+        w2,
     )
     atom_energy, chunks = call(
         functools.partial(second_kernel, rows_each),
         "second_layer",
-        [SM, VM, SM] + [VM] * 11,
+        [VM, VM, SM] + [VM] * 11,
         (array((frames, atoms)), array((slab_devs, chunk_rows, LANES))),
         [
             pltpu.VMEM((4, channels, atoms), f32),
-            pltpu.VMEM((4, channels, LANES), f32),
-            pltpu.VMEM((2 * channels, hidden), bf16),
+            pltpu.VMEM((4, channels, LANES), bf16),
+            pltpu.VMEM((2 * (LANES - XLU), 2 * LANES), bf16),
         ],
-        atom_count,
+        living,
         species,
         e_shift,
         neighbours,
@@ -551,9 +671,9 @@
         message,
         msg_below,
         msg_above,
-        w_rad2,
-        w_up,
-        w_out.reshape(1, channels),
+        w2,
+        wup,
+        wout,
         structure,
     )
     chunks = lax.all_to_all(chunks, "slab", 0, 0, tiled=True)

time: 106 us -> 84.9 us (0.80)
  local copies, waits for them, and re-layouts: 11.4 us -> 0.67 us
  Pallas kernels: 34 us -> 23.6 us
  starting transfers between devices: 19.3 us -> 21 us
    unnamed x42 -> x7, local copies, waits for them, and re-layouts: 11.4 us -> 0.67 us
    pallas_call x7, Pallas kernels: 34 us -> 23.6 us  [call(): pl.pallas_call(kernel, name=name, out_shape=outs, in_specs=ins, out_specs...]
    all_to_all x1, starting transfers between devices: 5.51 us -> 7.34 us  [per_device(): chunks = lax.all_to_all(chunks, 'slab', 0, 0, tiled=True)]
  transfers between devices with their start and end apart: 5 -> 5, of which waited for: 2 -> 1; matrix products, arithmetic and copies ran while one was open for 1% -> 0% of each run, Pallas kernels for 4% -> 5%
where the time goes in v2:
time: 84.9 us; the launch traced here: 84.6 us
  blocking collectives  27.2 us (32%)
  Pallas kernels  23.6 us (28%)
  starting transfers between devices  21 us (25%)
  waiting for transfers between devices  10.8 us (13%)
  between operations  1.4 us (2%)
    pallas_call x7, Pallas kernels, call(): pl.pallas_call(kernel, name=name, out_shape=outs, in_specs=ins, out_specs...  23.6 us
    all_to_all x1, blocking collectives, per_device(): totals = lax.all_to_all(totals, 'frame', 0, 0, tiled=True)  14.5 us
    all_to_all x1, blocking collectives, per_device(): grad_up = lax.all_to_all(grad_rows, 'slab', 0, 0, tiled=True)  12.7 us
    all_to_all x1, waiting for transfers between devices, per_device(): chunks = lax.all_to_all(chunks, 'slab', 0, 0, tiled=True)  10.8 us
    all_to_all x1, starting transfers between devices, per_device(): chunks = lax.all_to_all(chunks, 'slab', 0, 0, tiled=True)  7.34 us
    ppermute x1, starting transfers between devices, per_device(): above = lax.ppermute(leave_down, 'slab', down)  6.65 us
    ppermute x1, starting transfers between devices, per_device(): msg_above = lax.ppermute(msg_down, 'slab', down)  4.77 us
    ppermute x1, starting transfers between devices, per_device(): below = lax.ppermute(leave_up, 'slab', up)  2.12 us
  transfers between devices with their start and end apart: 5, of which 1 were waited for; matrix products, arithmetic and copies ran while one was open for 0% of the time, Pallas kernels for 5%

profile of v2, /device:TPU:1, one launch (start us, length us, event | category | flops | bytes accessed | tf_op | source)
XLA Modules:
  0.0 84.6 jit_solution(14792800092980281092)
XLA Ops:
  0.6 0.0 copy-start
  0.6 0.9 %halo_rows.1 = (f32[8,128]{1,0:T(8,128)S(1)}, f32[8,128]{1,0:T(8,128)S(1)}, f32[3,2,256]{2,1,0:T(2,128)S(1)}, s32[2,256]{1,0:T(2,128)S(1)}, s32[2,2,128]{2,1,0:T(2,128)S(1)}) custom-call(f32[3,2,256]{2,1,0:T(2,128)} %bitcast.12, s32[2,256]{1,0:T(2,128)} %spec_hbm.1, s32[2,2,128]{2,1,0:T(2,128)} %halo_hbm.1), custom_call_target="tpu_custom_call" | custom-call | tf_op jit(solution)/shard_map/halo_rows/pallas_call | solution.py:515
  1.5 2.1 %collective-permute-start = (f32[8,128]{1,0:T(8,128)S(1)}, f32[8,128]{1,0:T(8,128)S(1)}, u32[]{:S(2)}, u32[]{:S(2)}) collective-permute-start(f32[8,128]{1,0:T(8,128)S(1)} %get-tuple-element.32), channel_id=1, source_target_pairs={{0,1},{1,2},{2,3},{3,4},{4,5},{5,6},{6,7},{7,8},{8,9},{9,10},{10,1... | collective-permute-start | bytes 12296 | tf_op jit(solution)/shard_map/ppermute | solution.py:582
  3.6 6.6 %collective-permute-start.1 = (f32[8,128]{1,0:T(8,128)S(1)}, f32[8,128]{1,0:T(8,128)S(1)}, u32[]{:S(2)}, u32[]{:S(2)}) collective-permute-start(f32[8,128]{1,0:T(8,128)S(1)} %get-tuple-element.33), channel_id=1, source_target_pairs={{1,0},{2,1},{3,2},{4,3},{5,4},{6,5},{7,6},{8,7},{9,8},{10,9},{11,1... | collective-permute-start | bytes 12296 | tf_op jit(solution)/shard_map/ppermute | solution.py:583
  10.3 1.7 %staged_inputs.1 = (s32[2,6,8,256]{3,2,1,0:T(8,128)S(1)}, bf16[2,256,32]{2,1,0:T(8,128)(2,1)S(1)}, bf16[2,256,64]{2,1,0:T(8,128)(2,1)S(1)}, bf16[2,128,256]{2,1,...) custom-call(s32[1]{0:T(128)} %bitcast.slab_ref, ...), custom_call_target="tpu_custom_call" | custom-call | tf_op jit(solution)/shard_map/staged_inputs/pallas_call | solution.py:515
  12.0 0.0 collective-permute-done.below_ref
  12.0 0.0 collective-permute-done.1.above_ref
  12.0 7.2 %first_layer.1 = (f32[2,4,6,8,256]{4,3,2,1,0:T(8,128)S(1)}, f32[2,128,256]{2,1,0:T(8,128)S(1)}, bf16[2,128,256]{2,1,0:T(8,128)(2,1)S(1)}, bf16[2,128,128]{2,1,0:T(8,128)(2,1)S(1)}, bf16[2,128,128]{2,1,0:T(8,128)(2,1)S(1)}) custom-call(f32[3,2,256]{2,1,0:T(2,128)S(1)} %get-tuple-element.28.pos_ref, s32[2,256]{1,0:T(2,128)S(1)} %get-tuple-element.29.spec_ref, ...), custom_call_target="tpu_custom_call" | custom-call | tf_op jit(solution)/shard_map/first_layer/pallas_call | solution.py:515
  19.2 0.1 collective-permute-start.2
  19.3 4.8 %collective-permute-start.3 = (bf16[2,128,128]{2,1,0:T(8,128)(2,1)S(1)}, bf16[2,128,128]{2,1,0:T(8,128)(2,1)S(1)}, u32[]{:S(2)}, u32[]{:S(2)}) collective-permute-start(bf16[2,128,128]{2,1,0:T(8,128)(2,1)S(1)} %get-tuple-element.44), channel_id=1, source_target_pairs={{1,0},{2,1},{3,2},{4,3},{5,4},{6,5},{7,6},{8,7},{9,8},{10,9},{11,1... | collective-permute-start | bytes 196616 | tf_op jit(solution)/shard_map/ppermute | solution.py:642
  24.1 2.2 %radial_hidden.1.hid_ref = bf16[2,6,512,256]{3,2,1,0:T(8,128)(2,1)S(1)} custom-call(f32[2,4,6,8,256]{4,3,2,1,0:T(8,128)S(1)} %get-tuple-element.40.geo_ref, s32[2,6,8,256]{3,2,1,0:T(8,128)S(1)} %get-tuple-element.31.nb_ref, bf16[2,256,32]{2,1,0:T(8,128)(2,1)S(1)} %get-tuple-element.35.w1_ref, bf16[2,256,64]{2,1,0:T(8,128)(2,1)S(1)} %get-tuple-element.36.w2_ref), custom_call_target="tpu_custom_call" | custom-call | tf_op jit(solution)/shard_map/radial_hidden/pallas_call | solution.py:515
  26.3 0.0 copy-start.2
  26.3 0.0 copy-start.1
  26.3 0.0 collective-permute-done.2.below_ref
  26.3 0.0 collective-permute-done.3.above_ref
  26.3 0.0 copy-done
  26.3 10.4 %second_layer.1 = (f32[2,256]{1,0:T(2,128)}, f32[32,24,128]{2,1,0:T(8,128)}) custom-call(f32[2,256]{1,0:T(2,128)S(1)} %get-tuple-element.30.live_ref, s32[2,256]{1,0:T(2,128)S(1)} %get-tuple-element.29.spec_ref, f32[2]{0:T(128)S(1)} %copy-done, s32[2,6,8,256]{3,2,1,0:T(8,128)S(1)} %get-tuple-element.31.nb_ref, ...), custom_call_target="tpu_custom_call" | custom-call | tf_op jit(solution)/shard_map/second_layer/pallas_call | solution.py:515
  36.7 7.3 %all-to-all-start = ((f32[32,24,128]{2,1,0:T(8,128)}), f32[32,24,128]{2,1,0:T(8,128)S(1)}, u32[]{:S(2)}, u32[]{:S(2)}) async-start(f32[32,24,128]{2,1,0:T(8,128)} %get-tuple-element.48), calls=%async_computation | async-start | bytes 786432 | tf_op jit(solution)/shard_map/all_to_all | solution.py:679
  44.7 10.8 %all-to-all-done.in_ref = f32[32,24,128]{2,1,0:T(8,128)S(1)} async-done(((f32[32,24,128]{2,1,0:T(8,128)}), f32[32,24,128]{2,1,0:T(8,128)S(1)}, u32[]{:S(2)}, u32[]{:S(2)}) %all-to-all-start) | async-done | bytes 393248 | tf_op jit(solution)/shard_map/all_to_all | solution.py:679
  55.5 0.0 copy-done.2
  55.5 0.6 slab_totals.1
  56.1 14.5 %all_to_all.15.in_ref = f32[8,24,128]{2,1,0:T(8,128)S(1)} all-to-all(f32[8,24,128]{2,1,0:T(8,128)S(1)} %slab_totals.1), channel_id=1, replica_groups=mesh['frame'=8,'slab'=32] {'frame'}, dimensions={0} | all-to-all | bytes 196608 | tf_op jit(solution)/shard_map/all_to_all | solution.py:690
  70.6 0.0 copy-done.1
  70.6 0.6 reweighted.1
  71.3 12.7 %all_to_all.16 = f32[32,8,128]{2,1,0:T(8,128)S(1)} all-to-all(f32[32,8,128]{2,1,0:T(8,128)S(1)} %get-tuple-element.50), channel_id=1, replica_groups=mesh['frame'=8,'slab'=32] {'slab'}, dimensions={0} | all-to-all | bytes 262144 | tf_op jit(solution)/shard_map/all_to_all | solution.py:702
  84.0 0.7 copy.22
Async XLA Ops:
  0.6 25.7 %copy-start = (f32[2]{0:T(128)S(1)}, f32[2]{0:T(128)}, u32[]{:S(2)}) copy-start(f32[2]{0:T(128)} %eshift_ref.1) | copy-start | bytes 28
  1.5 10.5 %collective-permute-start = (f32[8,128]{1,0:T(8,128)S(1)}, f32[8,128]{1,0:T(8,128)S(1)}, u32[]{:S(2)}, u32[]{:S(2)}) collective-permute-start(f32[8,128]{1,0:T(8,128)S(1)} %get-tuple-element.32), channel_id=1, source_target_pairs={{0,1},{1,2},{2,3},{3,4},{4,5},{5,6},{6,7},{7,8},{8,9},{9,10},{10,1... | collective-permute-start | bytes 12296 | tf_op jit(solution)/shard_map/ppermute | solution.py:582
  3.6 8.4 %collective-permute-start.1 = (f32[8,128]{1,0:T(8,128)S(1)}, f32[8,128]{1,0:T(8,128)S(1)}, u32[]{:S(2)}, u32[]{:S(2)}) collective-permute-start(f32[8,128]{1,0:T(8,128)S(1)} %get-tuple-element.33), channel_id=1, source_target_pairs={{1,0},{2,1},{3,2},{4,3},{5,4},{6,5},{7,6},{8,7},{9,8},{10,9},{11,1... | collective-permute-start | bytes 12296 | tf_op jit(solution)/shard_map/ppermute | solution.py:583
  19.2 7.1 %collective-permute-start.2 = (bf16[2,128,128]{2,1,0:T(8,128)(2,1)S(1)}, bf16[2,128,128]{2,1,0:T(8,128)(2,1)S(1)}, u32[]{:S(2)}, u32[]{:S(2)}) collective-permute-start(bf16[2,128,128]{2,1,0:T(8,128)(2,1)S(1)} %get-tuple-element.43), channel_id=1, source_target_pairs={{0,1},{1,2},{2,3},{3,4},{4,5},{5,6},{6,7},{7,8},{8,9},{9,10},{10,1... | collective-permute-start | bytes 196616 | tf_op jit(solution)/shard_map/ppermute | solution.py:641
  19.3 7.0 %collective-permute-start.3 = (bf16[2,128,128]{2,1,0:T(8,128)(2,1)S(1)}, bf16[2,128,128]{2,1,0:T(8,128)(2,1)S(1)}, u32[]{:S(2)}, u32[]{:S(2)}) collective-permute-start(bf16[2,128,128]{2,1,0:T(8,128)(2,1)S(1)} %get-tuple-element.44), channel_id=1, source_target_pairs={{1,0},{2,1},{3,2},{4,3},{5,4},{6,5},{7,6},{8,7},{9,8},{10,9},{11,1... | collective-permute-start | bytes 196616 | tf_op jit(solution)/shard_map/ppermute | solution.py:642
  26.3 29.3 %copy-start.2 = (f32[2]{0:T(128)S(1)}, f32[2]{0:T(128)}, u32[]{:S(2)}) copy-start(f32[2]{0:T(128)} %uref_ref.1) | copy-start | bytes 28
  26.3 44.4 %copy-start.1 = (f32[16]{0:T(128)S(1)}, f32[16]{0:T(128)}, u32[]{:S(2)}) copy-start(f32[16]{0:T(128)} %param.31) | copy-start | bytes 196
  36.7 18.8 %all-to-all-start = ((f32[32,24,128]{2,1,0:T(8,128)}), f32[32,24,128]{2,1,0:T(8,128)S(1)}, u32[]{:S(2)}, u32[]{:S(2)}) async-start(f32[32,24,128]{2,1,0:T(8,128)} %get-tuple-element.48), calls=%async_computation | async-start | bytes 786432 | tf_op jit(solution)/shard_map/all_to_all | solution.py:679

commit v3 on v2

--- a/solution.py
+++ b/solution.py
@@ -113,9 +113,13 @@
 
 def stage_kernel(
     slab_ref,
+    beta_ref,
     pos_ref,
     spec_ref,
     nb_hbm,
+    target_hbm,
+    uref_hbm,
+    eshift_hbm,
     count_hbm,
     q_hbm,
     emb_hbm,
@@ -133,6 +137,10 @@
     wout_ref,
     struct_ref,
     live_ref,
+    scalar_ref,
+    target_ref,
+    uref_in,
+    eshift_in,
     count_in,
     q_in,
     emb_in,
@@ -145,6 +153,9 @@
 ):
     pairs = (
         (count_hbm, count_in),
+        (uref_hbm, uref_in),
+        (eshift_hbm, eshift_in),
+        (target_hbm, target_ref),
         (q_hbm, q_in),
         (wr1_hbm, wr1_in),
         (wr2_hbm, wr2_in),
@@ -191,6 +202,11 @@
         kind_ref[k] = column(emb[k : k + 1].astype(f32))
         kind_ref[2 + k] = column(table[k : k + 1])
     wout_ref[...] = column(wout_in[...])
+    for k in range(2):
+        scalar_ref[k : k + 1, :] = jnp.broadcast_to(uref_in[:, k : k + 1], (1, LANES))
+        scalar_ref[2 + k : 3 + k, :] = jnp.full((1, LANES), beta_ref[0], f32)
+        scalar_ref[4 + k : 5 + k, :] = jnp.broadcast_to(eshift_in[:, k : k + 1], (1, LANES))
+    scalar_ref[6:8, :] = jnp.zeros((2, LANES), f32)
     copies[-1].wait()
 
 
@@ -356,7 +372,7 @@
     rows_each,
     live_ref,
     spec_ref,
-    eshift_ref,
+    scalar_ref,
     nb_ref,
     geo_ref,
     hid_ref,
@@ -379,6 +395,7 @@
     hidden = w2_ref.shape[2]
     chunks = chunk_ref.shape[0]
     wout = jnp.concatenate([wout_ref[...]] * 2, axis=1)
+    shift = [jnp.concatenate([scalar_ref[4 + k : 5 + k, :]] * 2, axis=1) for k in range(2)]
     scale = slots**-0.5
     extra = [None] * EXTRA
     for f in range(frames):
@@ -450,7 +467,7 @@
         slope = (living * wout * (gate * (1.0 + update * (1.0 - gate)))).astype(bf16)
         kind = spec_ref[f : f + 1, :]
         readout = jnp.sum(features * wout, axis=0, keepdims=True)
-        energy = living * (readout + jnp.where(kind == 1, eshift_ref[1], eshift_ref[0]))
+        energy = living * (readout + jnp.where(kind == 1, shift[1], shift[0]))
         energy_ref[f : f + 1, :] = energy
         grad = lax.dot_general(mixed, slope, (((1,), (1,)), ((), ())), preferred_element_type=f32)
         chunk_ref[:, f * rows_each : (f + 1) * rows_each, :] = grad.reshape(
@@ -464,7 +481,7 @@
     chunk_ref[:, frames * rows_each :, :] = jnp.broadcast_to(block[None], (chunks, EXTRA, LANES))
 
 
-def total_kernel(uref_ref, beta_ref, in_ref, out_ref):
+def total_kernel(scalar_ref, in_ref, out_ref):
     rows = in_ref.shape[1]
     total = in_ref[0]
     for s in range(1, in_ref.shape[0]):
@@ -473,12 +490,14 @@
         out_ref[d] = total
     for f in range(2):
         row = total[rows - 2 + f : rows - 1 + f]
-        log_weight = -beta_ref[0] * (row - uref_ref[f])
+        log_weight = -scalar_ref[2 + f : 3 + f, :] * (row - scalar_ref[f : f + 1, :])
         for d in range(out_ref.shape[0]):
             out_ref[d, rows - 2 + f : rows - 1 + f, :] = log_weight
 
 
-def final_kernel(rows_each, atoms_all, beta_ref, in_ref, target_ref, chunk_ref, mean_ref, out_ref):
+def final_kernel(
+    rows_each, atoms_all, scalar_ref, in_ref, target_ref, chunk_ref, mean_ref, out_ref
+):
     devices = in_ref.shape[0]
     q = target_ref.shape[1]
     base = 2 * rows_each
@@ -494,7 +513,7 @@
     slope_sq = (mean - target_ref[...]) / target_var
     observed = jnp.sum(structure * slope_sq, axis=1, keepdims=True)
     average = jnp.sum(mean * slope_sq, axis=1, keepdims=True)
-    factor = (-beta_ref[0]) * weights * (observed - average)
+    factor = -scalar_ref[2:3, :] * weights * (observed - average)
     grad = jnp.zeros((rows_each, LANES), f32)
     for d in range(devices):
         for f in range(2):
@@ -581,7 +600,10 @@
     )
     below = lax.ppermute(leave_up, "slab", up)
     above = lax.ppermute(leave_down, "slab", down)
+    q = s_target.shape[0]
     small = (
+        u_reference.reshape(1, frames),
+        e_shift.reshape(1, 2),
         atom_count.reshape(1, frames),
         q_vectors,
         embedding,
@@ -591,10 +613,10 @@
         w_up,
         w_out.reshape(1, channels),
     )
-    neighbours, w1, w2, wup, wmsg, kinds, wout, structure, living = call(
+    neighbours, w1, w2, wup, wmsg, kinds, wout, structure, living, scalars, target = call(
         stage_kernel,
         "staged_inputs",
-        [SM, VM, VM] + [HB] * 9,
+        [SM, SM, VM, VM] + [HB] * 12,
         (
             array(neighbours.shape, jnp.int32),
             array((2, GROUP * hidden, GROUP * basis), bf16),
@@ -605,12 +627,16 @@
             array((channels, LANES)),
             array((EXTRA, LANES)),
             array((frames, atoms)),
+            array((8, LANES)),
+            array((1, q)),
         ),
-        [pltpu.VMEM(w.shape, w.dtype) for w in small] + [pltpu.SemaphoreType.DMA((9,))],
+        [pltpu.VMEM(w.shape, w.dtype) for w in small] + [pltpu.SemaphoreType.DMA((12,))],
         lax.axis_index("slab").reshape(1),
+        inverse_temp,
         positions,
         species,
         in_hbm(neighbours),
+        in_hbm(s_target.reshape(1, q)),
         *map(in_hbm, small),
     )
     halo_rows = array((frames, channels, halo), bf16)
@@ -654,7 +680,7 @@
     atom_energy, chunks = call(
         functools.partial(second_kernel, rows_each),
         "second_layer",
-        [VM, VM, SM] + [VM] * 11,
+        [VM] * 14,
         (array((frames, atoms)), array((slab_devs, chunk_rows, LANES))),
         [
             pltpu.VMEM((4, channels, atoms), f32),
@@ -663,7 +689,7 @@
         ],
         living,
         species,
-        e_shift,
+        scalars,
         neighbours,
         geometry,
         radial_hidden,
@@ -680,24 +706,22 @@
     totals = call(
         total_kernel,
         "slab_totals",
-        [SM, SM, VM],
+        [VM, VM],
         array((frame_devs, chunk_rows, LANES)),
         [],
-        u_reference,
-        inverse_temp,
+        scalars,
         chunks,
     )
     totals = lax.all_to_all(totals, "frame", 0, 0, tiled=True)
-    q = s_target.shape[0]
     grad_rows, mean_structure, grad_out = call(
         functools.partial(final_kernel, rows_each, atoms * slab_devs),
         "reweighted",
-        [SM, VM, VM],
+        [VM] * 3,
         (array((slab_devs, rows_each, LANES)), array((1, q)), array((1, channels))),
         [],
-        inverse_temp,
+        scalars,
         totals,
-        s_target.reshape(1, q),
+        target,
     )
     grad_up = lax.all_to_all(grad_rows, "slab", 0, 0, tiled=True)
     return (

time: 84.9 us -> 84.1 us (level)
  blocking collectives: 27.2 us -> 45.8 us
  waiting for transfers between devices: 10.8 us -> 0.01 us
  starting transfers between devices: 21 us -> 13.6 us
  Pallas kernels: 23.6 us -> 22.4 us
    all_to_all x0 -> x1, blocking collectives: none -> 18.6 us  [per_device(): chunks = lax.all_to_all(chunks, 'slab', 0, 0, tiled=True)]
    all_to_all x1 -> x0, waiting for transfers between devices: 10.8 us -> none  [per_device(): chunks = lax.all_to_all(chunks, 'slab', 0, 0, tiled=True)]
    all_to_all x1 -> x0, starting transfers between devices: 7.34 us -> none  [per_device(): chunks = lax.all_to_all(chunks, 'slab', 0, 0, tiled=True)]
    pallas_call x7, Pallas kernels: 23.6 us -> 22.4 us  [call(): pl.pallas_call(kernel, name=name, out_shape=outs, in_specs=ins, out_specs...]
  transfers between devices with their start and end apart: 5 -> 4, of which waited for: 1 -> 0; matrix products, arithmetic and copies ran while one was open for 0% -> 0% of each run, Pallas kernels for 5% -> 5%
where the time goes in v3:
time: 84.1 us; the launch traced here: 83.8 us
  blocking collectives  45.8 us (54%)
  Pallas kernels  22.4 us (27%)
  starting transfers between devices  13.6 us (16%)
  between operations  1.36 us (2%)
    pallas_call x7, Pallas kernels, call(): pl.pallas_call(kernel, name=name, out_shape=outs, in_specs=ins, out_specs...  22.4 us
    all_to_all x1, blocking collectives, per_device(): chunks = lax.all_to_all(chunks, 'slab', 0, 0, tiled=True)  18.6 us
    all_to_all x1, blocking collectives, per_device(): totals = lax.all_to_all(totals, 'frame', 0, 0, tiled=True)  14.5 us
    all_to_all x1, blocking collectives, per_device(): grad_up = lax.all_to_all(grad_rows, 'slab', 0, 0, tiled=True)  12.7 us
    ppermute x1, starting transfers between devices, per_device(): above = lax.ppermute(leave_down, 'slab', down)  6.65 us
    ppermute x1, starting transfers between devices, per_device(): msg_above = lax.ppermute(msg_down, 'slab', down)  4.77 us
    ppermute x1, starting transfers between devices, per_device(): below = lax.ppermute(leave_up, 'slab', up)  2.12 us
  transfers between devices with their start and end apart: 4, of which 0 were waited for; matrix products, arithmetic and copies ran while one was open for 0% of the time, Pallas kernels for 5%

profile of v3, /device:TPU:1, one launch (start us, length us, event | category | flops | bytes accessed | tf_op | source)
XLA Modules:
  0.0 83.8 jit_solution(8916029282577184403)
XLA Ops:
  0.6 0.9 %halo_rows.1 = (f32[8,128]{1,0:T(8,128)S(1)}, f32[8,128]{1,0:T(8,128)S(1)}, f32[3,2,256]{2,1,0:T(2,128)S(1)}, s32[2,256]{1,0:T(2,128)S(1)}, s32[2,2,128]{2,1,0:T(2,128)S(1)}) custom-call(f32[3,2,256]{2,1,0:T(2,128)} %bitcast.13, s32[2,256]{1,0:T(2,128)} %spec_hbm.1, s32[2,2,128]{2,1,0:T(2,128)} %halo_hbm.1), custom_call_target="tpu_custom_call" | custom-call | tf_op jit(solution)/shard_map/halo_rows/pallas_call | solution.py:534
  1.5 2.1 %collective-permute-start = (f32[8,128]{1,0:T(8,128)S(1)}, f32[8,128]{1,0:T(8,128)S(1)}, u32[]{:S(2)}, u32[]{:S(2)}) collective-permute-start(f32[8,128]{1,0:T(8,128)S(1)} %get-tuple-element.35), channel_id=1, source_target_pairs={{0,1},{1,2},{2,3},{3,4},{4,5},{5,6},{6,7},{7,8},{8,9},{9,10},{10,1... | collective-permute-start | bytes 12296 | tf_op jit(solution)/shard_map/ppermute | solution.py:601
  3.6 6.6 %collective-permute-start.1 = (f32[8,128]{1,0:T(8,128)S(1)}, f32[8,128]{1,0:T(8,128)S(1)}, u32[]{:S(2)}, u32[]{:S(2)}) collective-permute-start(f32[8,128]{1,0:T(8,128)S(1)} %get-tuple-element.36), channel_id=1, source_target_pairs={{1,0},{2,1},{3,2},{4,3},{5,4},{6,5},{7,6},{8,7},{9,8},{10,9},{11,1... | collective-permute-start | bytes 12296 | tf_op jit(solution)/shard_map/ppermute | solution.py:602
  10.9 2.0 %staged_inputs.1 = (s32[2,6,8,256]{3,2,1,0:T(8,128)S(1)}, bf16[2,256,32]{2,1,0:T(8,128)(2,1)S(1)}, bf16[2,256,64]{2,1,0:T(8,128)(2,1)S(1)}, bf16[2,128,256]{2,1,...) custom-call(s32[1]{0:T(128)} %bitcast.slab_ref, ...), custom_call_target="tpu_custom_call" | custom-call | tf_op jit(solution)/shard_map/staged_inputs/pallas_call | solution.py:534
  12.9 0.0 collective-permute-done.below_ref
  12.9 0.0 collective-permute-done.1.above_ref
  13.0 7.2 %first_layer.1 = (f32[2,4,6,8,256]{4,3,2,1,0:T(8,128)S(1)}, f32[2,128,256]{2,1,0:T(8,128)S(1)}, bf16[2,128,256]{2,1,0:T(8,128)(2,1)S(1)}, bf16[2,128,128]{2,1,0:T(8,128)(2,1)S(1)}, bf16[2,128,128]{2,1,0:T(8,128)(2,1)S(1)}) custom-call(f32[3,2,256]{2,1,0:T(2,128)S(1)} %get-tuple-element.30.pos_ref, s32[2,256]{1,0:T(2,128)S(1)} %get-tuple-element.31.spec_ref, ...), custom_call_target="tpu_custom_call" | custom-call | tf_op jit(solution)/shard_map/first_layer/pallas_call | solution.py:534
  20.2 0.1 collective-permute-start.2
  20.3 4.8 %collective-permute-start.3 = (bf16[2,128,128]{2,1,0:T(8,128)(2,1)S(1)}, bf16[2,128,128]{2,1,0:T(8,128)(2,1)S(1)}, u32[]{:S(2)}, u32[]{:S(2)}) collective-permute-start(bf16[2,128,128]{2,1,0:T(8,128)(2,1)S(1)} %get-tuple-element.47), channel_id=1, source_target_pairs={{1,0},{2,1},{3,2},{4,3},{5,4},{6,5},{7,6},{8,7},{9,8},{10,9},{11,1... | collective-permute-start | bytes 196616 | tf_op jit(solution)/shard_map/ppermute | solution.py:668
  25.1 2.2 %radial_hidden.1.hid_ref = bf16[2,6,512,256]{3,2,1,0:T(8,128)(2,1)S(1)} custom-call(f32[2,4,6,8,256]{4,3,2,1,0:T(8,128)S(1)} %get-tuple-element.43.geo_ref, s32[2,6,8,256]{3,2,1,0:T(8,128)S(1)} %get-tuple-element.34.nb_ref, bf16[2,256,32]{2,1,0:T(8,128)(2,1)S(1)} %get-tuple-element.38.w1_ref, bf16[2,256,64]{2,1,0:T(8,128)(2,1)S(1)} %get-tuple-element.39.w2_ref), custom_call_target="tpu_custom_call" | custom-call | tf_op jit(solution)/shard_map/radial_hidden/pallas_call | solution.py:534
  27.2 0.0 collective-permute-done.2.below_ref
  27.2 0.0 collective-permute-done.3.above_ref
  27.2 9.4 %second_layer.1 = (f32[2,256]{1,0:T(2,128)}, f32[32,24,128]{2,1,0:T(8,128)S(1)}) custom-call(f32[2,256]{1,0:T(2,128)S(1)} %get-tuple-element.32.live_ref, s32[2,256]{1,0:T(2,128)S(1)} %get-tuple-element.31.spec_ref, f32[8,128]{1,0:T(8,128)S(1)} %get-tuple-element.33.scalar_ref, s32[2,6,8,256]{3,2,1,0:T(8,128)S(1)} %get-tuple-element.34.nb_ref, ...), custom_call_target="tpu_custom_call" | custom-call | tf_op jit(solution)/shard_map/second_layer/pallas_call | solution.py:534
  36.7 18.6 %all_to_all.15.in_ref = f32[32,24,128]{2,1,0:T(8,128)S(1)} all-to-all(f32[32,24,128]{2,1,0:T(8,128)S(1)} %get-tuple-element.51), channel_id=1, replica_groups=mesh['frame'=8,'slab'=32] {'slab'}, dimensions={0} | all-to-all | bytes 786432 | tf_op jit(solution)/shard_map/all_to_all | solution.py:705
  55.3 14.5 %all_to_all.16.in_ref = f32[8,24,128]{2,1,0:T(8,128)S(1)} all-to-all(f32[8,24,128]{2,1,0:T(8,128)S(1)} %slab_totals.1), channel_id=1, replica_groups=mesh['frame'=8,'slab'=32] {'frame'}, dimensions={0} | all-to-all | bytes 196608 | tf_op jit(solution)/shard_map/all_to_all | solution.py:715
  69.9 0.6 reweighted.1
  70.5 12.7 %all_to_all.17 = f32[32,8,128]{2,1,0:T(8,128)S(1)} all-to-all(f32[32,8,128]{2,1,0:T(8,128)S(1)} %get-tuple-element.54), channel_id=1, replica_groups=mesh['frame'=8,'slab'=32] {'slab'}, dimensions={0} | all-to-all | bytes 262144 | tf_op jit(solution)/shard_map/all_to_all | solution.py:726
  83.2 0.7 copy.22
  (1 shorter events, 0.0 us)
Async XLA Ops:
  1.5 11.4 %collective-permute-start = (f32[8,128]{1,0:T(8,128)S(1)}, f32[8,128]{1,0:T(8,128)S(1)}, u32[]{:S(2)}, u32[]{:S(2)}) collective-permute-start(f32[8,128]{1,0:T(8,128)S(1)} %get-tuple-element.35), channel_id=1, source_target_pairs={{0,1},{1,2},{2,3},{3,4},{4,5},{5,6},{6,7},{7,8},{8,9},{9,10},{10,1... | collective-permute-start | bytes 12296 | tf_op jit(solution)/shard_map/ppermute | solution.py:601
  3.6 9.3 %collective-permute-start.1 = (f32[8,128]{1,0:T(8,128)S(1)}, f32[8,128]{1,0:T(8,128)S(1)}, u32[]{:S(2)}, u32[]{:S(2)}) collective-permute-start(f32[8,128]{1,0:T(8,128)S(1)} %get-tuple-element.36), channel_id=1, source_target_pairs={{1,0},{2,1},{3,2},{4,3},{5,4},{6,5},{7,6},{8,7},{9,8},{10,9},{11,1... | collective-permute-start | bytes 12296 | tf_op jit(solution)/shard_map/ppermute | solution.py:602
  20.2 7.0 %collective-permute-start.2 = (bf16[2,128,128]{2,1,0:T(8,128)(2,1)S(1)}, bf16[2,128,128]{2,1,0:T(8,128)(2,1)S(1)}, u32[]{:S(2)}, u32[]{:S(2)}) collective-permute-start(bf16[2,128,128]{2,1,0:T(8,128)(2,1)S(1)} %get-tuple-element.46), channel_id=1, source_target_pairs={{0,1},{1,2},{2,3},{3,4},{4,5},{5,6},{6,7},{7,8},{8,9},{9,10},{10,1... | collective-permute-start | bytes 196616 | tf_op jit(solution)/shard_map/ppermute | solution.py:667
  20.3 6.9 %collective-permute-start.3 = (bf16[2,128,128]{2,1,0:T(8,128)(2,1)S(1)}, bf16[2,128,128]{2,1,0:T(8,128)(2,1)S(1)}, u32[]{:S(2)}, u32[]{:S(2)}) collective-permute-start(bf16[2,128,128]{2,1,0:T(8,128)(2,1)S(1)} %get-tuple-element.47), channel_id=1, source_target_pairs={{1,0},{2,1},{3,2},{4,3},{5,4},{6,5},{7,6},{8,7},{9,8},{10,9},{11,1... | collective-permute-start | bytes 196616 | tf_op jit(solution)/shard_map/ppermute | solution.py:668

commit v4 on v3

--- a/solution.py
+++ b/solution.py
@@ -14,6 +14,7 @@
 LANES = 128
 GROUP = 4
 EXTRA = 8
+EMPTY = 1.0e4
 XLU = 32
 UN1 = 6
 UNH = 3
@@ -112,102 +113,49 @@
 
 
 def stage_kernel(
-    slab_ref,
     beta_ref,
-    pos_ref,
-    spec_ref,
     nb_hbm,
-    target_hbm,
-    uref_hbm,
-    eshift_hbm,
-    count_hbm,
-    q_hbm,
     emb_hbm,
     wmsg_hbm,
     wr1_hbm,
     wr2_hbm,
     wup_hbm,
-    wout_hbm,
     nb_ref,
     w1_ref,
     w2_ref,
     wup_ref,
     wmsg_ref,
     kind_ref,
-    wout_ref,
-    struct_ref,
-    live_ref,
-    scalar_ref,
-    target_ref,
-    uref_in,
-    eshift_in,
-    count_in,
-    q_in,
+    temp_ref,
     emb_in,
     wmsg_in,
     wr1_in,
     wr2_in,
     wup_in,
-    wout_in,
     sems,
 ):
     pairs = (
-        (count_hbm, count_in),
-        (uref_hbm, uref_in),
-        (eshift_hbm, eshift_in),
-        (target_hbm, target_ref),
-        (q_hbm, q_in),
+        (nb_hbm, nb_ref),
         (wr1_hbm, wr1_in),
-        (wr2_hbm, wr2_in),
-        (wup_hbm, wup_in),
+        (wr2_hbm.at[0], wr2_in),
+        (wup_hbm.at[0], wup_in),
         (wmsg_hbm, wmsg_in),
         (emb_hbm, emb_in),
-        (wout_hbm, wout_in),
-        (nb_hbm, nb_ref),
     )
     copies = fetch_all(sems, pairs)
-    for copy in copies[:-1]:
+    temp_ref[...] = jnp.full((1, LANES), beta_ref[0], f32)
+    for copy in copies:
         copy.wait()
-    _, frames, atoms = pos_ref.shape
-    number_q = q_in.shape[1]
-    same = lax.broadcasted_iota(jnp.int32, (number_q, number_q), 0) == lax.broadcasted_iota(
-        jnp.int32, (number_q, number_q), 1
-    )
-    q = [
-        jnp.sum(jnp.where(same, spread(q_in[c : c + 1, :], number_q), 0.0), axis=1, keepdims=True)
-        for c in range(3)
-    ]
-    lift = slab_ref[0].astype(f32) * slab_depth
-    number = lax.broadcasted_iota(jnp.int32, (1, atoms), 1)
-    struct_ref[...] = jnp.zeros_like(struct_ref)
-    for f in range(frames):
-        x, y, z = (pos_ref[c, f : f + 1, :] for c in range(3))
-        phases = q[0] * x + q[1] * y + q[2] * (z + lift)
-        lengths = jnp.where(spec_ref[f : f + 1, :] == 1, 1.0, hydrogen_length)
-        living = (number < count_in[:, f : f + 1]).astype(f32)
-        live_ref[f : f + 1, :] = living
-        lengths = living * lengths
-        cos_part = jnp.sum(lengths * jnp.cos(phases), axis=1, keepdims=True)
-        sin_part = jnp.sum(lengths * jnp.sin(phases), axis=1, keepdims=True)
-        struct_ref[2 + f : 3 + f, :] = as_row(cos_part)
-        struct_ref[4 + f : 5 + f, :] = as_row(sin_part)
     for layer in range(2):
         w1_ref[layer] = rad1_blocks(wr1_in[layer])
-        w2_ref[layer] = transposed(wr2_in[layer])
-        wup_ref[layer] = transposed(wup_in[layer])
+    w2_ref[...] = transposed(wr2_in[...])
+    wup_ref[...] = transposed(wup_in[...])
     wmsg_ref[...] = transposed(wmsg_in[1])
     emb = emb_in[...]
     table = mm(emb, wmsg_in[0]).astype(bf16).astype(f32)
     for k in range(2):
         kind_ref[k] = column(emb[k : k + 1].astype(f32))
         kind_ref[2 + k] = column(table[k : k + 1])
-    wout_ref[...] = column(wout_in[...])
-    for k in range(2):
-        scalar_ref[k : k + 1, :] = jnp.broadcast_to(uref_in[:, k : k + 1], (1, LANES))
-        scalar_ref[2 + k : 3 + k, :] = jnp.full((1, LANES), beta_ref[0], f32)
-        scalar_ref[4 + k : 5 + k, :] = jnp.broadcast_to(eshift_in[:, k : k + 1], (1, LANES))
-    scalar_ref[6:8, :] = jnp.zeros((2, LANES), f32)
-    copies[-1].wait()
 
 
 def basis_rows(dist_ref, f, i, first, atoms):
@@ -242,9 +190,9 @@
     _, frames, atoms = pos_ref.shape
     batches = nb_ref.shape[1]
     slots = batches * 8
-    hidden = w2_ref.shape[2]
-    w2s = jnp.concatenate([w2_ref[0, :LANES, :]] * 2, axis=1)
-    w2v = jnp.concatenate([w2_ref[0, LANES:, :]] * 2, axis=1)
+    hidden = w2_ref.shape[1]
+    w2s = jnp.concatenate([w2_ref[:LANES, :]] * 2, axis=1)
+    w2v = jnp.concatenate([w2_ref[LANES:, :]] * 2, axis=1)
     scale = slots**-0.5
     for f in range(frames):
         for half in range(atoms // LANES):
@@ -253,7 +201,6 @@
                 index = nb_ref[f, s, :, cols]
                 lane = index & (LANES - 1)
                 block = index >> 7
-                present = (index >= 0).astype(f32)
 
                 def fetch(own_row, halo_row):
                     parts = [
@@ -282,7 +229,7 @@
                     offsets.append(offset)
                     geo_ref[f, c, s, :, cols] = offset
                     squares = offset * offset if squares is None else squares + offset * offset
-                geo_ref[f, 3, s, :, cols] = jnp.sqrt(squares)
+                geo_ref[f, 3, s, :, cols] = jnp.where(index >= 0, jnp.sqrt(squares), EMPTY)
                 parts = fetch(spec_ref[f : f + 1, :].astype(f32), 4 * f + 3)
                 got = [lane_gather(spread(p, 8), lane) for p in parts]
                 kind = jnp.where(
@@ -290,11 +237,10 @@
                     got[0],
                     jnp.where(block == 1, got[1], jnp.where(block == 2, got[2], got[3])),
                 )
-                kinds = (present * (1.0 - kind), present * kind)
-                for k in range(2):
-                    wgt_ref[k, s, :, cols] = kinds[k]
-                    for c in range(3):
-                        wgt_ref[2 * (c + 1) + k, s, :, cols] = offsets[c] * kinds[k]
+                wgt_ref[0, s, :, cols] = kind
+                for c in range(3):
+                    wgt_ref[2 * c + 1, s, :, cols] = offsets[c] * (1.0 - kind)
+                    wgt_ref[2 * c + 2, s, :, cols] = offsets[c] * kind
         acc_ref[...] = jnp.zeros_like(acc_ref)
 
         def step(i, carry):
@@ -309,14 +255,20 @@
                     for j in range(8):
                         at = (j % GROUP) * hidden + part
                         hid.append(acts[j // GROUP][at : at + 32, cols])
-                    for k in range(8):
-                        total = acc_ref[k, part : part + 32, cols]
+                    total = hid[0]
+                    for j in range(1, 8):
+                        total = total + hid[j]
+                    acc_ref[0, part : part + 32, cols] += total
+                    for k in range(7):
+                        total = acc_ref[k + 1, part : part + 32, cols]
                         for j in range(8):
                             total = total + wgt_ref[k, i, j : j + 1, cols] * hid[j]
-                        acc_ref[k, part : part + 32, cols] = total
+                        acc_ref[k + 1, part : part + 32, cols] = total
             return carry
 
         lax.fori_loop(0, batches, step, 0, unroll=UN1)
+
+        acc_ref[0] = acc_ref[0] - acc_ref[1]
 
         def project(k, w):
             total = acc_ref[k]
@@ -334,7 +286,7 @@
             )
             squared = vec * vec if squared is None else squared + vec * vec
         mixed = jnp.concatenate([scalar, squared], axis=0).astype(bf16)
-        update = mm(wup_ref[0], mixed)
+        update = mm(wup_ref[...], mixed)
         e0 = jnp.concatenate([kind_ref[0]] * 2, axis=1)
         e1 = jnp.concatenate([kind_ref[1]] * 2, axis=1)
         features = jnp.where(spec_ref[f : f + 1, :] == 1, e1, e0) + silu(update)
@@ -350,22 +302,93 @@
             out[f] = jnp.where(index >= LANES, high_g, low_g).astype(bf16)
 
 
-def hidden_kernel(geo_ref, nb_ref, w1_ref, w2_ref, out_ref):
-    frames, batches, _, atoms = nb_ref.shape
-    hidden = w2_ref.shape[2]
+def hidden_kernel(
+    slab_ref,
+    geo_ref,
+    w1_ref,
+    temp_ref,
+    pos_ref,
+    spec_ref,
+    target_hbm,
+    uref_hbm,
+    eshift_hbm,
+    count_hbm,
+    q_hbm,
+    wr2_hbm,
+    wup_hbm,
+    wout_hbm,
+    out_ref,
+    w2_ref,
+    wup_ref,
+    wout_ref,
+    struct_ref,
+    live_ref,
+    scalar_ref,
+    target_ref,
+    uref_in,
+    eshift_in,
+    count_in,
+    q_in,
+    wr2_in,
+    wup_in,
+    wout_in,
+    sems,
+):
+    pairs = (
+        (target_hbm, target_ref),
+        (uref_hbm, uref_in),
+        (eshift_hbm, eshift_in),
+        (count_hbm, count_in),
+        (q_hbm, q_in),
+        (wr2_hbm.at[1], wr2_in),
+        (wup_hbm.at[1], wup_in),
+        (wout_hbm, wout_in),
+    )
+    copies = fetch_all(sems, pairs)
+    _, frames, atoms = pos_ref.shape
+    batches = geo_ref.shape[2]
+    hidden = wr2_in.shape[0]
     for f in range(frames):
 
         def step(i, carry):
             for first in range(0, 8, GROUP):
                 act = silu(mm(w1_ref[1], basis_rows(geo_ref, f, i, first, atoms)))
-                for j in range(GROUP):
-                    here = nb_ref[f, i, first + j : first + j + 1, :] >= 0
-                    rows = slice(j * hidden, (j + 1) * hidden)
-                    kept = jnp.where(here, act[rows], 0.0).astype(bf16)
-                    out_ref[f, i, (first + j) * hidden : (first + j + 1) * hidden, :] = kept
+                out_ref[f, i, first * hidden : (first + GROUP) * hidden, :] = act.astype(bf16)
             return carry
 
         lax.fori_loop(0, batches, step, 0, unroll=UNH)
+    for copy in copies:
+        copy.wait()
+    number_q = q_in.shape[1]
+    same = lax.broadcasted_iota(jnp.int32, (number_q, number_q), 0) == lax.broadcasted_iota(
+        jnp.int32, (number_q, number_q), 1
+    )
+    q = [
+        jnp.sum(jnp.where(same, spread(q_in[c : c + 1, :], number_q), 0.0), axis=1, keepdims=True)
+        for c in range(3)
+    ]
+    lift = slab_ref[0].astype(f32) * slab_depth
+    number = lax.broadcasted_iota(jnp.int32, (1, atoms), 1)
+    struct_ref[...] = jnp.zeros_like(struct_ref)
+    for f in range(frames):
+        x, y, z = (pos_ref[c, f : f + 1, :] for c in range(3))
+        phases = q[0] * x + q[1] * y + q[2] * (z + lift)
+        lengths = jnp.where(spec_ref[f : f + 1, :] == 1, 1.0, hydrogen_length)
+        living = (number < count_in[:, f : f + 1]).astype(f32)
+        live_ref[f : f + 1, :] = living
+        lengths = living * lengths
+        cos_part = jnp.sum(lengths * jnp.cos(phases), axis=1, keepdims=True)
+        sin_part = jnp.sum(lengths * jnp.sin(phases), axis=1, keepdims=True)
+        struct_ref[2 + f : 3 + f, :] = as_row(cos_part)
+        struct_ref[4 + f : 5 + f, :] = as_row(sin_part)
+    w2_ref[...] = transposed(wr2_in[...])
+    wup_ref[...] = transposed(wup_in[...])
+    wout_ref[...] = column(wout_in[...])
+    for k in range(2):
+        scalar_ref[k : k + 1, :] = jnp.broadcast_to(uref_in[:, k : k + 1], (1, LANES))
+        scalar_ref[2 + k : 3 + k, :] = temp_ref[...]
+        scalar_ref[4 + k : 5 + k, :] = jnp.broadcast_to(eshift_in[:, k : k + 1], (1, LANES))
+    scalar_ref[6:8, :] = jnp.zeros((2, LANES), f32)
 
 
 def second_kernel(
@@ -384,15 +407,17 @@
     wup_ref,
     wout_ref,
     struct_ref,
-    energy_ref,
+    energy_hbm,
     chunk_ref,
     acc_ref,
     src_ref,
     pair_ref,
+    energy_ref,
+    sem,
 ):
     frames, batches, _, atoms = nb_ref.shape
     slots = batches * 8
-    hidden = w2_ref.shape[2]
+    hidden = w2_ref.shape[1]
     chunks = chunk_ref.shape[0]
     wout = jnp.concatenate([wout_ref[...]] * 2, axis=1)
     shift = [jnp.concatenate([scalar_ref[4 + k : 5 + k, :]] * 2, axis=1) for k in range(2)]
@@ -409,7 +434,7 @@
 
         def step(i, carry):
             filters = [
-                mm(w2_ref[1], hid_ref[f, i, j * hidden : (j + 1) * hidden, :]) for j in range(8)
+                mm(w2_ref[...], hid_ref[f, i, j * hidden : (j + 1) * hidden, :]) for j in range(8)
             ]
             width = WIDTH
             if XLU < LANES:
@@ -460,7 +485,7 @@
             vec = (scale * vector_scale) * acc_ref[c + 1]
             squared = vec * vec if squared is None else squared + vec * vec
         mixed = jnp.concatenate([scalar, squared], axis=0).astype(bf16)
-        update = mm(wup_ref[1], mixed)
+        update = mm(wup_ref[...], mixed)
         gate = sigmoid(update)
         features = feat_ref[f] + update * gate
         living = live_ref[f : f + 1, :]
@@ -469,6 +494,9 @@
         readout = jnp.sum(features * wout, axis=0, keepdims=True)
         energy = living * (readout + jnp.where(kind == 1, shift[1], shift[0]))
         energy_ref[f : f + 1, :] = energy
+        if f == frames - 1:
+            leaving = pltpu.make_async_copy(energy_ref, energy_hbm, sem)
+            leaving.start()
         grad = lax.dot_general(mixed, slope, (((1,), (1,)), ((), ())), preferred_element_type=f32)
         chunk_ref[:, f * rows_each : (f + 1) * rows_each, :] = grad.reshape(
             chunks, rows_each, LANES
@@ -479,6 +507,7 @@
         extra[6 + f] = jnp.broadcast_to(jnp.sum(energy, axis=1, keepdims=True), (1, LANES))
     block = jnp.concatenate(extra, axis=0)
     chunk_ref[:, frames * rows_each :, :] = jnp.broadcast_to(block[None], (chunks, EXTRA, LANES))
+    leaving.wait()
 
 
 def total_kernel(scalar_ref, in_ref, out_ref):
@@ -530,13 +559,13 @@
 HB = pl.BlockSpec(memory_space=pltpu.HBM)
 
 
-def call(kernel, name, ins, outs, scratch, *operands):
+def call(kernel, name, ins, outs, scratch, *operands, specs=None):
     return pl.pallas_call(
         kernel,
         name=name,
         out_shape=outs,
         in_specs=ins,
-        out_specs=jax.tree.map(lambda _: VM, outs),
+        out_specs=specs or jax.tree.map(lambda _: VM, outs),
         scratch_shapes=scratch,
         compiler_params=pltpu.CompilerParams(vmem_limit_bytes=VMEM_BYTES),
     )(*operands)
@@ -601,43 +630,25 @@
     below = lax.ppermute(leave_up, "slab", up)
     above = lax.ppermute(leave_down, "slab", down)
     q = s_target.shape[0]
-    small = (
-        u_reference.reshape(1, frames),
-        e_shift.reshape(1, 2),
-        atom_count.reshape(1, frames),
-        q_vectors,
-        embedding,
-        w_msg,
-        w_rad1,
-        w_rad2,
-        w_up,
-        w_out.reshape(1, channels),
-    )
-    neighbours, w1, w2, wup, wmsg, kinds, wout, structure, living, scalars, target = call(
+    staged = (embedding, w_msg, w_rad1)
+    halves = (array(w_rad2.shape[1:], bf16), array(w_up.shape[1:], bf16))
+    neighbours, w1, w2, wup, wmsg, kinds, temp = call(
         stage_kernel,
         "staged_inputs",
-        [SM, SM, VM, VM] + [HB] * 12,
+        [SM] + [HB] * 6,
         (
             array(neighbours.shape, jnp.int32),
             array((2, GROUP * hidden, GROUP * basis), bf16),
-            array((2, 2 * channels, hidden), bf16),
-            array((2, channels, 2 * channels), bf16),
+            array((2 * channels, hidden), bf16),
+            array((channels, 2 * channels), bf16),
             array((channels, channels), bf16),
             array((4, channels, LANES)),
-            array((channels, LANES)),
-            array((EXTRA, LANES)),
-            array((frames, atoms)),
-            array((8, LANES)),
-            array((1, q)),
+            array((1, LANES)),
         ),
-        [pltpu.VMEM(w.shape, w.dtype) for w in small] + [pltpu.SemaphoreType.DMA((12,))],
-        lax.axis_index("slab").reshape(1),
+        [pltpu.VMEM(w.shape, w.dtype) for w in (*staged, *halves)]
+        + [pltpu.SemaphoreType.DMA((6,))],
         inverse_temp,
-        positions,
-        species,
-        in_hbm(neighbours),
-        in_hbm(s_target.reshape(1, q)),
-        *map(in_hbm, small),
+        *map(in_hbm, (neighbours, *staged, w_rad2, w_up)),
     )
     halo_rows = array((frames, channels, halo), bf16)
     geometry, features, message, msg_down, msg_up = call(
@@ -651,7 +662,7 @@
             halo_rows,
             halo_rows,
         ),
-        [pltpu.VMEM((8, slots // 8, 8, atoms), f32), pltpu.VMEM((8, hidden, atoms), f32)],
+        [pltpu.VMEM((7, slots // 8, 8, atoms), f32), pltpu.VMEM((8, hidden, atoms), f32)],
         positions,
         species,
         below,
@@ -666,16 +677,36 @@
     )
     msg_below = lax.ppermute(msg_up, "slab", up)
     msg_above = lax.ppermute(msg_down, "slab", down)
-    radial_hidden = call(
+    small = (
+        u_reference.reshape(1, frames),
+        e_shift.reshape(1, 2),
+        atom_count.reshape(1, frames),
+        q_vectors,
+    )
+    wout_row = w_out.reshape(1, channels)
+    radial_hidden, w2, wup, wout, structure, living, scalars, target = call(
         hidden_kernel,
         "radial_hidden",
-        [VM] * 4,
-        array((frames, slots // 8, 8 * hidden, atoms), bf16),
-        [],
+        [SM] + [VM] * 5 + [HB] * 8,
+        (
+            array((frames, slots // 8, 8 * hidden, atoms), bf16),
+            array((2 * channels, hidden), bf16),
+            array((channels, 2 * channels), bf16),
+            array((channels, LANES)),
+            array((EXTRA, LANES)),
+            array((frames, atoms)),
+            array((8, LANES)),
+            array((1, q)),
+        ),
+        [pltpu.VMEM(w.shape, w.dtype) for w in (*small, *halves, wout_row)]
+        + [pltpu.SemaphoreType.DMA((8,))],
+        lax.axis_index("slab").reshape(1),
         geometry,
-        neighbours,
         w1,
-        w2,
+        temp,
+        positions,
+        species,
+        *map(in_hbm, (s_target.reshape(1, q), *small, w_rad2, w_up, wout_row)),
     )
     atom_energy, chunks = call(
         functools.partial(second_kernel, rows_each),
@@ -686,6 +717,8 @@
             pltpu.VMEM((4, channels, atoms), f32),
             pltpu.VMEM((4, channels, LANES), bf16),
             pltpu.VMEM((2 * (LANES - XLU), 2 * LANES), bf16),
+            pltpu.VMEM((frames, atoms), f32),
+            pltpu.SemaphoreType.DMA,
         ],
         living,
         species,
@@ -701,6 +734,7 @@
         wup,
         wout,
         structure,
+        specs=(HB, VM),
     )
     chunks = lax.all_to_all(chunks, "slab", 0, 0, tiled=True)
     totals = call(

time: 84.1 us -> 83.1 us (0.988)
  Pallas kernels: 22.4 us -> 21.5 us
    pallas_call x7, Pallas kernels: 22.4 us -> 21.5 us  [call(): pl.pallas_call(kernel, name=name, out_shape=outs, in_specs=ins, out_specs...]
  transfers between devices with their start and end apart: 4 -> 4, of which waited for: 0 -> 0; matrix products, arithmetic and copies ran while one was open for 0% -> 0% of each run, Pallas kernels for 5% -> 4%
where the time goes in v4:
time: 83.1 us; the launch traced here: 82.8 us
  blocking collectives  45.7 us (55%)
  Pallas kernels  21.5 us (26%)
  starting transfers between devices  13.6 us (16%)
  between operations  1.37 us (2%)
    pallas_call x7, Pallas kernels, call(): pl.pallas_call(kernel, name=name, out_shape=outs, in_specs=ins, out_specs...  21.5 us
    all_to_all x1, blocking collectives, per_device(): chunks = lax.all_to_all(chunks, 'slab', 0, 0, tiled=True)  18.5 us
    all_to_all x1, blocking collectives, per_device(): totals = lax.all_to_all(totals, 'frame', 0, 0, tiled=True)  14.5 us
    all_to_all x1, blocking collectives, per_device(): grad_up = lax.all_to_all(grad_rows, 'slab', 0, 0, tiled=True)  12.7 us
    ppermute x1, starting transfers between devices, per_device(): above = lax.ppermute(leave_down, 'slab', down)  6.65 us
    ppermute x1, starting transfers between devices, per_device(): msg_above = lax.ppermute(msg_down, 'slab', down)  4.77 us
    ppermute x1, starting transfers between devices, per_device(): below = lax.ppermute(leave_up, 'slab', up)  2.12 us
  transfers between devices with their start and end apart: 4, of which 0 were waited for; matrix products, arithmetic and copies ran while one was open for 0% of the time, Pallas kernels for 4%

profile of v4, /device:TPU:1, one launch (start us, length us, event | category | flops | bytes accessed | tf_op | source)
XLA Modules:
  0.0 82.8 jit_solution(3487208505543496456)
XLA Ops:
  0.6 0.9 %halo_rows.1 = (f32[8,128]{1,0:T(8,128)S(1)}, f32[8,128]{1,0:T(8,128)S(1)}, f32[3,2,256]{2,1,0:T(2,128)S(1)}, s32[2,256]{1,0:T(2,128)S(1)}, s32[2,2,128]{2,1,0:T(2,128)S(1)}) custom-call(f32[3,2,256]{2,1,0:T(2,128)} %bitcast.13, s32[2,256]{1,0:T(2,128)} %spec_hbm.1, s32[2,2,128]{2,1,0:T(2,128)} %halo_hbm.1), custom_call_target="tpu_custom_call" | custom-call | tf_op jit(solution)/shard_map/halo_rows/pallas_call | solution.py:563
  1.5 2.1 %collective-permute-start = (f32[8,128]{1,0:T(8,128)S(1)}, f32[8,128]{1,0:T(8,128)S(1)}, u32[]{:S(2)}, u32[]{:S(2)}) collective-permute-start(f32[8,128]{1,0:T(8,128)S(1)} %get-tuple-element.36), channel_id=1, source_target_pairs={{0,1},{1,2},{2,3},{3,4},{4,5},{5,6},{6,7},{7,8},{8,9},{9,10},{10,1... | collective-permute-start | bytes 12296 | tf_op jit(solution)/shard_map/ppermute | solution.py:630
  3.6 6.6 %collective-permute-start.1 = (f32[8,128]{1,0:T(8,128)S(1)}, f32[8,128]{1,0:T(8,128)S(1)}, u32[]{:S(2)}, u32[]{:S(2)}) collective-permute-start(f32[8,128]{1,0:T(8,128)S(1)} %get-tuple-element.37), channel_id=1, source_target_pairs={{1,0},{2,1},{3,2},{4,3},{5,4},{6,5},{7,6},{8,7},{9,8},{10,9},{11,1... | collective-permute-start | bytes 12296 | tf_op jit(solution)/shard_map/ppermute | solution.py:631
  10.9 1.3 %staged_inputs.1 = (s32[2,6,8,256]{3,2,1,0:T(8,128)S(1)}, bf16[2,256,32]{2,1,0:T(8,128)(2,1)S(1)}, bf16[256,64]{1,0:T(8,128)(2,1)S(1)}, bf16[128,256]{1,0:T(8,12...) custom-call(f32[1]{0:T(128)S(6)} %copy.21.beta_ref, ...), custom_call_target="tpu_custom_call" | custom-call | tf_op jit(solution)/shard_map/staged_inputs/pallas_call | solution.py:563
  12.2 0.0 collective-permute-done.below_ref
  12.2 0.0 collective-permute-done.1.above_ref
  12.2 6.9 %first_layer.1 = (f32[2,4,6,8,256]{4,3,2,1,0:T(8,128)S(1)}, f32[2,128,256]{2,1,0:T(8,128)S(1)}, bf16[2,128,256]{2,1,0:T(8,128)(2,1)S(1)}, bf16[2,128,128]{2,1,0:T(8,128)(2,1)S(1)}, bf16[2,128,128]{2,1,0:T(8,128)(2,1)S(1)}) custom-call(f32[3,2,256]{2,1,0:T(2,128)S(1)} %get-tuple-element.34.pos_ref, s32[2,256]{1,0:T(2,128)S(1)} %get-tuple-element.35.spec_ref, ...), custom_call_target="tpu_custom_call" | custom-call | tf_op jit(solution)/shard_map/first_layer/pallas_call | solution.py:563
  19.1 0.1 collective-permute-start.2
  19.2 4.8 %collective-permute-start.3 = (bf16[2,128,128]{2,1,0:T(8,128)(2,1)S(1)}, bf16[2,128,128]{2,1,0:T(8,128)(2,1)S(1)}, u32[]{:S(2)}, u32[]{:S(2)}) collective-permute-start(bf16[2,128,128]{2,1,0:T(8,128)(2,1)S(1)} %get-tuple-element.53), channel_id=1, source_target_pairs={{1,0},{2,1},{3,2},{4,3},{5,4},{6,5},{7,6},{8,7},{9,8},{10,9},{11,1... | collective-permute-start | bytes 196616 | tf_op jit(solution)/shard_map/ppermute | solution.py:679
  24.0 2.3 %radial_hidden.1 = (bf16[2,6,512,256]{3,2,1,0:T(8,128)(2,1)S(1)}, bf16[256,64]{1,0:T(8,128)(2,1)S(1)}, bf16[128,256]{1,0:T(8,128)(2,1)S(1)}, f32[128,128]{1,0:T(...) custom-call(s32[1]{0:T(128)} %bitcast.slab_ref, ...), custom_call_target="tpu_custom_call" | custom-call | tf_op jit(solution)/shard_map/radial_hidden/pallas_call | solution.py:563
  26.3 0.0 collective-permute-done.2.below_ref
  26.3 0.0 collective-permute-done.3.above_ref
  26.3 9.5 %second_layer.1 = (f32[2,256]{1,0:T(2,128)}, f32[32,24,128]{2,1,0:T(8,128)S(1)}) custom-call(f32[2,256]{1,0:T(2,128)S(1)} %get-tuple-element.47.live_ref, s32[2,256]{1,0:T(2,128)S(1)} %get-tuple-element.35.spec_ref, f32[8,128]{1,0:T(8,128)S(1)} %get-tuple-element.48.scalar_ref, s32[2,6,8,256]{3,2,1,0:T(8,128)S(1)} %get-tuple-element.38.nb_ref, ...), custom_call_target="tpu_custom_call" | custom-call | tf_op jit(solution)/shard_map/second_layer/pallas_call | solution.py:563
  35.8 18.5 %all_to_all.15.in_ref = f32[32,24,128]{2,1,0:T(8,128)S(1)} all-to-all(f32[32,24,128]{2,1,0:T(8,128)S(1)} %get-tuple-element.59), channel_id=1, replica_groups=mesh['frame'=8,'slab'=32] {'slab'}, dimensions={0} | all-to-all | bytes 786432 | tf_op jit(solution)/shard_map/all_to_all | solution.py:739
  54.3 14.5 %all_to_all.16.in_ref = f32[8,24,128]{2,1,0:T(8,128)S(1)} all-to-all(f32[8,24,128]{2,1,0:T(8,128)S(1)} %slab_totals.1), channel_id=1, replica_groups=mesh['frame'=8,'slab'=32] {'frame'}, dimensions={0} | all-to-all | bytes 196608 | tf_op jit(solution)/shard_map/all_to_all | solution.py:749
  68.9 0.6 reweighted.1
  69.5 12.7 %all_to_all.17 = f32[32,8,128]{2,1,0:T(8,128)S(1)} all-to-all(f32[32,8,128]{2,1,0:T(8,128)S(1)} %get-tuple-element.62), channel_id=1, replica_groups=mesh['frame'=8,'slab'=32] {'slab'}, dimensions={0} | all-to-all | bytes 262144 | tf_op jit(solution)/shard_map/all_to_all | solution.py:760
  82.2 0.7 copy.22
  (1 shorter events, 0.0 us)
Async XLA Ops:
  1.5 10.7 %collective-permute-start = (f32[8,128]{1,0:T(8,128)S(1)}, f32[8,128]{1,0:T(8,128)S(1)}, u32[]{:S(2)}, u32[]{:S(2)}) collective-permute-start(f32[8,128]{1,0:T(8,128)S(1)} %get-tuple-element.36), channel_id=1, source_target_pairs={{0,1},{1,2},{2,3},{3,4},{4,5},{5,6},{6,7},{7,8},{8,9},{9,10},{10,1... | collective-permute-start | bytes 12296 | tf_op jit(solution)/shard_map/ppermute | solution.py:630
  3.6 8.6 %collective-permute-start.1 = (f32[8,128]{1,0:T(8,128)S(1)}, f32[8,128]{1,0:T(8,128)S(1)}, u32[]{:S(2)}, u32[]{:S(2)}) collective-permute-start(f32[8,128]{1,0:T(8,128)S(1)} %get-tuple-element.37), channel_id=1, source_target_pairs={{1,0},{2,1},{3,2},{4,3},{5,4},{6,5},{7,6},{8,7},{9,8},{10,9},{11,1... | collective-permute-start | bytes 12296 | tf_op jit(solution)/shard_map/ppermute | solution.py:631
  19.1 7.2 %collective-permute-start.2 = (bf16[2,128,128]{2,1,0:T(8,128)(2,1)S(1)}, bf16[2,128,128]{2,1,0:T(8,128)(2,1)S(1)}, u32[]{:S(2)}, u32[]{:S(2)}) collective-permute-start(bf16[2,128,128]{2,1,0:T(8,128)(2,1)S(1)} %get-tuple-element.52), channel_id=1, source_target_pairs={{0,1},{1,2},{2,3},{3,4},{4,5},{5,6},{6,7},{7,8},{8,9},{9,10},{10,1... | collective-permute-start | bytes 196616 | tf_op jit(solution)/shard_map/ppermute | solution.py:678
  19.2 7.1 %collective-permute-start.3 = (bf16[2,128,128]{2,1,0:T(8,128)(2,1)S(1)}, bf16[2,128,128]{2,1,0:T(8,128)(2,1)S(1)}, u32[]{:S(2)}, u32[]{:S(2)}) collective-permute-start(bf16[2,128,128]{2,1,0:T(8,128)(2,1)S(1)} %get-tuple-element.53), channel_id=1, source_target_pairs={{1,0},{2,1},{3,2},{4,3},{5,4},{6,5},{7,6},{8,7},{9,8},{10,9},{11,1... | collective-permute-start | bytes 196616 | tf_op jit(solution)/shard_map/ppermute | solution.py:679

commit v5 on v4

--- a/solution.py
+++ b/solution.py
@@ -15,10 +15,9 @@
 GROUP = 4
 EXTRA = 8
 EMPTY = 1.0e4
-XLU = 32
 UN1 = 6
 UNH = 3
-UN2 = 2
+UN2 = 3
 WIDTH = 32
 VMEM_BYTES = 48 * 1024 * 1024
 
@@ -293,13 +292,13 @@
         feat_ref[f] = features
         message = mm(wmsg_ref[...], features.astype(bf16)).astype(bf16)
         msg_ref[f] = message
-        message = message.astype(f32)
         for side, out in ((0, down_ref), (1, up_ref)):
-            index = halo_ref[f, side : side + 1, :]
-            lane = spread(index & (LANES - 1), LANES)
+            index = spread(halo_ref[f, side : side + 1, :], LANES)
+            lane = (index & (LANES - 1)).astype(jnp.int16)
+            high = (index >> 7).astype(jnp.int16) > 0
             low_g = lane_gather(message[:, :LANES], lane)
             high_g = lane_gather(message[:, LANES:], lane)
-            out[f] = jnp.where(index >= LANES, high_g, low_g).astype(bf16)
+            out[f] = jnp.where(high, high_g, low_g)
 
 
 def hidden_kernel(
@@ -407,13 +406,10 @@
     wup_ref,
     wout_ref,
     struct_ref,
-    energy_hbm,
+    energy_ref,
     chunk_ref,
     acc_ref,
-    src_ref,
     pair_ref,
-    energy_ref,
-    sem,
 ):
     frames, batches, _, atoms = nb_ref.shape
     slots = batches * 8
@@ -424,53 +420,30 @@
     scale = slots**-0.5
     extra = [None] * EXTRA
     for f in range(frames):
-        src_ref[0] = msg_ref[f, :, :LANES]
-        src_ref[1] = msg_ref[f, :, LANES:]
-        src_ref[2] = below_ref[f]
-        src_ref[3] = above_ref[f]
-        halo = jnp.concatenate([below_ref[f, XLU:, :], above_ref[f, XLU:, :]], axis=1)
-        pair_ref[...] = jnp.concatenate([msg_ref[f, XLU:, :], halo], axis=0)
+        halo = jnp.concatenate([below_ref[f], above_ref[f]], axis=1)
+        pair_ref[...] = jnp.concatenate([msg_ref[f], halo], axis=0)
         acc_ref[...] = jnp.zeros_like(acc_ref)
 
         def step(i, carry):
-            filters = [
-                mm(w2_ref[...], hid_ref[f, i, j * hidden : (j + 1) * hidden, :]) for j in range(8)
-            ]
-            width = WIDTH
-            if XLU < LANES:
-                target = lax.broadcasted_iota(jnp.int32, (2 * LANES, atoms), 0).astype(bf16)
-                found = []
-                for j in range(8):
-                    want = (nb_ref[f, i, j : j + 1, :] & (2 * LANES - 1)).astype(f32).astype(bf16)
-                    hot = jnp.where(target == want, jnp.asarray(1, bf16), jnp.asarray(0, bf16))
-                    found.append(mm(pair_ref[...], hot))
+            target = lax.broadcasted_iota(jnp.int32, (2 * LANES, atoms), 0).astype(bf16)
+            filters, found = [], []
+            for j in range(8):
+                want = (nb_ref[f, i, j : j + 1, :] & (2 * LANES - 1)).astype(f32).astype(bf16)
+                hot = jnp.where(target == want, jnp.asarray(1, bf16), jnp.asarray(0, bf16))
+                found.append(mm(pair_ref[...], hot))
+                filters.append(mm(w2_ref[...], hid_ref[f, i, j * hidden : (j + 1) * hidden, :]))
             for half in range(atoms // LANES):
                 cols = slice(half * LANES, (half + 1) * LANES)
-                index = [nb_ref[f, i, j : j + 1, cols] for j in range(8)]
-                lane = [spread(v & (LANES - 1), width).astype(jnp.int16) for v in index]
-                block = [spread(v >> 7, width) for v in index]
-                block16 = [v.astype(jnp.int16) for v in block]
+                own = [spread(nb_ref[f, i, j : j + 1, cols], WIDTH) < 2 * LANES for j in range(8)]
                 offset = [[geo_ref[f, c, i, j : j + 1, cols] for c in range(3)] for j in range(8)]
-                for part in range(0, LANES, width):
-                    rows = slice(part, part + width)
+                for part in range(0, LANES, WIDTH):
+                    rows = slice(part, part + WIDTH)
+                    lower = slice(LANES + part, LANES + part + WIDTH)
                     total = [acc_ref[k, rows, cols] for k in range(4)]
                     for j in range(8):
-                        if part < XLU:
-                            got = [lane_gather(src_ref[b, rows, :], lane[j]) for b in range(4)]
-                            there = jnp.where(
-                                block16[j] < 2,
-                                jnp.where(block16[j] == 1, got[1], got[0]),
-                                jnp.where(block16[j] == 2, got[2], got[3]),
-                            ).astype(f32)
-                        else:
-                            at = part - XLU
-                            there = jnp.where(
-                                block[j] < 2,
-                                found[j][at : at + width, cols],
-                                found[j][LANES - XLU + at : LANES - XLU + at + width, cols],
-                            )
+                        there = jnp.where(own[j], found[j][rows, cols], found[j][lower, cols])
                         total[0] = total[0] + filters[j][rows, cols] * there
-                        vec = filters[j][LANES + part : LANES + part + width, cols] * there
+                        vec = filters[j][lower, cols] * there
                         for c in range(3):
                             total[c + 1] = total[c + 1] + offset[j][c] * vec
                     for k in range(4):
@@ -494,9 +467,6 @@
         readout = jnp.sum(features * wout, axis=0, keepdims=True)
         energy = living * (readout + jnp.where(kind == 1, shift[1], shift[0]))
         energy_ref[f : f + 1, :] = energy
-        if f == frames - 1:
-            leaving = pltpu.make_async_copy(energy_ref, energy_hbm, sem)
-            leaving.start()
         grad = lax.dot_general(mixed, slope, (((1,), (1,)), ((), ())), preferred_element_type=f32)
         chunk_ref[:, f * rows_each : (f + 1) * rows_each, :] = grad.reshape(
             chunks, rows_each, LANES
@@ -507,7 +477,6 @@
         extra[6 + f] = jnp.broadcast_to(jnp.sum(energy, axis=1, keepdims=True), (1, LANES))
     block = jnp.concatenate(extra, axis=0)
     chunk_ref[:, frames * rows_each :, :] = jnp.broadcast_to(block[None], (chunks, EXTRA, LANES))
-    leaving.wait()
 
 
 def total_kernel(scalar_ref, in_ref, out_ref):
@@ -525,7 +494,14 @@
 
 
 def final_kernel(
-    rows_each, atoms_all, scalar_ref, in_ref, target_ref, chunk_ref, mean_ref, out_ref
+    rows_each,
+    atoms_all,
+    scalar_ref,
+    in_ref,
+    target_ref,
+    chunk_ref,
+    mean_ref,
+    out_ref,
 ):
     devices = in_ref.shape[0]
     q = target_ref.shape[1]
@@ -543,13 +519,13 @@
     observed = jnp.sum(structure * slope_sq, axis=1, keepdims=True)
     average = jnp.sum(mean * slope_sq, axis=1, keepdims=True)
     factor = -scalar_ref[2:3, :] * weights * (observed - average)
+    mean_ref[...] = mean
+    out_ref[...] = jnp.sum(factor * gather(0), axis=0, keepdims=True)
     grad = jnp.zeros((rows_each, LANES), f32)
     for d in range(devices):
         for f in range(2):
             k = 2 * d + f
             grad = grad + factor[k : k + 1] * in_ref[d, f * rows_each : (f + 1) * rows_each, :]
-    mean_ref[...] = mean
-    out_ref[...] = jnp.sum(factor * gather(0), axis=0, keepdims=True)
     for s in range(chunk_ref.shape[0]):
         chunk_ref[s] = grad
 
@@ -559,13 +535,13 @@
 HB = pl.BlockSpec(memory_space=pltpu.HBM)
 
 
-def call(kernel, name, ins, outs, scratch, *operands, specs=None):
+def call(kernel, name, ins, outs, scratch, *operands):
     return pl.pallas_call(
         kernel,
         name=name,
         out_shape=outs,
         in_specs=ins,
-        out_specs=specs or jax.tree.map(lambda _: VM, outs),
+        out_specs=jax.tree.map(lambda _: VM, outs),
         scratch_shapes=scratch,
         compiler_params=pltpu.CompilerParams(vmem_limit_bytes=VMEM_BYTES),
     )(*operands)
@@ -715,10 +691,7 @@
         (array((frames, atoms)), array((slab_devs, chunk_rows, LANES))),
         [
             pltpu.VMEM((4, channels, atoms), f32),
-            pltpu.VMEM((4, channels, LANES), bf16),
-            pltpu.VMEM((2 * (LANES - XLU), 2 * LANES), bf16),
-            pltpu.VMEM((frames, atoms), f32),
-            pltpu.SemaphoreType.DMA,
+            pltpu.VMEM((2 * channels, 2 * LANES), bf16),
         ],
         living,
         species,
@@ -734,7 +707,6 @@
         wup,
         wout,
         structure,
-        specs=(HB, VM),
     )
     chunks = lax.all_to_all(chunks, "slab", 0, 0, tiled=True)
     totals = call(

time: 83.1 us -> 82.9 us (level)
  no operation moved by 1% of the time
where the time goes in v5:
time: 82.9 us; the launch traced here: 82.6 us
  blocking collectives  45.7 us (55%)
  Pallas kernels  21.3 us (26%)
  starting transfers between devices  13.6 us (16%)
  between operations  1.36 us (2%)
    pallas_call x7, Pallas kernels, call(): pl.pallas_call(kernel, name=name, out_shape=outs, in_specs=ins, out_specs...  21.3 us
    all_to_all x1, blocking collectives, per_device(): chunks = lax.all_to_all(chunks, 'slab', 0, 0, tiled=True)  18.5 us
    all_to_all x1, blocking collectives, per_device(): totals = lax.all_to_all(totals, 'frame', 0, 0, tiled=True)  14.5 us
    all_to_all x1, blocking collectives, per_device(): grad_up = lax.all_to_all(grad_rows, 'slab', 0, 0, tiled=True)  12.7 us
    ppermute x1, starting transfers between devices, per_device(): above = lax.ppermute(leave_down, 'slab', down)  6.65 us
    ppermute x1, starting transfers between devices, per_device(): msg_above = lax.ppermute(msg_down, 'slab', down)  4.77 us
    ppermute x1, starting transfers between devices, per_device(): below = lax.ppermute(leave_up, 'slab', up)  2.12 us
  transfers between devices with their start and end apart: 4, of which 0 were waited for; matrix products, arithmetic and copies ran while one was open for 0% of the time, Pallas kernels for 4%

profile of v5, /device:TPU:1, one launch (start us, length us, event | category | flops | bytes accessed | tf_op | source)
XLA Modules:
  0.0 82.6 jit_solution(2966694457711844067)
XLA Ops:
  0.6 0.9 %halo_rows.1 = (f32[8,128]{1,0:T(8,128)S(1)}, f32[8,128]{1,0:T(8,128)S(1)}, f32[3,2,256]{2,1,0:T(2,128)S(1)}, s32[2,256]{1,0:T(2,128)S(1)}, s32[2,2,128]{2,1,0:T(2,128)S(1)}) custom-call(f32[3,2,256]{2,1,0:T(2,128)} %bitcast.13, s32[2,256]{1,0:T(2,128)} %spec_hbm.1, s32[2,2,128]{2,1,0:T(2,128)} %halo_hbm.1), custom_call_target="tpu_custom_call" | custom-call | tf_op jit(solution)/shard_map/halo_rows/pallas_call | solution.py:539
  1.5 2.1 %collective-permute-start = (f32[8,128]{1,0:T(8,128)S(1)}, f32[8,128]{1,0:T(8,128)S(1)}, u32[]{:S(2)}, u32[]{:S(2)}) collective-permute-start(f32[8,128]{1,0:T(8,128)S(1)} %get-tuple-element.36), channel_id=1, source_target_pairs={{0,1},{1,2},{2,3},{3,4},{4,5},{5,6},{6,7},{7,8},{8,9},{9,10},{10,1... | collective-permute-start | bytes 12296 | tf_op jit(solution)/shard_map/ppermute | solution.py:606
  3.6 6.6 %collective-permute-start.1 = (f32[8,128]{1,0:T(8,128)S(1)}, f32[8,128]{1,0:T(8,128)S(1)}, u32[]{:S(2)}, u32[]{:S(2)}) collective-permute-start(f32[8,128]{1,0:T(8,128)S(1)} %get-tuple-element.37), channel_id=1, source_target_pairs={{1,0},{2,1},{3,2},{4,3},{5,4},{6,5},{7,6},{8,7},{9,8},{10,9},{11,1... | collective-permute-start | bytes 12296 | tf_op jit(solution)/shard_map/ppermute | solution.py:607
  10.9 1.3 %staged_inputs.1 = (s32[2,6,8,256]{3,2,1,0:T(8,128)S(1)}, bf16[2,256,32]{2,1,0:T(8,128)(2,1)S(1)}, bf16[256,64]{1,0:T(8,128)(2,1)S(1)}, bf16[128,256]{1,0:T(8,12...) custom-call(f32[1]{0:T(128)S(6)} %copy.21.beta_ref, ...), custom_call_target="tpu_custom_call" | custom-call | tf_op jit(solution)/shard_map/staged_inputs/pallas_call | solution.py:539
  12.2 0.0 collective-permute-done.below_ref
  12.2 0.0 collective-permute-done.1.above_ref
  12.2 6.9 %first_layer.1 = (f32[2,4,6,8,256]{4,3,2,1,0:T(8,128)S(1)}, f32[2,128,256]{2,1,0:T(8,128)S(1)}, bf16[2,128,256]{2,1,0:T(8,128)(2,1)S(1)}, bf16[2,128,128]{2,1,0:T(8,128)(2,1)S(1)}, bf16[2,128,128]{2,1,0:T(8,128)(2,1)S(1)}) custom-call(f32[3,2,256]{2,1,0:T(2,128)S(1)} %get-tuple-element.34.pos_ref, s32[2,256]{1,0:T(2,128)S(1)} %get-tuple-element.35.spec_ref, ...), custom_call_target="tpu_custom_call" | custom-call | tf_op jit(solution)/shard_map/first_layer/pallas_call | solution.py:539
  19.1 0.1 collective-permute-start.2
  19.2 4.8 %collective-permute-start.3 = (bf16[2,128,128]{2,1,0:T(8,128)(2,1)S(1)}, bf16[2,128,128]{2,1,0:T(8,128)(2,1)S(1)}, u32[]{:S(2)}, u32[]{:S(2)}) collective-permute-start(bf16[2,128,128]{2,1,0:T(8,128)(2,1)S(1)} %get-tuple-element.53), channel_id=1, source_target_pairs={{1,0},{2,1},{3,2},{4,3},{5,4},{6,5},{7,6},{8,7},{9,8},{10,9},{11,1... | collective-permute-start | bytes 196616 | tf_op jit(solution)/shard_map/ppermute | solution.py:655
  24.0 2.3 %radial_hidden.1 = (bf16[2,6,512,256]{3,2,1,0:T(8,128)(2,1)S(1)}, bf16[256,64]{1,0:T(8,128)(2,1)S(1)}, bf16[128,256]{1,0:T(8,128)(2,1)S(1)}, f32[128,128]{1,0:T(...) custom-call(s32[1]{0:T(128)} %bitcast.slab_ref, ...), custom_call_target="tpu_custom_call" | custom-call | tf_op jit(solution)/shard_map/radial_hidden/pallas_call | solution.py:539
  26.3 0.0 collective-permute-done.2.below_ref
  26.3 0.0 collective-permute-done.3.above_ref
  26.3 9.3 %second_layer.1 = (f32[2,256]{1,0:T(2,128)}, f32[32,24,128]{2,1,0:T(8,128)S(1)}) custom-call(f32[2,256]{1,0:T(2,128)S(1)} %get-tuple-element.47.live_ref, s32[2,256]{1,0:T(2,128)S(1)} %get-tuple-element.35.spec_ref, f32[8,128]{1,0:T(8,128)S(1)} %get-tuple-element.48.scalar_ref, s32[2,6,8,256]{3,2,1,0:T(8,128)S(1)} %get-tuple-element.38.nb_ref, ...), custom_call_target="tpu_custom_call" | custom-call | tf_op jit(solution)/shard_map/second_layer/pallas_call | solution.py:539
  35.6 18.5 %all_to_all.15.in_ref = f32[32,24,128]{2,1,0:T(8,128)S(1)} all-to-all(f32[32,24,128]{2,1,0:T(8,128)S(1)} %get-tuple-element.59), channel_id=1, replica_groups=mesh['frame'=8,'slab'=32] {'slab'}, dimensions={0} | all-to-all | bytes 786432 | tf_op jit(solution)/shard_map/all_to_all | solution.py:711
  54.1 14.5 %all_to_all.16.in_ref = f32[8,24,128]{2,1,0:T(8,128)S(1)} all-to-all(f32[8,24,128]{2,1,0:T(8,128)S(1)} %slab_totals.1), channel_id=1, replica_groups=mesh['frame'=8,'slab'=32] {'frame'}, dimensions={0} | all-to-all | bytes 196608 | tf_op jit(solution)/shard_map/all_to_all | solution.py:721
  68.6 0.6 reweighted.1
  69.3 12.7 %all_to_all.17 = f32[32,8,128]{2,1,0:T(8,128)S(1)} all-to-all(f32[32,8,128]{2,1,0:T(8,128)S(1)} %get-tuple-element.62), channel_id=1, replica_groups=mesh['frame'=8,'slab'=32] {'slab'}, dimensions={0} | all-to-all | bytes 262144 | tf_op jit(solution)/shard_map/all_to_all | solution.py:732
  81.9 0.7 copy.22
  (1 shorter events, 0.0 us)
Async XLA Ops:
  1.5 10.7 %collective-permute-start = (f32[8,128]{1,0:T(8,128)S(1)}, f32[8,128]{1,0:T(8,128)S(1)}, u32[]{:S(2)}, u32[]{:S(2)}) collective-permute-start(f32[8,128]{1,0:T(8,128)S(1)} %get-tuple-element.36), channel_id=1, source_target_pairs={{0,1},{1,2},{2,3},{3,4},{4,5},{5,6},{6,7},{7,8},{8,9},{9,10},{10,1... | collective-permute-start | bytes 12296 | tf_op jit(solution)/shard_map/ppermute | solution.py:606
  3.6 8.6 %collective-permute-start.1 = (f32[8,128]{1,0:T(8,128)S(1)}, f32[8,128]{1,0:T(8,128)S(1)}, u32[]{:S(2)}, u32[]{:S(2)}) collective-permute-start(f32[8,128]{1,0:T(8,128)S(1)} %get-tuple-element.37), channel_id=1, source_target_pairs={{1,0},{2,1},{3,2},{4,3},{5,4},{6,5},{7,6},{8,7},{9,8},{10,9},{11,1... | collective-permute-start | bytes 12296 | tf_op jit(solution)/shard_map/ppermute | solution.py:607
  19.1 7.2 %collective-permute-start.2 = (bf16[2,128,128]{2,1,0:T(8,128)(2,1)S(1)}, bf16[2,128,128]{2,1,0:T(8,128)(2,1)S(1)}, u32[]{:S(2)}, u32[]{:S(2)}) collective-permute-start(bf16[2,128,128]{2,1,0:T(8,128)(2,1)S(1)} %get-tuple-element.52), channel_id=1, source_target_pairs={{0,1},{1,2},{2,3},{3,4},{4,5},{5,6},{6,7},{7,8},{8,9},{9,10},{10,1... | collective-permute-start | bytes 196616 | tf_op jit(solution)/shard_map/ppermute | solution.py:654
  19.2 7.1 %collective-permute-start.3 = (bf16[2,128,128]{2,1,0:T(8,128)(2,1)S(1)}, bf16[2,128,128]{2,1,0:T(8,128)(2,1)S(1)}, u32[]{:S(2)}, u32[]{:S(2)}) collective-permute-start(bf16[2,128,128]{2,1,0:T(8,128)(2,1)S(1)} %get-tuple-element.53), channel_id=1, source_target_pairs={{1,0},{2,1},{3,2},{4,3},{5,4},{6,5},{7,6},{8,7},{9,8},{10,9},{11,1... | collective-permute-start | bytes 196616 | tf_op jit(solution)/shard_map/ppermute | solution.py:655

commit v6 on v5

--- a/solution.py
+++ b/solution.py
@@ -66,13 +66,17 @@
     return half + half * jnp.tanh(half)
 
 
+def silu_of_twice(half):
+    return half + half * jnp.tanh(half)
+
+
 def mm(a, b):
     return jnp.dot(a, b, preferred_element_type=f32)
 
 
 def rad1_blocks(w_rad1):
     basis, hidden = w_rad1.shape
-    w = w_rad1.astype(f32)
+    w = 0.5 * w_rad1.astype(f32)
     wide = jnp.concatenate([w] * GROUP, axis=1)
     tall = jnp.concatenate([wide] * GROUP, axis=0)
     row = lax.broadcasted_iota(jnp.int32, tall.shape, 0) // basis
@@ -246,7 +250,7 @@
             acts = []
             for first in range(0, 8, GROUP):
                 pre = mm(w1_ref[0], basis_rows(geo_ref, f, i, first, atoms))
-                acts.append(silu(pre).astype(bf16).astype(f32))
+                acts.append(silu_of_twice(pre).astype(bf16).astype(f32))
             for half in range(atoms // LANES):
                 cols = slice(half * LANES, (half + 1) * LANES)
                 for part in range(0, hidden, 32):
@@ -351,7 +355,7 @@
 
         def step(i, carry):
             for first in range(0, 8, GROUP):
-                act = silu(mm(w1_ref[1], basis_rows(geo_ref, f, i, first, atoms)))
+                act = silu_of_twice(mm(w1_ref[1], basis_rows(geo_ref, f, i, first, atoms)))
                 out_ref[f, i, first * hidden : (first + GROUP) * hidden, :] = act.astype(bf16)
             return carry
 

time: 82.9 us -> 82.4 us (level)
  no operation moved by 1% of the time
where the time goes in v6:
time: 82.4 us; the launch traced here: 82.2 us
  blocking collectives  45.9 us (56%)
  Pallas kernels  20.6 us (25%)
  starting transfers between devices  13.6 us (17%)
  between operations  1.36 us (2%)
    pallas_call x7, Pallas kernels, call(): pl.pallas_call(kernel, name=name, out_shape=outs, in_specs=ins, out_specs...  20.6 us
    all_to_all x1, blocking collectives, per_device(): chunks = lax.all_to_all(chunks, 'slab', 0, 0, tiled=True)  18.7 us
    all_to_all x1, blocking collectives, per_device(): totals = lax.all_to_all(totals, 'frame', 0, 0, tiled=True)  14.5 us
    all_to_all x1, blocking collectives, per_device(): grad_up = lax.all_to_all(grad_rows, 'slab', 0, 0, tiled=True)  12.7 us
    ppermute x1, starting transfers between devices, per_device(): above = lax.ppermute(leave_down, 'slab', down)  6.65 us
    ppermute x1, starting transfers between devices, per_device(): msg_above = lax.ppermute(msg_down, 'slab', down)  4.77 us
    ppermute x1, starting transfers between devices, per_device(): below = lax.ppermute(leave_up, 'slab', up)  2.12 us
  transfers between devices with their start and end apart: 4, of which 0 were waited for; matrix products, arithmetic and copies ran while one was open for 0% of the time, Pallas kernels for 4%

profile of v6, /device:TPU:1, one launch (start us, length us, event | category | flops | bytes accessed | tf_op | source)
XLA Modules:
  0.0 82.2 jit_solution(261611601218358535)
XLA Ops:
  0.6 0.9 %halo_rows.1 = (f32[8,128]{1,0:T(8,128)S(1)}, f32[8,128]{1,0:T(8,128)S(1)}, f32[3,2,256]{2,1,0:T(2,128)S(1)}, s32[2,256]{1,0:T(2,128)S(1)}, s32[2,2,128]{2,1,0:T(2,128)S(1)}) custom-call(f32[3,2,256]{2,1,0:T(2,128)} %bitcast.13, s32[2,256]{1,0:T(2,128)} %spec_hbm.1, s32[2,2,128]{2,1,0:T(2,128)} %halo_hbm.1), custom_call_target="tpu_custom_call" | custom-call | tf_op jit(solution)/shard_map/halo_rows/pallas_call | solution.py:543
  1.5 2.1 %collective-permute-start = (f32[8,128]{1,0:T(8,128)S(1)}, f32[8,128]{1,0:T(8,128)S(1)}, u32[]{:S(2)}, u32[]{:S(2)}) collective-permute-start(f32[8,128]{1,0:T(8,128)S(1)} %get-tuple-element.36), channel_id=1, source_target_pairs={{0,1},{1,2},{2,3},{3,4},{4,5},{5,6},{6,7},{7,8},{8,9},{9,10},{10,1... | collective-permute-start | bytes 12296 | tf_op jit(solution)/shard_map/ppermute | solution.py:610
  3.6 6.6 %collective-permute-start.1 = (f32[8,128]{1,0:T(8,128)S(1)}, f32[8,128]{1,0:T(8,128)S(1)}, u32[]{:S(2)}, u32[]{:S(2)}) collective-permute-start(f32[8,128]{1,0:T(8,128)S(1)} %get-tuple-element.37), channel_id=1, source_target_pairs={{1,0},{2,1},{3,2},{4,3},{5,4},{6,5},{7,6},{8,7},{9,8},{10,9},{11,1... | collective-permute-start | bytes 12296 | tf_op jit(solution)/shard_map/ppermute | solution.py:611
  10.9 1.3 %staged_inputs.1 = (s32[2,6,8,256]{3,2,1,0:T(8,128)S(1)}, bf16[2,256,32]{2,1,0:T(8,128)(2,1)S(1)}, bf16[256,64]{1,0:T(8,128)(2,1)S(1)}, bf16[128,256]{1,0:T(8,12...) custom-call(f32[1]{0:T(128)S(6)} %copy.21.beta_ref, ...), custom_call_target="tpu_custom_call" | custom-call | tf_op jit(solution)/shard_map/staged_inputs/pallas_call | solution.py:543
  12.2 0.0 collective-permute-done.below_ref
  12.2 0.0 collective-permute-done.1.above_ref
  12.2 6.4 %first_layer.1 = (f32[2,4,6,8,256]{4,3,2,1,0:T(8,128)S(1)}, f32[2,128,256]{2,1,0:T(8,128)S(1)}, bf16[2,128,256]{2,1,0:T(8,128)(2,1)S(1)}, bf16[2,128,128]{2,1,0:T(8,128)(2,1)S(1)}, bf16[2,128,128]{2,1,0:T(8,128)(2,1)S(1)}) custom-call(f32[3,2,256]{2,1,0:T(2,128)S(1)} %get-tuple-element.34.pos_ref, s32[2,256]{1,0:T(2,128)S(1)} %get-tuple-element.35.spec_ref, ...), custom_call_target="tpu_custom_call" | custom-call | tf_op jit(solution)/shard_map/first_layer/pallas_call | solution.py:543
  18.7 0.1 collective-permute-start.2
  18.8 4.8 %collective-permute-start.3 = (bf16[2,128,128]{2,1,0:T(8,128)(2,1)S(1)}, bf16[2,128,128]{2,1,0:T(8,128)(2,1)S(1)}, u32[]{:S(2)}, u32[]{:S(2)}) collective-permute-start(bf16[2,128,128]{2,1,0:T(8,128)(2,1)S(1)} %get-tuple-element.53), channel_id=1, source_target_pairs={{1,0},{2,1},{3,2},{4,3},{5,4},{6,5},{7,6},{8,7},{9,8},{10,9},{11,1... | collective-permute-start | bytes 196616 | tf_op jit(solution)/shard_map/ppermute | solution.py:659
  23.5 2.0 %radial_hidden.1 = (bf16[2,6,512,256]{3,2,1,0:T(8,128)(2,1)S(1)}, bf16[256,64]{1,0:T(8,128)(2,1)S(1)}, bf16[128,256]{1,0:T(8,128)(2,1)S(1)}, f32[128,128]{1,0:T(...) custom-call(s32[1]{0:T(128)} %bitcast.slab_ref, ...), custom_call_target="tpu_custom_call" | custom-call | tf_op jit(solution)/shard_map/radial_hidden/pallas_call | solution.py:543
  25.6 0.0 collective-permute-done.2.below_ref
  25.6 0.0 collective-permute-done.3.above_ref
  25.6 9.3 %second_layer.1 = (f32[2,256]{1,0:T(2,128)}, f32[32,24,128]{2,1,0:T(8,128)S(1)}) custom-call(f32[2,256]{1,0:T(2,128)S(1)} %get-tuple-element.47.live_ref, s32[2,256]{1,0:T(2,128)S(1)} %get-tuple-element.35.spec_ref, f32[8,128]{1,0:T(8,128)S(1)} %get-tuple-element.48.scalar_ref, s32[2,6,8,256]{3,2,1,0:T(8,128)S(1)} %get-tuple-element.38.nb_ref, ...), custom_call_target="tpu_custom_call" | custom-call | tf_op jit(solution)/shard_map/second_layer/pallas_call | solution.py:543
  34.9 18.7 %all_to_all.15.in_ref = f32[32,24,128]{2,1,0:T(8,128)S(1)} all-to-all(f32[32,24,128]{2,1,0:T(8,128)S(1)} %get-tuple-element.59), channel_id=1, replica_groups=mesh['frame'=8,'slab'=32] {'slab'}, dimensions={0} | all-to-all | bytes 786432 | tf_op jit(solution)/shard_map/all_to_all | solution.py:715
  53.7 14.5 %all_to_all.16.in_ref = f32[8,24,128]{2,1,0:T(8,128)S(1)} all-to-all(f32[8,24,128]{2,1,0:T(8,128)S(1)} %slab_totals.1), channel_id=1, replica_groups=mesh['frame'=8,'slab'=32] {'frame'}, dimensions={0} | all-to-all | bytes 196608 | tf_op jit(solution)/shard_map/all_to_all | solution.py:725
  68.2 0.6 reweighted.1
  68.9 12.7 %all_to_all.17 = f32[32,8,128]{2,1,0:T(8,128)S(1)} all-to-all(f32[32,8,128]{2,1,0:T(8,128)S(1)} %get-tuple-element.62), channel_id=1, replica_groups=mesh['frame'=8,'slab'=32] {'slab'}, dimensions={0} | all-to-all | bytes 262144 | tf_op jit(solution)/shard_map/all_to_all | solution.py:736
  81.5 0.7 copy.22
  (1 shorter events, 0.0 us)
Async XLA Ops:
  1.5 10.7 %collective-permute-start = (f32[8,128]{1,0:T(8,128)S(1)}, f32[8,128]{1,0:T(8,128)S(1)}, u32[]{:S(2)}, u32[]{:S(2)}) collective-permute-start(f32[8,128]{1,0:T(8,128)S(1)} %get-tuple-element.36), channel_id=1, source_target_pairs={{0,1},{1,2},{2,3},{3,4},{4,5},{5,6},{6,7},{7,8},{8,9},{9,10},{10,1... | collective-permute-start | bytes 12296 | tf_op jit(solution)/shard_map/ppermute | solution.py:610
  3.6 8.6 %collective-permute-start.1 = (f32[8,128]{1,0:T(8,128)S(1)}, f32[8,128]{1,0:T(8,128)S(1)}, u32[]{:S(2)}, u32[]{:S(2)}) collective-permute-start(f32[8,128]{1,0:T(8,128)S(1)} %get-tuple-element.37), channel_id=1, source_target_pairs={{1,0},{2,1},{3,2},{4,3},{5,4},{6,5},{7,6},{8,7},{9,8},{10,9},{11,1... | collective-permute-start | bytes 12296 | tf_op jit(solution)/shard_map/ppermute | solution.py:611
  18.7 6.9 %collective-permute-start.2 = (bf16[2,128,128]{2,1,0:T(8,128)(2,1)S(1)}, bf16[2,128,128]{2,1,0:T(8,128)(2,1)S(1)}, u32[]{:S(2)}, u32[]{:S(2)}) collective-permute-start(bf16[2,128,128]{2,1,0:T(8,128)(2,1)S(1)} %get-tuple-element.52), channel_id=1, source_target_pairs={{0,1},{1,2},{2,3},{3,4},{4,5},{5,6},{6,7},{7,8},{8,9},{9,10},{10,1... | collective-permute-start | bytes 196616 | tf_op jit(solution)/shard_map/ppermute | solution.py:658
  18.8 6.8 %collective-permute-start.3 = (bf16[2,128,128]{2,1,0:T(8,128)(2,1)S(1)}, bf16[2,128,128]{2,1,0:T(8,128)(2,1)S(1)}, u32[]{:S(2)}, u32[]{:S(2)}) collective-permute-start(bf16[2,128,128]{2,1,0:T(8,128)(2,1)S(1)} %get-tuple-element.53), channel_id=1, source_target_pairs={{1,0},{2,1},{3,2},{4,3},{5,4},{6,5},{7,6},{8,7},{9,8},{10,9},{11,1... | collective-permute-start | bytes 196616 | tf_op jit(solution)/shard_map/ppermute | solution.py:659

commit v7 on v6

--- a/solution.py
+++ b/solution.py
@@ -404,8 +404,8 @@
     hid_ref,
     feat_ref,
     msg_ref,
+    above_ref,
     below_ref,
-    above_ref,
     w2_ref,
     wup_ref,
     wout_ref,
@@ -655,8 +655,8 @@
         wmsg,
         kinds,
     )
+    msg_above = lax.ppermute(msg_down, "slab", down)
     msg_below = lax.ppermute(msg_up, "slab", up)
-    msg_above = lax.ppermute(msg_down, "slab", down)
     small = (
         u_reference.reshape(1, frames),
         e_shift.reshape(1, 2),
@@ -705,8 +705,8 @@
         radial_hidden,
         features,
         message,
+        msg_above,
         msg_below,
-        msg_above,
         w2,
         wup,
         wout,

time: 82.4 us -> 83.8 us (1.017)
  waiting for transfers between devices: 0.01 us -> 4.4 us
  blocking collectives: 45.9 us -> 43.9 us
  starting transfers between devices: 13.6 us -> 12.6 us
    ppermute x1, waiting for transfers between devices: 0.01 us -> 4.4 us  [per_device(): msg_below = lax.ppermute(msg_up, 'slab', up)]
    all_to_all x1, blocking collectives: 18.7 us -> 16.8 us  [per_device(): chunks = lax.all_to_all(chunks, 'slab', 0, 0, tiled=True)]
    ppermute x1, starting transfers between devices: 4.77 us -> 3.88 us  [per_device(): msg_above = lax.ppermute(msg_down, 'slab', down)]
  transfers between devices with their start and end apart: 4 -> 4, of which waited for: 0 -> 1; matrix products, arithmetic and copies ran while one was open for 0% -> 0% of each run, Pallas kernels for 4% -> 4%
where the time goes in v7:
time: 83.8 us; the launch traced here: 83.5 us
  blocking collectives  43.9 us (52%)
  Pallas kernels  20.6 us (25%)
  starting transfers between devices  12.6 us (15%)
  waiting for transfers between devices  4.4 us (5%)
  between operations  1.35 us (2%)
    pallas_call x7, Pallas kernels, call(): pl.pallas_call(kernel, name=name, out_shape=outs, in_specs=ins, out_specs...  20.6 us
    all_to_all x1, blocking collectives, per_device(): chunks = lax.all_to_all(chunks, 'slab', 0, 0, tiled=True)  16.8 us
    all_to_all x1, blocking collectives, per_device(): totals = lax.all_to_all(totals, 'frame', 0, 0, tiled=True)  14.3 us
    all_to_all x1, blocking collectives, per_device(): grad_up = lax.all_to_all(grad_rows, 'slab', 0, 0, tiled=True)  12.7 us
    ppermute x1, starting transfers between devices, per_device(): above = lax.ppermute(leave_down, 'slab', down)  6.65 us
    ppermute x1, waiting for transfers between devices, per_device(): msg_below = lax.ppermute(msg_up, 'slab', up)  4.4 us
    ppermute x1, starting transfers between devices, per_device(): msg_above = lax.ppermute(msg_down, 'slab', down)  3.88 us
    ppermute x1, starting transfers between devices, per_device(): below = lax.ppermute(leave_up, 'slab', up)  2.12 us
  transfers between devices with their start and end apart: 4, of which 1 were waited for; matrix products, arithmetic and copies ran while one was open for 0% of the time, Pallas kernels for 4%

profile of v7, /device:TPU:1, one launch (start us, length us, event | category | flops | bytes accessed | tf_op | source)
XLA Modules:
  0.0 83.5 jit_solution(2868320618035397293)
XLA Ops:
  0.6 0.9 %halo_rows.1 = (f32[8,128]{1,0:T(8,128)S(1)}, f32[8,128]{1,0:T(8,128)S(1)}, f32[3,2,256]{2,1,0:T(2,128)S(1)}, s32[2,256]{1,0:T(2,128)S(1)}, s32[2,2,128]{2,1,0:T(2,128)S(1)}) custom-call(f32[3,2,256]{2,1,0:T(2,128)} %bitcast.13, s32[2,256]{1,0:T(2,128)} %spec_hbm.1, s32[2,2,128]{2,1,0:T(2,128)} %halo_hbm.1), custom_call_target="tpu_custom_call" | custom-call | tf_op jit(solution)/shard_map/halo_rows/pallas_call | solution.py:543
  1.5 2.1 %collective-permute-start = (f32[8,128]{1,0:T(8,128)S(1)}, f32[8,128]{1,0:T(8,128)S(1)}, u32[]{:S(2)}, u32[]{:S(2)}) collective-permute-start(f32[8,128]{1,0:T(8,128)S(1)} %get-tuple-element.36), channel_id=1, source_target_pairs={{0,1},{1,2},{2,3},{3,4},{4,5},{5,6},{6,7},{7,8},{8,9},{9,10},{10,1... | collective-permute-start | bytes 12296 | tf_op jit(solution)/shard_map/ppermute | solution.py:610
  3.6 6.6 %collective-permute-start.1 = (f32[8,128]{1,0:T(8,128)S(1)}, f32[8,128]{1,0:T(8,128)S(1)}, u32[]{:S(2)}, u32[]{:S(2)}) collective-permute-start(f32[8,128]{1,0:T(8,128)S(1)} %get-tuple-element.37), channel_id=1, source_target_pairs={{1,0},{2,1},{3,2},{4,3},{5,4},{6,5},{7,6},{8,7},{9,8},{10,9},{11,1... | collective-permute-start | bytes 12296 | tf_op jit(solution)/shard_map/ppermute | solution.py:611
  10.9 1.3 %staged_inputs.1 = (s32[2,6,8,256]{3,2,1,0:T(8,128)S(1)}, bf16[2,256,32]{2,1,0:T(8,128)(2,1)S(1)}, bf16[256,64]{1,0:T(8,128)(2,1)S(1)}, bf16[128,256]{1,0:T(8,12...) custom-call(f32[1]{0:T(128)S(6)} %copy.21.beta_ref, ...), custom_call_target="tpu_custom_call" | custom-call | tf_op jit(solution)/shard_map/staged_inputs/pallas_call | solution.py:543
  12.2 0.0 collective-permute-done.below_ref
  12.2 0.0 collective-permute-done.1.above_ref
  12.2 6.4 %first_layer.1 = (f32[2,4,6,8,256]{4,3,2,1,0:T(8,128)S(1)}, f32[2,128,256]{2,1,0:T(8,128)S(1)}, bf16[2,128,256]{2,1,0:T(8,128)(2,1)S(1)}, bf16[2,128,128]{2,1,0:T(8,128)(2,1)S(1)}, bf16[2,128,128]{2,1,0:T(8,128)(2,1)S(1)}) custom-call(f32[3,2,256]{2,1,0:T(2,128)S(1)} %get-tuple-element.34.pos_ref, s32[2,256]{1,0:T(2,128)S(1)} %get-tuple-element.35.spec_ref, ...), custom_call_target="tpu_custom_call" | custom-call | tf_op jit(solution)/shard_map/first_layer/pallas_call | solution.py:543
  18.7 3.9 %collective-permute-start.2 = (bf16[2,128,128]{2,1,0:T(8,128)(2,1)S(1)}, bf16[2,128,128]{2,1,0:T(8,128)(2,1)S(1)}, u32[]{:S(2)}, u32[]{:S(2)}) collective-permute-start(bf16[2,128,128]{2,1,0:T(8,128)(2,1)S(1)} %get-tuple-element.52), channel_id=1, source_target_pairs={{1,0},{2,1},{3,2},{4,3},{5,4},{6,5},{7,6},{8,7},{9,8},{10,9},{11,1... | collective-permute-start | bytes 196616 | tf_op jit(solution)/shard_map/ppermute | solution.py:658
  22.5 0.0 collective-permute-start.3
  22.6 2.0 %radial_hidden.1 = (bf16[2,6,512,256]{3,2,1,0:T(8,128)(2,1)S(1)}, bf16[256,64]{1,0:T(8,128)(2,1)S(1)}, bf16[128,256]{1,0:T(8,128)(2,1)S(1)}, f32[128,128]{1,0:T(...) custom-call(s32[1]{0:T(128)} %bitcast.slab_ref, ...), custom_call_target="tpu_custom_call" | custom-call | tf_op jit(solution)/shard_map/radial_hidden/pallas_call | solution.py:543
  24.6 0.0 collective-permute-done.2.above_ref
  24.6 4.4 %collective-permute-done.3.below_ref = bf16[2,128,128]{2,1,0:T(8,128)(2,1)S(1)} collective-permute-done((bf16[2,128,128]{2,1,0:T(8,128)(2,1)S(1)}, bf16[2,128,128]{2,1,0:T(8,128)(2,1)S(1)}, u32[]{:S(2)}, u32[]{:S(2)}) %collective-permute-start.3) | collective-permute-done | bytes 65568 | tf_op jit(solution)/shard_map/ppermute | solution.py:659
  29.0 9.3 %second_layer.1 = (f32[2,256]{1,0:T(2,128)}, f32[32,24,128]{2,1,0:T(8,128)S(1)}) custom-call(f32[2,256]{1,0:T(2,128)S(1)} %get-tuple-element.47.live_ref, s32[2,256]{1,0:T(2,128)S(1)} %get-tuple-element.35.spec_ref, f32[8,128]{1,0:T(8,128)S(1)} %get-tuple-element.48.scalar_ref, s32[2,6,8,256]{3,2,1,0:T(8,128)S(1)} %get-tuple-element.38.nb_ref, ...), custom_call_target="tpu_custom_call" | custom-call | tf_op jit(solution)/shard_map/second_layer/pallas_call | solution.py:543
  38.3 16.8 %all_to_all.15.in_ref = f32[32,24,128]{2,1,0:T(8,128)S(1)} all-to-all(f32[32,24,128]{2,1,0:T(8,128)S(1)} %get-tuple-element.59), channel_id=1, replica_groups=mesh['frame'=8,'slab'=32] {'slab'}, dimensions={0} | all-to-all | bytes 786432 | tf_op jit(solution)/shard_map/all_to_all | solution.py:715
  55.2 14.3 %all_to_all.16.in_ref = f32[8,24,128]{2,1,0:T(8,128)S(1)} all-to-all(f32[8,24,128]{2,1,0:T(8,128)S(1)} %slab_totals.1), channel_id=1, replica_groups=mesh['frame'=8,'slab'=32] {'frame'}, dimensions={0} | all-to-all | bytes 196608 | tf_op jit(solution)/shard_map/all_to_all | solution.py:725
  69.5 0.6 reweighted.1
  70.1 12.7 %all_to_all.17 = f32[32,8,128]{2,1,0:T(8,128)S(1)} all-to-all(f32[32,8,128]{2,1,0:T(8,128)S(1)} %get-tuple-element.62), channel_id=1, replica_groups=mesh['frame'=8,'slab'=32] {'slab'}, dimensions={0} | all-to-all | bytes 262144 | tf_op jit(solution)/shard_map/all_to_all | solution.py:736
  82.9 0.7 copy.22
  (1 shorter events, 0.0 us)
Async XLA Ops:
  1.5 10.7 %collective-permute-start = (f32[8,128]{1,0:T(8,128)S(1)}, f32[8,128]{1,0:T(8,128)S(1)}, u32[]{:S(2)}, u32[]{:S(2)}) collective-permute-start(f32[8,128]{1,0:T(8,128)S(1)} %get-tuple-element.36), channel_id=1, source_target_pairs={{0,1},{1,2},{2,3},{3,4},{4,5},{5,6},{6,7},{7,8},{8,9},{9,10},{10,1... | collective-permute-start | bytes 12296 | tf_op jit(solution)/shard_map/ppermute | solution.py:610
  3.6 8.6 %collective-permute-start.1 = (f32[8,128]{1,0:T(8,128)S(1)}, f32[8,128]{1,0:T(8,128)S(1)}, u32[]{:S(2)}, u32[]{:S(2)}) collective-permute-start(f32[8,128]{1,0:T(8,128)S(1)} %get-tuple-element.37), channel_id=1, source_target_pairs={{1,0},{2,1},{3,2},{4,3},{5,4},{6,5},{7,6},{8,7},{9,8},{10,9},{11,1... | collective-permute-start | bytes 12296 | tf_op jit(solution)/shard_map/ppermute | solution.py:611
  18.7 5.9 %collective-permute-start.2 = (bf16[2,128,128]{2,1,0:T(8,128)(2,1)S(1)}, bf16[2,128,128]{2,1,0:T(8,128)(2,1)S(1)}, u32[]{:S(2)}, u32[]{:S(2)}) collective-permute-start(bf16[2,128,128]{2,1,0:T(8,128)(2,1)S(1)} %get-tuple-element.52), channel_id=1, source_target_pairs={{1,0},{2,1},{3,2},{4,3},{5,4},{6,5},{7,6},{8,7},{9,8},{10,9},{11,1... | collective-permute-start | bytes 196616 | tf_op jit(solution)/shard_map/ppermute | solution.py:658
  22.5 6.4 %collective-permute-start.3 = (bf16[2,128,128]{2,1,0:T(8,128)(2,1)S(1)}, bf16[2,128,128]{2,1,0:T(8,128)(2,1)S(1)}, u32[]{:S(2)}, u32[]{:S(2)}) collective-permute-start(bf16[2,128,128]{2,1,0:T(8,128)(2,1)S(1)} %get-tuple-element.53), channel_id=1, source_target_pairs={{0,1},{1,2},{2,3},{3,4},{4,5},{5,6},{6,7},{7,8},{8,9},{9,10},{10,1... | collective-permute-start | bytes 196616 | tf_op jit(solution)/shard_map/ppermute | solution.py:659
